TPU v7x, 32 devices: a whole 2x2x4 slice. The times are simulated.
32 devices in a mesh: dp: 8 (over z, y), stream: 4 (over x, core).
Axes of the slice: x: 2, y: 2, z: 4, core: 2. Of those that a mesh axis runs over, the one named last changes fastest.
Arguments:
- patches: bfloat16 [16384, 768], P(('dp', 'stream')), may hold values from -6 to 6
- src_kind: int32 [32768], P(('dp', 'stream')), may hold values from 0 to 1, as said below
- src_index: int32 [32768], P(('dp', 'stream')), may hold values from 0 to 4015, as said below
- layout_coords: int32 [4, 32768], P(None, ('dp', 'stream')), may hold values from 0 to 1023
- placing: int32 [32768], P(('dp', 'stream')), may hold values from 0 to 8191, as said below
- segments: int32 [32, 1024], P(('dp', 'stream')), may hold values from 0 to 7, never falling along the last dimension, each value on 1 to 512 neighbouring positions
- text_table: bfloat16 [32128, 768], P('dp'), may hold values from -6 to 6
- layout_tables: bfloat16 [4, 1024, 768], P(None, 'dp'), may hold values from -3 to 3
- patch_proj: bfloat16 [768, 768], P('dp'), may hold values from -0.21875 to 0.21875
- rel_table: float32 [32, 12], replicated, may hold values from -4 to 4
- norm_gains: bfloat16 [2, 768], P(None, 'dp'), may hold values from 0.5 to 1.5
- w_qkv: bfloat16 [3, 768, 768], P(None, 'dp'), may hold values from -0.21875 to 0.21875
- w_attn_out: bfloat16 [768, 768], P('dp'), may hold values from -1.25 to 1.25
- w_ff_in: bfloat16 [768, 3072], P('dp'), may hold values from -0.21875 to 0.21875
- w_ff_out: bfloat16 [3072, 768], P('dp'), may hold values from -0.109375 to 0.109375
- out_grad: bfloat16 [32768, 768], P(('dp', 'stream')), may hold values from -6 to 6
Outputs:
- out_rows: bfloat16 [32768, 768], P(('dp', 'stream'))
- grad_patches: float32 [16384, 768], P(('dp', 'stream'))
- grad_text: float32 [32128, 768], P('dp')
- grad_layout: float32 [4, 1024, 768], P(None, 'dp')
- grad_patch_proj: float32 [768, 768], P('dp')
- grad_rel: float32 [32, 12], replicated
- grad_gains: float32 [2, 768], P(None, 'dp')
- grad_qkv: float32 [3, 768, 768], P(None, 'dp')
- grad_attn_out: float32 [768, 768], P('dp')
- grad_ff_in: float32 [768, 3072], P('dp')
- grad_ff_out: float32 [3072, 768], P('dp')
Inputs may be any that keep to these rules, and one draw needn't show every extreme that they name: `src_kind`: each device holds exactly 512 visual tokens (0); the rest of its 1024 source tokens are text tokens (1). `src_index`: A visual token names a patch of its own device, each of the device's 512 patches named by exactly one token. A text token names one of the 4016 text table rows of its data index. For each stream index, placing over the source tokens of that stream index is a permutation of the 8192 packed places; value // 1024 is the owner's data index and value % 1024 the place in the owner's rows. One device sends at most 256 tokens to one owner, and exactly 256 to some owners. `segments`: within each packed row the segment numbers never fall.
All inputs are finite; a program needn't handle non-finite values.
Results may differ from a plain program's by a relative error of at most 0.015.
Values may be sent and summed in bfloat16 or wider, within the bound.
No kernel may reach another device: no remote copies, remote signals or barrier semaphores. Data moves between devices by JAX's collectives and lax.ppermute only.
A program may use at most 256 MiB of HBM per device.

v0:
```python
from functools import partial
import math

import jax
import jax.numpy as jnp
from jax import lax
from jax.experimental import pallas as pl
from jax.experimental.pallas import tpu as pltpu
from jax.sharding import PartitionSpec as P

EPSILON = 1e-06
THRESHOLDS = (12, 16, 23, 32, 46, 64, 91)
BLK = 256
NEG = -1e30
RATE = math.sqrt(2.0 / math.pi)
VMEM_LIMIT = 56 * 2**20
SMALL = pl.CostEstimate(flops=1, bytes_accessed=1, transcendentals=0)


class Line:
    def __init__(self):
        self.last = jnp.zeros((8, 128), jnp.float32)


def launch(line, kernel, operands, in_specs, out_shape, out_specs, grid, name, scalars=(), scratch=()):
    held, given, made = len(scalars), len(operands), len(out_shape)
    token = pl.BlockSpec((8, 128), lambda *_: (0, 0))

    def body(*refs):
        outs = held + given + 1
        refs[outs + made][...] = refs[outs - 1][...]
        kernel(*refs[: outs - 1], *refs[outs : outs + made], *refs[outs + made + 1 :])

    out_shape = [jax.ShapeDtypeStruct(value.shape, value.dtype) for value in out_shape]
    results = pl.pallas_call(
        body,
        out_shape=tuple(out_shape) + (jax.ShapeDtypeStruct((8, 128), jnp.float32),),
        grid_spec=pltpu.PrefetchScalarGridSpec(
            num_scalar_prefetch=held,
            grid=grid,
            in_specs=list(in_specs) + [token],
            out_specs=tuple(out_specs) + (token,),
            scratch_shapes=list(scratch),
        ),
        compiler_params=pltpu.CompilerParams(vmem_limit_bytes=VMEM_LIMIT),
        cost_estimate=SMALL,
        name=name,
    )(*scalars, *operands, line.last)
    line.last = results[-1]
    return results[:-1]


def fixed(value):
    return pl.BlockSpec(value.shape, lambda *_: (0,) * len(value.shape))


def bf16(*shape):
    return jax.ShapeDtypeStruct(shape, jnp.bfloat16)


def f32(*shape):
    return jax.ShapeDtypeStruct(shape, jnp.float32)


def i32(*shape):
    return jax.ShapeDtypeStruct(shape, jnp.int32)


def bucket_of(relative):
    magnitude = jnp.abs(relative)
    beyond = 8 + sum(((magnitude >= threshold).astype(jnp.int32) for threshold in THRESHOLDS))
    return jnp.where(relative > 0, 16, 0).astype(jnp.int32) + jnp.where(
        magnitude < 8, magnitude, beyond
    )


def dot_nt(a, b):
    return lax.dot_general(a, b, (((1,), (1,)), ((), ())), preferred_element_type=jnp.float32)

def dot_nn(a, b):
    return lax.dot_general(a, b, (((1,), (0,)), ((), ())), preferred_element_type=jnp.float32)

def dot_tn(a, b):
    return lax.dot_general(a, b, (((0,), (0,)), ((), ())), preferred_element_type=jnp.float32)


def pieces(value):
    one = value.astype(jnp.bfloat16)
    rest = value - one.astype(jnp.float32)
    two = rest.astype(jnp.bfloat16)
    three = (rest - two.astype(jnp.float32)).astype(jnp.bfloat16)
    return one, two, three

def put_pieces(base, value, lane):
    one, two, three = pieces(value)
    base = jnp.where(jnp.logical_or(lane == 8, lane == 72), one, base)
    base = jnp.where(jnp.logical_or(lane == 9, lane == 73), two, base)
    return jnp.where(jnp.logical_or(lane == 10, lane == 74), three, base)

def diagonal_sums(block):
    wide = jnp.concatenate([block, jnp.zeros_like(block)], axis=1)
    total = wide[:128]
    for start in range(128, BLK, 128):
        total = total + pltpu.roll(wide[start : start + 128], 2 * BLK - start, 1)
    eight = total[:8]
    for start in range(8, 128, 8):
        eight = eight + pltpu.roll(total[start : start + 8], 2 * BLK - start, 1)
    one = eight[:1]
    for row in range(1, 8):
        one = one + pltpu.roll(eight[row : row + 1], 2 * BLK - row, 1)
    return one


def window_of(block, count):
    low = max(0, block * BLK - 2 * BLK + 1) // BLK
    high = min(count - 1, (block * BLK + BLK - 1 + 2 * BLK - 1) // BLK)
    return low, high + 1

def fill_strip(strip, table, slot, count):
    middle = (count - 1) * BLK
    for step in (-1, 0, 1):
        window = table[slot : slot + 1, BLK * step + BLK : BLK * step + 3 * BLK]
        spread = jnp.broadcast_to(window, (BLK, 2 * BLK))
        start = middle + step * BLK
        strip[slot, :, start : start + BLK] = pltpu.roll(spread, 0, 1, stride=1, stride_axis=0)[:, BLK:]
    low = jnp.broadcast_to(table[slot : slot + 1, 0:1], (BLK, middle - BLK))
    high = jnp.broadcast_to(table[slot : slot + 1, 4 * BLK - 1 : 4 * BLK], (BLK, middle - BLK))
    strip[slot, :, 0 : middle - BLK] = low
    strip[slot, :, middle + 2 * BLK :] = high

def forward_kernel(q_ref, k_ref, v_ref, aug_q, aug_k, table, out_ref, lse_ref, strip, ka, va):
    length = q_ref.shape[0]
    count = length // BLK
    lane = lax.broadcasted_iota(jnp.int32, (1, 128), 1)
    left = lane < 64
    for h in range(2):
        fill_strip(strip, table, h, count)
        mine = left if h == 0 else jnp.logical_not(left)
        ka[h] = jnp.where(mine, k_ref[...], aug_k[...])
        va[h] = jnp.where(mine, v_ref[...], aug_k[...])
    for qb in range(count):
        rows = slice(qb * BLK, qb * BLK + BLK)
        low, high = window_of(qb, count)
        keys = slice(low * BLK, high * BLK)
        offset = (count - 1 - qb) * BLK
        query = q_ref[rows, :] * jnp.bfloat16(0.125)
        outs = []
        lses = []
        for h in range(2):
            qa = jnp.where(left if h == 0 else jnp.logical_not(left), query, aug_q[rows, :])
            s = dot_nt(qa, ka[h, keys, :]) + strip[h, :, offset + low * BLK : offset + high * BLK]
            peak = jnp.max(s, axis=1, keepdims=True)
            p = jnp.exp(s - peak).astype(jnp.bfloat16)
            acc = dot_nn(p, va[h, keys, :])
            mark = 72 if h == 0 else 8
            total = acc[:, mark : mark + 1]
            outs.append(acc / total)
            lses.append(jnp.broadcast_to(peak + jnp.log(total), (BLK, 128)))
        out_ref[rows, :] = jnp.where(left, outs[0], outs[1]).astype(jnp.bfloat16)
        lse_ref[rows, :] = jnp.where(left, lses[0], lses[1])

def backward_kernel(
    q_ref, k_ref, v_ref, mixed_ref, grad_ref, lse_ref, aug_q, aug_k, table,
    grads_ref, rel_ref,
    strip, rel, ka, va, qa, ga, dq_acc,
):
    length = q_ref.shape[0]
    count = length // BLK
    middle = (count - 1) * BLK
    lane = lax.broadcasted_iota(jnp.int32, (1, 128), 1)
    left = lane < 64
    rel[...] = jnp.zeros_like(rel)
    dq_acc[...] = jnp.zeros_like(dq_acc)
    inner = mixed_ref[...].astype(jnp.float32) * grad_ref[...].astype(jnp.float32)
    query = q_ref[...] * jnp.bfloat16(0.125)
    for h in range(2):
        fill_strip(strip, table, h, count)
        mine = left if h == 0 else jnp.logical_not(left)
        ka[h] = jnp.where(mine, k_ref[...], aug_k[...])
        va[h] = jnp.where(mine, v_ref[...], aug_k[...])
        at = 0 if h == 0 else 64
        qa[h] = jnp.where(mine, query, put_pieces(aug_q[...], -lse_ref[:, at : at + 1], lane))
        delta = jnp.sum(jnp.where(mine, inner, 0.0), axis=1, keepdims=True)
        spare = put_pieces(jnp.zeros((length, 128), jnp.bfloat16), -delta, lane)
        ga[h] = jnp.where(mine, grad_ref[...], spare)
    for kb in range(count):
        keys = slice(kb * BLK, kb * BLK + BLK)
        low, high = window_of(kb, count)
        rows = slice(low * BLK, high * BLK)
        offset = middle - kb * BLK
        cut = slice(offset + low * BLK, offset + high * BLK)
        dks, dvs = [], []
        for h in range(2):
            s = dot_nt(ka[h, keys, :], qa[h, rows, :]) + strip[h, :, cut]
            p = jnp.exp(s)
            ds = p * dot_nt(va[h, keys, :], ga[h, rows, :])
            rel[h, :, cut] += ds
            p = p.astype(jnp.bfloat16)
            ds = ds.astype(jnp.bfloat16)
            dvs.append(dot_nn(p, ga[h, rows, :]))
            dks.append(dot_nn(ds, qa[h, rows, :]))
            dq_acc[h, :, rows] += dot_tn(ka[h, keys, :], ds)
        grads_ref[1, keys, :] = jnp.where(left, dks[0], dks[1]).astype(jnp.bfloat16)
        grads_ref[2, keys, :] = jnp.where(left, dvs[0], dvs[1]).astype(jnp.bfloat16)
    row = lax.broadcasted_iota(jnp.int32, (128, 1), 0)
    dq = jnp.where(row < 64, dq_acc[0], dq_acc[1]).T
    grads_ref[0] = (dq * 0.125).astype(jnp.bfloat16)
    for h in range(2):
        out = []
        for place in range(5):
            start = middle + (2 - place) * BLK
            if place == 0:
                far = rel[h, :, middle + 2 * BLK :]
                summed = jnp.sum(jnp.sum(far, axis=0, keepdims=True).reshape(-1, BLK), axis=0, keepdims=True)
                out.append(jnp.concatenate([summed, jnp.zeros_like(summed)], axis=1))
            elif place == 4:
                far = rel[h, :, : middle - BLK]
                summed = jnp.sum(jnp.sum(far, axis=0, keepdims=True).reshape(-1, BLK), axis=0, keepdims=True)
                out.append(jnp.concatenate([summed, jnp.zeros_like(summed)], axis=1))
            else:
                out.append(diagonal_sums(rel[h, :, start : start + BLK]))
        rel_ref[h] = jnp.concatenate(out + [jnp.zeros((3, 2 * BLK), jnp.float32)], axis=0)


def attention_forward(line, qkv, aug_q, aug_k, table):
    _, length, width = qkv.shape
    col = pl.BlockSpec((length, 128), lambda p: (0, p))
    buf = pltpu.VMEM((2, length, 128), jnp.bfloat16)
    return launch(
        line, forward_kernel, (qkv, qkv, qkv, aug_q, aug_k, table),
        [
            pl.BlockSpec((None, length, 128), lambda p: (0, 0, p)),
            pl.BlockSpec((None, length, 128), lambda p: (1, 0, p)),
            pl.BlockSpec((None, length, 128), lambda p: (2, 0, p)),
            fixed(aug_q), fixed(aug_k),
            pl.BlockSpec((None, 2, table.shape[2]), lambda p: (p, 0, 0)),
        ],
        (bf16(length, width), f32(length, width)), (col, col), (width // 128,),
        "attention_forward",
        scratch=[pltpu.VMEM((2, BLK, 2 * length - BLK), jnp.float32), buf, buf],
    )


def attention_backward(line, qkv, mixed, grad_mixed, lse, aug_q, aug_k, table):
    _, length, width = qkv.shape
    col = pl.BlockSpec((length, 128), lambda p: (0, p))
    buf = pltpu.VMEM((2, length, 128), jnp.bfloat16)
    strip = pltpu.VMEM((2, BLK, 2 * length - BLK), jnp.float32)
    return launch(
        line, backward_kernel,
        (qkv, qkv, qkv, mixed, grad_mixed, lse, aug_q, aug_k, table),
        [
            pl.BlockSpec((None, length, 128), lambda p: (0, 0, p)),
            pl.BlockSpec((None, length, 128), lambda p: (1, 0, p)),
            pl.BlockSpec((None, length, 128), lambda p: (2, 0, p)),
            col, col, col, fixed(aug_q), fixed(aug_k),
            pl.BlockSpec((None, 2, table.shape[2]), lambda p: (p, 0, 0)),
        ],
        (bf16(3, length, width), f32(width // 64, 8, 2 * BLK)),
        (
            pl.BlockSpec((3, length, 128), lambda p: (0, 0, p)),
            pl.BlockSpec((2, 8, 2 * BLK), lambda p: (p, 0, 0)),
        ),
        (width // 128,), "attention_backward",
        scratch=[strip, strip, buf, buf, buf, buf, pltpu.VMEM((2, 128, length), jnp.float32)],
    )


def bucket_choice(offsets, count):
    return (bucket_of(offsets)[:, None] == jnp.arange(count, dtype=jnp.int32)[None, :]).astype(jnp.float32)

def prepare(segments, rel_table):
    heads = rel_table.shape[1]
    offsets = jnp.arange(4 * BLK, dtype=jnp.int32) - 2 * BLK
    tables = []
    for sign in (1, -1):
        choose = bucket_choice(sign * offsets, rel_table.shape[0])
        table = lax.dot_general(rel_table, choose, (((0,), (1,)), ((), ())), precision=lax.Precision.HIGHEST)
        tables.append(table.reshape(heads // 2, 2, 4 * BLK))
    lane = (jnp.arange(128, dtype=jnp.int32) % 64)[None, :]
    row = segments.reshape(-1)[:, None]
    same = lane == row
    aug_q = jnp.where(jnp.logical_or(same, lane >= 8), 0.0, NEG).astype(jnp.bfloat16)
    aug_k = jnp.where(jnp.logical_or(same, jnp.logical_and(lane >= 8, lane < 11)), 1.0, 0.0).astype(jnp.bfloat16)
    return aug_q, aug_k, tables[0], tables[1]

def rel_gradient(rel, count):
    lane = jnp.arange(2 * BLK, dtype=jnp.int32)
    parts = []
    for place in range(5):
        if place == 0:
            offset = jnp.full((2 * BLK,), -600, jnp.int32)
        elif place == 4:
            offset = jnp.full((2 * BLK,), 600, jnp.int32)
        else:
            offset = BLK * (place - 2) - jnp.where(lane < BLK, lane, lane - 2 * BLK)
        parts.append(bucket_choice(offset, count))
    choose = jnp.concatenate(parts + [jnp.zeros((3 * 2 * BLK, count), jnp.float32)], axis=0)
    flat = rel.reshape(rel.shape[0], -1)
    return lax.dot_general(choose, flat, (((0,), (1,)), ((), ())), precision=lax.Precision.HIGHEST)


def iota(shape, axis):
    return lax.broadcasted_iota(jnp.int32, shape, axis)


def as_bf16(flag):
    return jnp.where(flag, 1.0, 0.0).astype(jnp.bfloat16)


def slots_kernel(owners, capacity, shift, place_ref, kind_ref, index_ref, coords_ref,
                 meta_ref, keys_ref, text_ref):
    tokens = place_ref.shape[1]
    place = place_ref[...]
    text = kind_ref[...] == 1
    owner = jnp.right_shift(place, shift)
    position = jnp.bitwise_and(place, (1 << shift) - 1)
    rows = owners + 16
    row = iota((rows, tokens), 0)
    member = jnp.logical_or(row == owner, jnp.logical_and(row == owners, text))
    upto = as_bf16(iota((tokens, tokens), 0) <= iota((tokens, tokens), 1))
    counts = dot_nn(as_bf16(member), upto)
    rank = jnp.sum(jnp.where(row == owner, counts, 0.0), axis=0, keepdims=True)
    rank = rank.astype(jnp.int32) - 1
    text_rank = jnp.where(text, counts[owners : owners + 1].astype(jnp.int32) - 1, 0)
    slot = owner * capacity + rank
    index = index_ref[...]
    coords = coords_ref[...]
    low = jnp.bitwise_and(coords, 3)
    high = jnp.right_shift(coords, 2)
    meta = jnp.concatenate(
        [
            kind_ref[...] + 1,
            jnp.right_shift(position, 2), jnp.bitwise_and(position, 3),
            high, low,
            jnp.right_shift(index, 4), jnp.bitwise_and(index, 15),
            jnp.right_shift(text_rank, 2), jnp.bitwise_and(text_rank, 3),
            jnp.zeros_like(index),
        ],
        axis=0,
    ).astype(jnp.float32).astype(jnp.bfloat16)
    slots = meta_ref.shape[1]
    for start in range(0, slots, 512):
        pick = as_bf16(iota((512, tokens), 0) + start == slot)
        meta_ref[:, start : start + 512] = dot_nt(meta, pick).astype(jnp.bfloat16)
        down = dot_nt(pick, meta)
        index = down[:, 11:12] * 16.0 + down[:, 12:13]
        rank = down[:, 13:14] * 4.0 + down[:, 14:15] + float(tokens - text_ref.shape[1])
        key = jnp.where(down[:, 0:1] > 1.5, rank, jnp.where(down[:, 0:1] > 0.5, index, -1.0))
        keys_ref[start : start + 512, :] = jnp.broadcast_to(key.astype(jnp.int32), (512, 8))
    texts = text_ref.shape[1]
    chosen = as_bf16(jnp.logical_and(iota((texts, tokens), 0) == text_rank, text))
    found = dot_nt(meta, chosen)
    text_ref[...] = jnp.broadcast_to(
        (found[11:12] * 16.0 + found[12:13]).astype(jnp.int32), text_ref.shape
    )


def find_slots(line, owners, capacity, shift, placing, src_kind, src_index, coords, texts):
    slots = owners * capacity
    operands = (placing.reshape(1, -1), src_kind.reshape(1, -1), src_index.reshape(1, -1), coords)
    shapes = (bf16(16, slots), i32(slots, 8), i32(8, texts))
    return launch(
        line, partial(slots_kernel, owners, capacity, shift), operands,
        [fixed(value) for value in operands], shapes, [fixed(value) for value in shapes], (1,),
        "find_slots",
    )


def unpack_kernel(key_ref, rows_ref, index_ref, out_ref):
    texts, tokens = index_ref.shape[1], rows_ref.shape[1]
    count, width = rows_ref.shape[0], out_ref.shape[1]
    total = None
    small = None
    for d in range(count):
        pick = as_bf16(iota((texts, tokens), 0) == key_ref[d : d + 1, :])
        part = dot_nn(pick, rows_ref[d])
        total = part if total is None else total + part
        part = join_small(rows_ref[d, tokens - 16 :, :])
        small = part if small is None else small + part
    out_ref[:texts, :] = total.astype(jnp.bfloat16)
    index = index_ref[...]
    row = iota((16, texts), 0)
    high = jnp.broadcast_to(jnp.right_shift(index[0:1], 4), (16, texts))
    low = jnp.broadcast_to(jnp.bitwise_and(index[0:1], 15), (16, texts))
    index = jnp.where(row == 0, high, jnp.where(row == 1, low, 0)).astype(jnp.float32)
    index = jnp.concatenate([index, jnp.zeros((16, width - texts), jnp.float32)], axis=1)
    out_ref[texts : texts + 16, :] = index.astype(jnp.bfloat16)
    out_ref[texts + 16 :, :] = split_small(small)


def unpack_text(line, keys, rows, index):
    width = rows.shape[2]
    shape = bf16(index.shape[1] + 32, width)
    return launch(
        line, unpack_kernel, (keys, rows, index), [fixed(keys), fixed(rows), fixed(index)],
        (shape,), (fixed(shape),), (1,), "unpack_text",
    )[0]


def pack_kernel(key_ref, patch_ref, text_ref, *refs):
    out_ref = refs[len(refs) // 2]
    size, patches, texts = out_ref.shape[0], patch_ref.shape[0], text_ref.shape[0]
    key = key_ref[:, 0:1]
    out = dot_nn(as_bf16(iota((size, patches), 1) == key), patch_ref[...])
    out = out + dot_nn(as_bf16(iota((size, texts), 1) + patches == key), text_ref[...])
    out_ref[...] = out.astype(jnp.bfloat16)

    @pl.when(pl.program_id(0) == 0)
    def _():
        for n in range(len(refs) // 2):
            refs[len(refs) // 2 + 1 + n][...] = refs[n][...]


def pack(line, keys, patches, text_rows, later):
    slots = keys.shape[0]
    width = patches.shape[1]
    return launch(
        line, pack_kernel, (keys, patches, text_rows) + later,
        [pl.BlockSpec((512, 8), lambda i: (i, 0)), fixed(patches), fixed(text_rows)]
        + [fixed(value) for value in later],
        (bf16(slots, width),) + later,
        (pl.BlockSpec((512, width), lambda i: (i, 0)),) + tuple(fixed(value) for value in later),
        (slots // 512,), "pack",
    )


def place_kernel(meta_ref, column_ref, row_ref, place_ref):
    slots, tokens = meta_ref.shape[1], row_ref.shape[1]
    meta = meta_ref[...]
    wide = meta.astype(jnp.float32)
    place = (wide[1:2] * 4.0 + wide[2:3]).astype(jnp.int32)
    place = jnp.where(wide[0:1] > 0.5, place, -1)
    place_ref[...] = jnp.broadcast_to(place, place_ref.shape)
    for start in range(0, tokens, 256):
        pick = as_bf16(iota((256, slots), 0) + start == place)
        down = dot_nt(pick, meta)
        values = [down[:, 0:1]] + [down[:, 3 + c : 4 + c] * 4.0 + down[:, 7 + c : 8 + c] for c in range(4)]
        lane = iota((256, 8), 1)
        block = jnp.zeros((256, 8), jnp.float32)
        for c in range(5):
            block = jnp.where(lane == c, values[c], block)
        column_ref[start : start + 256, :] = block.astype(jnp.int32)
        across = dot_nt(meta, pick)
        row_ref[:, start : start + 256] = jnp.concatenate(
            [across[0:1], across[3:7] * 4.0 + across[7:11], jnp.zeros((3, 256), jnp.float32)], axis=0
        ).astype(jnp.int32)


def place_meta(line, meta, tokens):
    shapes = (i32(tokens, 8), i32(8, tokens), i32(8, meta.shape[1]))
    return launch(
        line, place_kernel, (meta,), [fixed(meta)], shapes, [fixed(value) for value in shapes],
        (1,), "place_meta",
    )


def lookup_kernel(rows, fresh, side, mine_ref, other_ref, table_ref, *refs):
    width = table_ref.shape[2]
    outs = refs[-2:]
    entries = table_ref.shape[0] * rows
    for n, coords in enumerate((mine_ref, other_ref)):
        total = jnp.zeros(outs[n].shape, jnp.float32) if fresh else refs[n][...]
        for k in range(2):
            key = jnp.where(side[0] == 0, coords[:, k + 1 : k + 2], coords[:, k + 3 : k + 4])
            pick = as_bf16(iota((total.shape[0], entries), 1) == key)
            table = table_ref[:, k * rows : k * rows + rows, :].reshape(entries, width)
            total = total + dot_nn(pick, table)
        outs[n][...] = total


def layout_lookup(line, side, mine, other, columns, rows, sums=()):
    tokens = mine.shape[0]
    width = columns.shape[2]
    column = pl.BlockSpec((256, 8), lambda i, s: (i, 0))
    out = pl.BlockSpec((256, width), lambda i, s: (i, 0))
    return launch(
        line, partial(lookup_kernel, rows, not sums), (mine, other, columns, *sums),
        [column, column, fixed(columns)] + [out] * len(sums),
        (f32(tokens, width), f32(tokens, width)), (out, out), (tokens // 256,), "layout_lookup",
        scalars=(side,),
    )


def embed_kernel(place_ref, column_ref, arrived_ref, own_ref, got_ref, half_ref, project_ref,
                 gain_ref, weight_ref, visual_ref, packed_ref, normed_ref, out_ref):
    rows, slots = packed_ref.shape[0], arrived_ref.shape[0]
    pick = as_bf16(iota((rows, slots), 0) + pl.program_id(0) * rows == place_ref[0:1, :])
    raw = dot_nn(pick, arrived_ref[...])
    narrow = raw.astype(jnp.bfloat16)
    kind = column_ref[:, 0:1]
    visual_ref[...] = jnp.where(kind == 1, raw, 0.0).T.astype(jnp.bfloat16)
    projected = dot_nn(narrow, project_ref[...])
    first = half_ref[0:1, 0:1] == 0
    own, got = own_ref[...], got_ref[...]
    layout = jnp.concatenate([jnp.where(first, own, got), jnp.where(first, got, own)], axis=1)
    embedded = jnp.where(kind == 2, raw, projected) + layout
    packed_ref[...] = embedded.astype(jnp.bfloat16)
    packed = packed_ref[...].astype(jnp.float32)
    scale = lax.rsqrt(jnp.mean(packed * packed, axis=-1, keepdims=True) + EPSILON)
    normed = packed * scale * gain_ref[0:1, :].astype(jnp.float32)
    normed_ref[...] = normed.T.astype(jnp.bfloat16)
    normed = normed.astype(jnp.bfloat16)
    for part in range(3):
        out_ref[part] = dot_nn(normed, weight_ref[part]).astype(jnp.bfloat16)


def embed(line, places, column, arrived, own, got, half, matrices, gains, tokens):
    width = arrived.shape[1]
    rows = 256
    wide = pl.BlockSpec((rows, width), lambda i: (i, 0))
    part = pl.BlockSpec((rows, own.shape[1]), lambda i: (i, 0))
    across = pl.BlockSpec((width, rows), lambda i: (0, i))
    return launch(
        line, embed_kernel, (places, column, arrived, own, got, half, matrices, gains, matrices),
        [
            fixed(places), pl.BlockSpec((rows, 8), lambda i: (i, 0)), fixed(arrived), part, part,
            fixed(half), pl.BlockSpec((None, width, width), lambda i: (3, 0, 0)), fixed(gains),
            pl.BlockSpec((3, width, width), lambda i: (0, 0, 0)),
        ],
        (bf16(width, tokens), bf16(tokens, width), bf16(width, tokens), bf16(3, tokens, width)),
        (across, wide, across, pl.BlockSpec((3, rows, width), lambda i: (0, i, 0))),
        (tokens // rows,), "embed",
    )


def input_grad_kernel(which, packed_ref, upper_ref, grads_ref, weight_ref, gain_ref,
                      out_ref, own_ref, other_ref, sum_ref):
    total = dot_nt(grads_ref[0], weight_ref[0])
    total = total + dot_nt(grads_ref[1], weight_ref[1])
    total = total + dot_nt(grads_ref[2], weight_ref[2])
    packed = packed_ref[...].astype(jnp.float32)
    scale = lax.rsqrt(jnp.mean(packed * packed, axis=-1, keepdims=True) + EPSILON)
    unit = packed * scale
    back = total * gain_ref[0:1, :].astype(jnp.float32)
    back = scale * (back - unit * jnp.mean(back * unit, axis=-1, keepdims=True))
    back = back + upper_ref[...]
    out_ref[...] = back.astype(jnp.bfloat16)
    put_halves(which, back, own_ref, other_ref)

    @pl.when(pl.program_id(0) == 0)
    def _():
        sum_ref[...] = jnp.zeros_like(sum_ref)

    sum_ref[0:1, :] += jnp.sum(total * unit, axis=0, keepdims=True)


def input_grad(line, which, packed, upper, grads, matrices, gains):
    tokens, width = packed.shape
    rows = 256
    half = width // 2
    wide = pl.BlockSpec((rows, width), lambda i, w: (i, 0))
    part = pl.BlockSpec((rows, half), lambda i, w: (i, 0))
    return launch(
        line, input_grad_kernel, (packed, upper, grads, matrices, gains),
        [
            wide, wide, pl.BlockSpec((3, rows, width), lambda i, w: (0, i, 0)),
            pl.BlockSpec((3, width, width), lambda i, w: (0, 0, 0)), fixed(gains),
        ],
        (bf16(tokens, width), bf16(tokens, half), bf16(tokens, half), f32(8, width)),
        (wide, part, part, pl.BlockSpec((8, width), lambda i, w: (0, 0))),
        (tokens // rows,), "input_grad", scalars=(which,),
    )


def split_small(small):
    parts = [part.astype(jnp.float32) for part in pieces(small)]
    pad = jnp.zeros((16 - 3 * small.shape[0], small.shape[1]), jnp.float32)
    return jnp.concatenate(parts + [pad], axis=0).astype(jnp.bfloat16)


def join_small(rows):
    rows = rows[:9].astype(jnp.float32)
    return rows[0:3] + rows[3:6] + rows[6:9]


def return_kernel(place_ref, rows_ref, small_ref, out_ref):
    capacity = place_ref.shape[0]
    pick = as_bf16(iota((capacity, rows_ref.shape[0]), 1) == place_ref[...])
    out_ref[:capacity, :] = dot_nn(pick, rows_ref[...]).astype(jnp.bfloat16)
    out_ref[capacity:, :] = split_small(small_ref[0:3, :])


def return_rows(line, places, rows, small, capacity):
    count = places.shape[0] // capacity
    width = rows.shape[1]
    return launch(
        line, return_kernel, (places, rows, small),
        [pl.BlockSpec((capacity, 1), lambda i: (i, 0)), fixed(rows), fixed(small)],
        (bf16(count, capacity + 16, width),),
        (pl.BlockSpec((None, capacity + 16, width), lambda i: (i, 0, 0)),), (count,), "return_rows",
    )[0]


def layout_grad_kernel(side, mine_ref, other_ref, first_ref, second_ref, keep_ref, give_ref):
    pair = pl.program_id(0)
    shards, rows, width = keep_ref.shape
    entries = shards * rows
    table = 2 * jnp.where(pair < 2, 1 - side[0], side[0]) + jnp.bitwise_and(pair, 1)
    total = jnp.zeros((entries, width), jnp.float32)
    for coords, grads in ((mine_ref, first_ref), (other_ref, second_ref)):
        tokens = grads.shape[0]
        key = coords[pl.ds(table + 1, 1), :]
        pick = as_bf16(iota((entries, tokens), 0) + pl.program_id(1) * entries == key)
        total = total + dot_nn(pick, grads[...])
    total = total.reshape(shards, rows, width).astype(jnp.bfloat16)

    @pl.when(pair < 2)
    def _():
        give_ref[...] = total

    @pl.when(pair >= 2)
    def _():
        keep_ref[...] = total


def layout_grad(line, side, mine, other, first, second, shards, rows):
    width = first.shape[1]
    step = max(1, min(shards, 512 // rows))
    last = shards // step - 1
    block = (step, None, rows, width)
    shape = bf16(shards, 2, rows, width)
    return launch(
        line, layout_grad_kernel, (mine, other, first, second),
        [fixed(mine), fixed(other), fixed(first), fixed(second)], (shape, shape),
        (
            pl.BlockSpec(
                block, lambda t, i, s: (jnp.where(t < 2, 0, i), jnp.maximum(t - 2, 0), 0, 0)
            ),
            pl.BlockSpec(
                block, lambda t, i, s: (jnp.where(t < 2, i, last), jnp.minimum(t, 1), 0, 0)
            ),
        ),
        (4, shards // step), "layout_grad", scalars=(side,),
    )


def patch_kernel(key_ref, rows_ref, weight_ref, grad_ref):
    patches, tokens = grad_ref.shape[0], rows_ref.shape[1]
    total = None
    for d in range(rows_ref.shape[0]):
        pick = as_bf16(iota((patches, tokens), 0) == key_ref[d : d + 1, :])
        part = dot_nn(pick, rows_ref[d])
        total = part if total is None else total + part
    grad_ref[...] = dot_nt(total.astype(jnp.bfloat16), weight_ref[...])


def patch_grads(line, keys, rows, matrices, patches):
    width = rows.shape[2]
    shape = f32(patches, width)
    return launch(
        line, patch_kernel, (keys, rows, matrices),
        [fixed(keys), fixed(rows), pl.BlockSpec((None, width, width), lambda i: (3, 0, 0))],
        (shape,), (fixed(shape),), (1,), "patch_grads",
    )[0]


def text_kernel(*refs):
    out_ref = refs[4]
    size = out_ref.shape[0]
    parts = []
    for rows_ref in refs[:4]:
        texts = rows_ref.shape[0] - 32
        index = rows_ref[texts : texts + 16, :texts].astype(jnp.float32)
        key = (index[0:1] * 16.0 + index[1:2]).astype(jnp.int32)
        place = iota((size, texts), 0) + pl.program_id(0) * size
        parts.append(dot_nn(as_bf16(place == key), rows_ref[:texts, :]))
    out_ref[...] = (parts[0] + parts[1]) + (parts[2] + parts[3])


def text_grads(line, rows, entries):
    width = rows[0].shape[1]
    size = 512
    return launch(
        line, text_kernel, rows, [fixed(value) for value in rows],
        (f32(entries, width),), (pl.BlockSpec((size, width), lambda i: (i, 0)),),
        (pl.cdiv(entries, size),), "text_grads",
    )[0]


def feed_forward_kernel(core, packed_ref, mixed_ref, grad_ref, own_ref, other_ref, in_ref, down_ref,
                        gain_ref, result_ref, active_ref, hidden_ref, normed_ref, turned_ref, upper_ref,
                        branch_ref, back_ref, sum_ref):
    own, other = own_ref[...], other_ref[...]
    first = core[0] == 0
    mix = jnp.concatenate([jnp.where(first, own, other), jnp.where(first, other, own)], axis=1)
    attended = packed_ref[...].astype(jnp.float32) + dot_nn(mixed_ref[...], mix)
    turned_ref[...] = mixed_ref[...].astype(jnp.float32).T.astype(jnp.bfloat16)
    scale = lax.rsqrt(jnp.mean(attended * attended, axis=-1, keepdims=True) + EPSILON)
    unit = attended * scale
    gain = gain_ref[0:1, :].astype(jnp.float32)
    normed = unit * gain
    normed_ref[...] = normed.T.astype(jnp.bfloat16)
    normed = normed.astype(jnp.bfloat16)
    out_grad = grad_ref[...]
    result = attended
    back = jnp.zeros_like(attended)
    width = attended.shape[1]
    for part in range(in_ref.shape[0]):
        cut = slice(part * width, part * width + width)
        hidden = dot_nn(normed, in_ref[part])
        square = hidden * hidden
        tanh = jnp.tanh(hidden * (RATE + RATE * 0.044715 * square))
        half = 0.5 + 0.5 * tanh
        active = hidden * half
        active_ref[cut, :] = active.T.astype(jnp.bfloat16)
        active = active.astype(jnp.bfloat16)
        slope = half + hidden * half * (1.0 - tanh) * (RATE + 3.0 * 0.044715 * RATE * square)
        result = result + dot_nn(active, down_ref[cut, :])
        grad_hidden = (dot_nt(out_grad, down_ref[cut, :]) * slope).astype(jnp.bfloat16)
        hidden_ref[:, cut] = grad_hidden
        back = back + dot_nt(grad_hidden, in_ref[part])
    result_ref[...] = result.astype(jnp.bfloat16)

    @pl.when(pl.program_id(0) == 0)
    def _():
        sum_ref[...] = jnp.zeros_like(sum_ref)

    sum_ref[0:1, :] += jnp.sum(back * unit, axis=0, keepdims=True)
    back = back * gain
    back = scale * (back - unit * jnp.mean(back * unit, axis=-1, keepdims=True))
    back = back + out_grad.astype(jnp.float32)
    upper_ref[...] = back
    branch = back.astype(jnp.bfloat16)
    branch_ref[...] = branch
    back_ref[...] = dot_nt(branch, mix).astype(jnp.bfloat16)


def feed_forward(line, core, packed, mixed, out_grad, mix_own, mix_other, full_in, full_down, gains):
    tokens, width = packed.shape
    hidden = full_down.shape[0]
    rows = 256
    wide = pl.BlockSpec((rows, width), lambda i, c: (i, 0))
    tall = pl.BlockSpec((rows, hidden), lambda i, c: (i, 0))
    across = pl.BlockSpec((width, rows), lambda i, c: (0, i))
    narrow, turned = bf16(tokens, width), bf16(width, tokens)
    operands = (packed, mixed, out_grad, mix_own, mix_other, full_in, full_down, gains)
    return launch(
        line, feed_forward_kernel, operands,
        [wide, wide, wide] + [fixed(value) for value in operands[3:]],
        (
            narrow, bf16(hidden, tokens), bf16(tokens, hidden), turned, turned,
            f32(tokens, width), narrow, narrow, f32(8, width),
        ),
        (
            wide, pl.BlockSpec((hidden, rows), lambda i, c: (0, i)), tall, across, across,
            wide, wide, wide, pl.BlockSpec((8, width), lambda i, c: (0, 0)),
        ),
        (tokens // rows,), "feed_forward", scalars=(core,),
    )


def put_halves(which, total, keep_ref, give_ref):
    half = total.shape[1] // 2
    first, second = total[:, :half], total[:, half:]
    mine = which[0] == 0
    keep_ref[...] = jnp.where(mine, first, second).astype(jnp.bfloat16)
    give_ref[...] = jnp.where(mine, second, first).astype(jnp.bfloat16)


def contract_halves_kernel(which, left_ref, right_ref, keep_ref, give_ref):
    put_halves(which, dot_nn(left_ref[...], right_ref[...]), keep_ref, give_ref)


def contract_halves(line, which, left, right):
    count, tokens = left.shape
    width = right.shape[1]
    size, half = min(count, width), width // 2
    out = pl.BlockSpec((size, half), lambda i, w: (i, 0))
    shape = bf16(count, half)
    return launch(
        line, contract_halves_kernel, (left, right),
        [pl.BlockSpec((size, tokens), lambda i, w: (i, 0)), fixed(right)],
        (shape, shape), (out, out), (count // size,), "contract_halves", scalars=(which,),
    )


def contract_quarters_kernel(which, left_ref, right_ref, keep_ref, give_ref):
    del which
    total = dot_nn(left_ref[...], right_ref[...])
    shards, _, rows, half = keep_ref.shape

    def put(out_ref):
        for d in range(shards):
            for h in range(2):
                part = total[d * rows : d * rows + rows, h * half : h * half + half]
                out_ref[d, h] = part.astype(jnp.bfloat16)

    @pl.when(pl.program_id(0) < 2)
    def _():
        put(give_ref)

    @pl.when(pl.program_id(0) >= 2)
    def _():
        put(keep_ref)


def contract_quarters(line, which, left, right, shards):
    count, tokens = left.shape
    quarter = right.shape[1] // 4
    block = (shards, 2, count // shards, quarter // 2)
    shape = bf16(2, *block)

    def column(i, w):
        return (0, jnp.where(i < 2, 2 * i + 1 - w[0], 2 * (i - 2) + w[0]))

    return launch(
        line, contract_quarters_kernel, (left, right),
        [fixed(left), pl.BlockSpec((tokens, quarter), column)], (shape, shape),
        (
            pl.BlockSpec((None,) + block, lambda i, w: (jnp.maximum(i - 2, 0), 0, 0, 0, 0)),
            pl.BlockSpec((None,) + block, lambda i, w: (jnp.minimum(i, 1), 0, 0, 0, 0)),
        ),
        (4,), "contract_quarters", scalars=(which,),
    )


def square_kernel(which, normed_ref, grads_ref, visual_ref, packed_ref, keep_ref, give_ref):
    shards, rows, half = keep_ref.shape

    def put(total):
        mine = which[0] == 0
        for d in range(shards):
            part = total[d * rows : d * rows + rows]
            first, second = part[:, :half], part[:, half:]
            keep_ref[d] = jnp.where(mine, first, second).astype(jnp.bfloat16)
            give_ref[d] = jnp.where(mine, second, first).astype(jnp.bfloat16)

    @pl.when(pl.program_id(0) < 3)
    def _():
        put(dot_nn(normed_ref[...], grads_ref[...]))

    @pl.when(pl.program_id(0) == 3)
    def _():
        put(dot_nn(visual_ref[...], packed_ref[...]))


def square_grads(line, which, normed, grads, visual, grad_packed, shards):
    width, tokens = normed.shape
    rows, half = width // shards, width // 2
    out = pl.BlockSpec((shards, None, None, rows, half), lambda m, w: (0, m // 2, m % 2, 0, 0))
    shape = bf16(shards, 2, 2, rows, half)
    return launch(
        line, square_kernel, (normed, grads, visual, grad_packed),
        [
            fixed(normed),
            pl.BlockSpec((None, tokens, width), lambda m, w: (jnp.minimum(m, 2), 0, 0)),
            fixed(visual), fixed(grad_packed),
        ],
        (shape, shape), (out, out), (4,), "square_grads", scalars=(which,),
    )


def fold_kernel(bit, value_ref, got_ref, keep_ref, give_ref):
    del bit
    total = value_ref[...].astype(jnp.float32) + got_ref[...].astype(jnp.float32)

    @pl.when(pl.program_id(0) == 0)
    def _():
        give_ref[...] = total.astype(give_ref.dtype)

    @pl.when(pl.program_id(0) == 1)
    def _():
        keep_ref[...] = total.astype(keep_ref.dtype)


def fold(line, bit, value, got):
    a, _, b, rows, width = value.shape
    step = a
    while step > 1 and step * b * rows * width * value.dtype.itemsize > 800_000:
        step //= 2
    count = a // step
    source = pl.BlockSpec(
        (step, None, b, rows, width), lambda n, i, s: (i, jnp.where(n == 0, 1 - s[0], s[0]), 0, 0, 0)
    )
    block = (step, b, rows, width)
    shape = jax.ShapeDtypeStruct((a, b, rows, width), value.dtype)
    return launch(
        line, fold_kernel, (value, got), [source, source], (shape, shape),
        (
            pl.BlockSpec(block, lambda n, i, s: (jnp.where(n == 0, 0, i), 0, 0, 0)),
            pl.BlockSpec(block, lambda n, i, s: (jnp.where(n == 0, i, count - 1), 0, 0, 0)),
        ),
        (2, count), "fold", scalars=(bit,),
    )


def add_kernel(value_ref, got_ref, out_ref):
    total = value_ref[...].astype(jnp.float32) + got_ref[...].astype(jnp.float32)
    out_ref[...] = total.astype(out_ref.dtype)


def add(line, value, got):
    shape = jax.ShapeDtypeStruct(value.shape, value.dtype)
    return launch(
        line, add_kernel, (value, got), [fixed(value), fixed(got)], (shape,), (fixed(shape),),
        (1,), "add",
    )[0]


def rows_fold_kernel(side, down_ref, down_got_ref, mix_ref, mix_got_ref, keep_ref, give_ref):
    del side
    down = down_ref[...].astype(jnp.float32) + down_got_ref[...].astype(jnp.float32)
    mix = mix_ref[...].astype(jnp.float32) + mix_got_ref[...].astype(jnp.float32)
    total = jnp.concatenate([down, mix], axis=1).astype(jnp.bfloat16)

    @pl.when(pl.program_id(0) == 0)
    def _():
        give_ref[...] = total

    @pl.when(pl.program_id(0) == 1)
    def _():
        keep_ref[...] = total


def rows_fold(line, side, down, down_got, mix, mix_got):
    parts, _, rows, width = down.shape
    extra = mix.shape[2]
    step = max(1, parts // 2)

    def source(count):
        return pl.BlockSpec(
            (step, None, count, width), lambda n, i, s: (i, jnp.where(n == 0, 1 - s[0], s[0]), 0, 0)
        )

    shape = bf16(parts, rows + extra, width)
    block = (step, rows + extra, width)
    last = parts // step - 1
    return launch(
        line, rows_fold_kernel, (down, down_got, mix, mix_got),
        [source(rows), source(rows), source(extra), source(extra)], (shape, shape),
        (
            pl.BlockSpec(block, lambda n, i, s: (jnp.where(n == 0, 0, i), 0, 0)),
            pl.BlockSpec(block, lambda n, i, s: (jnp.where(n == 0, i, last), 0, 0)),
        ),
        (2, parts // step), "rows_fold", scalars=(side,),
    )


def stack_kernel(bit, value_ref, got_ref, out_ref):
    del bit

    @pl.when(pl.program_id(0) == 0)
    def _():
        out_ref[...] = value_ref[...]

    @pl.when(pl.program_id(0) == 1)
    def _():
        out_ref[...] = got_ref[...]


def stack(line, bit, value, got):
    a, rows, width = value.shape
    return launch(
        line, stack_kernel, (value, got), [fixed(value), fixed(got)],
        (jax.ShapeDtypeStruct((a, 2, rows, width), value.dtype),),
        (
            pl.BlockSpec(
                (a, None, rows, width), lambda n, s: (0, jnp.where(n == 0, s[0], 1 - s[0]), 0, 0)
            ),
        ),
        (2,), "stack", scalars=(bit,),
    )[0]


def split_stack_kernel(parts, bit, value_ref, got_ref, *outs):
    del bit

    def put(source_ref):
        start = 0
        for rows, out_ref in zip(parts, outs):
            out_ref[...] = source_ref[:, start : start + rows, :]
            start += rows

    @pl.when(pl.program_id(0) == 0)
    def _():
        put(value_ref)

    @pl.when(pl.program_id(0) == 1)
    def _():
        put(got_ref)


def split_stack(line, bit, value, got, parts):
    a, _, width = value.shape
    return launch(
        line, partial(split_stack_kernel, parts), (value, got), [fixed(value), fixed(got)],
        [bf16(a, 2, rows, width) for rows in parts],
        [
            pl.BlockSpec(
                (a, None, rows, width), lambda n, s: (0, jnp.where(n == 0, s[0], 1 - s[0]), 0, 0)
            )
            for rows in parts
        ],
        (2,), "split_stack", scalars=(bit,),
    )


def both_sides(line, side, value, got):
    return stack(line, side, value, got)


def arrange_kernel(me, *refs):
    del me
    for n in range(4):

        @pl.when(pl.program_id(0) == n)
        def _():
            refs[4][...] = refs[n][...]


def arrange(line, me, values):
    shape = values[0].shape
    return launch(
        line, arrange_kernel, tuple(values), [fixed(value) for value in values],
        (bf16(4, *shape),),
        (pl.BlockSpec((None,) + shape, lambda n, s: (jnp.bitwise_xor(n, s[0]), 0, 0)),),
        (4,), "arrange", scalars=(me,),
    )[0]


def assemble_forward_kernel(me, *refs):
    del me
    down_ref, mix_ref, in_ref = refs[4:]
    for n in range(4):

        @pl.when(pl.program_id(0) == n)
        def _():
            start = 0
            for out_ref in (down_ref, mix_ref):
                rows = out_ref.shape[0]
                out_ref[...] = refs[n][start : start + rows, :].astype(jnp.float32)
                start += rows
            rows = in_ref.shape[0]
            first = refs[n][start : start + rows, :]
            second = refs[n][start + rows : start + 2 * rows, :]
            in_ref[...] = jnp.concatenate([first, second], axis=1).astype(jnp.float32)


def assemble_forward(line, me, values, down_rows, mix_rows, shard_rows):
    half = values[0].shape[1]

    def part(rows):
        return pl.BlockSpec(
            (None, rows, half),
            lambda n, s: (jnp.bitwise_xor(n, s[0]) // 2, 0, jnp.bitwise_xor(n, s[0]) % 2),
        )

    return launch(
        line, assemble_forward_kernel, tuple(values), [fixed(value) for value in values],
        (
            f32(2, down_rows, 2 * half), f32(2, mix_rows, 2 * half), f32(shard_rows, 8 * half),
        ),
        (
            part(down_rows), part(mix_rows),
            pl.BlockSpec((shard_rows, 2 * half), lambda n, s: (0, jnp.bitwise_xor(n, s[0]))),
        ),
        (4,), "assemble_forward", scalars=(me,),
    )


def assemble_backward_kernel(me, *refs):
    layout_ref, qkv_ref, project_ref = refs[4:]
    device, k = pl.program_id(0), pl.program_id(1)
    layout_rows, rows = layout_ref.shape[0], project_ref.shape[0]
    for n in range(4):

        @pl.when(device == jnp.bitwise_xor(me[0], n))
        def _():
            for part in range(2):

                @pl.when(k == part)
                def _():
                    start = part * layout_rows
                    layout_ref[...] = refs[n][start : start + layout_rows, :].astype(jnp.float32)
                    start = 2 * layout_rows + part * rows
                    matrix = refs[n][start : start + rows, :].astype(jnp.float32)
                    last = jnp.logical_and(device >= 2, k == 1)

                    @pl.when(jnp.logical_not(last))
                    def _():
                        qkv_ref[...] = matrix

                    @pl.when(last)
                    def _():
                        project_ref[...] = matrix


def assemble_backward(line, me, values, layout_rows, rows):
    half = values[0].shape[1]
    return launch(
        line, assemble_backward_kernel, tuple(values), [fixed(value) for value in values],
        (f32(4, layout_rows, 2 * half), f32(3, rows, 2 * half), f32(rows, 2 * half)),
        (
            pl.BlockSpec(
                (None, layout_rows, half), lambda t, k, s: (2 * (t // 2) + k, 0, t % 2)
            ),
            pl.BlockSpec(
                (None, rows, half), lambda t, k, s: (jnp.minimum(2 * (t // 2) + k, 2), 0, t % 2)
            ),
            pl.BlockSpec((rows, half), lambda t, k, s: (0, jnp.where(t == 3, 1, 0))),
        ),
        (4, 2), "assemble_backward", scalars=(me,),
    )


def swap(value, axis, bit):
    count = lax.axis_size(axis)
    return lax.ppermute(value, axis, [(i, i ^ bit) for i in range(count)])


def bit_of(axis, bit):
    return jnp.bitwise_and(lax.axis_index(axis), bit) != 0


def bit_index(axis, bit):
    return bit_of(axis, bit).astype(jnp.int32).reshape(1)


class Gather:
    def __init__(self, line, value):
        self.line = line
        self.value = value[None]
        self.bit = lax.axis_size("dp") // 2
        self.got = swap(self.value, "dp", self.bit)

    def step(self):
        rows, width = self.value.shape[1:]
        value = stack(self.line, bit_index("dp", self.bit), self.value, self.got)
        self.value = value.reshape(-1, rows, width)
        self.bit //= 2
        self.got = swap(self.value, "dp", self.bit)

    def finish(self, parts):
        while self.bit > 1:
            self.step()
        values = split_stack(self.line, bit_index("dp", 1), self.value, self.got, parts)
        return [value.reshape((-1,) + value.shape[2:]) for value in values]


def padded(value):
    return jnp.pad(value, ((0, -value.shape[0] % 16), (0, 0)))


class Sum:
    def __init__(self, line, bits, value, got):
        self.line, self.bits, self.value, self.got = line, list(bits), value, got
        self.done = False

    def step(self):
        if self.done:
            return
        rows, width = self.value.shape[-2:]
        if not self.bits:
            self.value = add(self.line, self.value.reshape(rows, width), self.got.reshape(rows, width))
            self.done = True
            return
        bit = self.bits.pop()
        shape = (-1, 2, 1, rows, width)
        value, give = fold(
            self.line, bit_index("dp", bit), self.value.reshape(shape), self.got.reshape(shape)
        )
        self.value, self.got = value, swap(give, "dp", bit)

    def finish(self):
        while not self.done:
            self.step()
        return self.value


def shards(
    patches,
    src_kind,
    src_index,
    layout_coords,
    placing,
    segments,
    text_table,
    layout_tables,
    patch_proj,
    rel_table,
    norm_gains,
    w_qkv,
    w_attn_out,
    w_ff_in,
    w_ff_out,
    out_grad,
):
    data_count = lax.axis_size("dp")
    tokens = placing.shape[0]
    capacity = 2 * tokens // data_count
    width = text_table.shape[1]
    half_width = width // 2
    texts = tokens - patches.shape[0]
    shift = tokens.bit_length() - 1
    shard_rows = w_attn_out.shape[0]
    layout_rows = layout_tables.shape[1]
    stream = lax.axis_index("stream")
    core = jnp.bitwise_and(stream, 1)
    side = jnp.right_shift(stream, 1)
    gain_count = norm_gains.shape[1]

    own_core, own_side = core.reshape(1), side.reshape(1)
    dp_bits = [1 << n for n in reversed(range(data_count.bit_length() - 1))]
    line = Line()

    def own_half(value):
        return lax.dynamic_slice_in_dim(value, core * half_width, half_width, axis=-1)

    in_quarter = lax.dynamic_index_in_dim(
        w_ff_in.reshape(shard_rows, 4, -1), stream, 1, keepdims=False
    )
    down_quarter = lax.dynamic_index_in_dim(
        w_ff_out.reshape(4, -1, width), stream, 0, keepdims=False
    )
    layout_part = own_half(
        lax.dynamic_slice_in_dim(layout_tables, side * 2, 2, axis=0)
    ).reshape(-1, half_width)
    mix_part = own_half(
        lax.dynamic_slice_in_dim(w_attn_out, side * (shard_rows // 2), shard_rows // 2, axis=0)
    )
    gain_part = jnp.pad(norm_gains, ((0, 0), (0, half_width - gain_count)))
    table_rows, mix_rows = layout_part.shape[0], mix_part.shape[0]
    square = jnp.concatenate([w_qkv, patch_proj[None]], axis=0)
    square = lax.dynamic_index_in_dim(square, stream, 0, keepdims=False)
    mix_part, gain_part = padded(mix_part), padded(gain_part)
    columns = Gather(line, jnp.concatenate([layout_part, mix_part, gain_part], axis=0))
    square = Gather(line, square)
    full_in = lax.all_gather(in_quarter, ("stream", "dp"), axis=0, tiled=True)
    full_in = full_in.reshape(4, width, -1)

    meta, slot_keys, text_index = find_slots(
        line, data_count, capacity, shift, placing, src_kind, src_index, layout_coords, texts
    )
    arrived_meta = lax.all_to_all(
        meta.reshape(16, data_count, capacity), "dp", split_axis=1, concat_axis=1, tiled=True
    ).reshape(16, -1)
    columns.step()
    square.step()
    columns.step()
    square.step()
    column, across, place = place_meta(line, arrived_meta, tokens)
    column_other = swap(column, "stream", 1)
    across_other = column_other.T
    tables, mix, gains = columns.finish((table_rows, mix_part.shape[0], gain_part.shape[0]))
    tables_got = swap(tables, "stream", 2)
    (square,) = square.finish((shard_rows,))
    square = square.reshape(width, width)
    square_got = swap(square, "stream", 2)
    mix_got = swap(mix, "stream", 2)
    gains = gains[:, :2, :gain_count].transpose(1, 0, 2).reshape(2, width)
    text_rows = jnp.take(text_table, text_index[0], axis=0)
    send_rows, down_quarter = pack(line, slot_keys, patches, text_rows, (down_quarter,))
    arrived = lax.all_to_all(
        send_rows.reshape(data_count, capacity, width), "dp", split_axis=0, concat_axis=0, tiled=True
    ).reshape(-1, width)
    full_down = lax.all_gather(down_quarter, ("dp", "stream"), axis=0, tiled=True)
    sums = layout_lookup(line, own_side, column, column_other, tables, layout_rows)
    matrices = arrange(
        line, stream.reshape(1),
        (square, swap(square, "stream", 1), square_got, swap(square_got, "stream", 1)),
    )
    own_sum, other_sum = layout_lookup(
        line, 1 - own_side, column, column_other, tables_got, layout_rows, sums
    )
    got_sum = swap(other_sum, "stream", 1)
    half_index = jnp.broadcast_to(core, (8, 128)).astype(jnp.int32)
    visual, packed, normed_one, projections = embed(
        line, place, column, arrived, own_sum, got_sum, half_index, matrices, gains[:1], tokens
    )
    mix_own = both_sides(line, own_side, mix, mix_got)
    mix_own = mix_own[:, :, :mix_rows].reshape(width, half_width)
    mix_other = swap(mix_own, "stream", 1)
    aug_q, aug_k, table, mirrored = prepare(segments, rel_table)
    mixed, lse = attention_forward(line, projections, aug_q, aug_k, table)
    (
        result, active, grad_hidden, normed_two, turned, upper, grad_branch, grad_mixed,
        gain_two_sum,
    ) = feed_forward(
        line, own_core, packed, mixed, out_grad, mix_own, mix_other, full_in, full_down, gains[1:]
    )

    down_keep, down_give = contract_halves(line, own_core, active, out_grad)
    down_got = swap(down_give, "stream", 1)
    mix_keep, mix_give = contract_halves(line, own_core, turned, grad_branch)
    mix_got = swap(mix_give, "stream", 1)
    in_keep, in_give = contract_quarters(
        line, own_core, normed_two, grad_hidden, data_count
    )
    in_got = swap(in_give, "stream", 1)
    down_shape = (data_count, 2, down_keep.shape[0] // data_count // 2, half_width)
    mix_shape = (data_count, 2, mix_rows, half_width)
    rows_keep, rows_give = rows_fold(
        line, own_side, down_keep.reshape(down_shape), down_got.reshape(down_shape),
        mix_keep.reshape(mix_shape), mix_got.reshape(mix_shape),
    )
    rows_got = swap(rows_give, "stream", 2)
    in_shape = (data_count, 2, 2 * shard_rows, half_width)
    in_keep, in_give = fold(
        line, bit_index("dp", 1), in_keep.reshape(in_shape)[:, :, None],
        in_got.reshape(in_shape)[:, :, None],
    )
    in_got = swap(in_give, "dp", 1)

    qkv_grads, grad_rel = attention_backward(
        line, projections, mixed, grad_mixed, lse, aug_q, aug_k, mirrored
    )
    rows_shape = (data_count // 2, 2, 1) + rows_keep.shape[1:]
    rows_keep, rows_give = fold(
        line, bit_index("dp", 1), rows_keep.reshape(rows_shape), rows_got.reshape(rows_shape)
    )
    rows_got = swap(rows_give, "dp", 1)
    in_shape = (1, 2, data_count // 2, 2 * shard_rows, half_width)
    in_keep, in_give = fold(line, own_side, in_keep.reshape(in_shape), in_got.reshape(in_shape))
    in_got = swap(in_give, "stream", 2)
    grad_packed, own_columns, other_columns, gain_one_sum = input_grad(
        line, own_core, packed, upper, qkv_grads, matrices, gains[:1]
    )
    other_columns = swap(other_columns, "stream", 1)
    rows_shape = (data_count // 4, 2) + rows_keep.shape[-2:]
    in_shape = (data_count // 4, 2) + in_keep.shape[-2:]
    value, give = rows_fold(
        line, bit_index("dp", 2), rows_keep.reshape(rows_shape), rows_got.reshape(rows_shape),
        in_keep.reshape(in_shape), in_got.reshape(in_shape),
    )
    forward_sum = Sum(line, dp_bits[:-2], value, swap(give, "dp", 2))
    rel = rel_gradient(grad_rel, rel_table.shape[0])
    rel_row = jnp.pad(rel.reshape(1, -1), ((0, 0), (0, width - rel.size)))
    small = jnp.concatenate([gain_one_sum[:1], gain_two_sum[:1], rel_row], axis=0)
    returned = return_rows(
        line, place[:1].reshape(-1, 1), grad_packed, jnp.pad(small, ((0, 5), (0, 0))), capacity
    )
    came_back = lax.all_to_all(returned, "dp", split_axis=0, concat_axis=0, tiled=True)

    table_keep, table_give = layout_grad(
        line, own_side, across, across_other, own_columns, other_columns, data_count, layout_rows
    )
    table_got = swap(table_give, "stream", 2)
    square_keep, square_give = square_grads(
        line, own_core, normed_one, qkv_grads, visual, grad_packed, data_count
    )
    square_got = swap(square_give, "stream", 1)
    square_shape = (data_count, 2, 1, 2 * shard_rows, half_width)
    square_keep, square_give = fold(
        line, own_side, square_keep.reshape(square_shape), square_got.reshape(square_shape)
    )
    square_got = swap(square_give, "stream", 2)
    table_shape = (data_count // 2, 2, 1, table_rows, half_width)
    table_keep, table_give = fold(
        line, bit_index("dp", 1), table_keep.reshape(table_shape), table_got.reshape(table_shape)
    )
    table_got = swap(table_give, "dp", 1)

    def stream_group(value):
        across_sides = swap(value, "stream", 2)
        return (value, swap(value, "stream", 1), across_sides, swap(across_sides, "stream", 1))

    wide_meta = meta.astype(jnp.float32)
    slot_kind = wide_meta[:1]
    slot_index = (wide_meta[11:12] * 16.0 + wide_meta[12:13]).astype(jnp.int32)
    slot_text = (wide_meta[13:14] * 4.0 + wide_meta[14:15]).astype(jnp.int32)

    def slot_keys_of(kind, value):
        keys = jnp.where(slot_kind == kind, value, -1).reshape(data_count, capacity)
        return jnp.pad(keys, ((0, 0), (0, 16)), constant_values=-1)

    text_grad_rows = unpack_text(line, slot_keys_of(2.0, slot_text), came_back, text_index)
    rows_side = swap(text_grad_rows, "stream", 2)
    rows_core = swap(text_grad_rows, "stream", 1)
    square_shape = (data_count // 2, 2, 1, 2 * shard_rows, half_width)
    square_keep, square_give = fold(
        line, bit_index("dp", 1), square_keep.reshape(square_shape),
        square_got.reshape(square_shape),
    )
    square_got = swap(square_give, "dp", 1)
    forward_sum.step()
    rows_both = swap(rows_side, "stream", 1)
    table_shape = (data_count // 4, 2, table_rows, half_width)
    square_shape = (data_count // 4, 2, 2 * shard_rows, half_width)
    value, give = rows_fold(
        line, bit_index("dp", 2), table_keep.reshape(table_shape), table_got.reshape(table_shape),
        square_keep.reshape(square_shape), square_got.reshape(square_shape),
    )
    backward_sum = Sum(line, dp_bits[:-2], value, swap(give, "dp", 2))
    grad_patches = patch_grads(
        line, slot_keys_of(1.0, slot_index), came_back, matrices, patches.shape[0]
    )
    backward_sum.step()
    forward_sum.finish()
    forward_group = stream_group(forward_sum.value)
    text_grad_rows = (text_grad_rows, rows_side, rows_core, rows_both)
    grad_text = text_grads(line, text_grad_rows, text_table.shape[0])
    backward_sum.finish()
    small = [join_small(rows[texts + 16 :]) for rows in text_grad_rows]
    small = (small[0] + small[1]) + (small[2] + small[3])

    shard_down, shard_mix, shard_in = assemble_forward(
        line, stream.reshape(1), forward_group, down_shape[2], mix_rows,
        shard_rows,
    )
    shard_layout, shard_qkv, shard_project = assemble_backward(
        line, stream.reshape(1), stream_group(backward_sum.value), layout_rows, shard_rows
    )
    grad_gains = lax.dynamic_slice_in_dim(
        small[:2], lax.axis_index("dp") * gain_count, gain_count, axis=1
    )
    return (
        result,
        grad_patches,
        grad_text,
        shard_layout,
        shard_project,
        small[2, : rel.size].reshape(rel.shape),
        grad_gains,
        shard_qkv,
        shard_mix.reshape(shard_rows, width),
        shard_in,
        shard_down.reshape(-1, width),
    )


def solution(mesh):
    return jax.shard_map(
        shards,
        mesh=mesh,
        in_specs=(
            P(("dp", "stream"), None),
            P(("dp", "stream")),
            P(("dp", "stream")),
            P(None, ("dp", "stream")),
            P(("dp", "stream")),
            P(("dp", "stream"), None),
            P("dp", None),
            P(None, "dp", None),
            P("dp", None),
            P(),
            P(None, "dp"),
            P(None, "dp", None),
            P("dp", None),
            P("dp", None),
            P("dp", None),
            P(("dp", "stream"), None),
        ),
        out_specs=(
            P(("dp", "stream"), None),
            P(("dp", "stream"), None),
            P("dp", None),
            P(None, "dp", None),
            P("dp", None),
            P(),
            P(None, "dp"),
            P(None, "dp", None),
            P("dp", None),
            P("dp", None),
            P("dp", None),
        ),
        check_vma=False,
    )
```

profile of v0, /device:TPU:1, one launch (start us, length us, event | category | flops | bytes accessed | tf_op | source)
XLA Modules:
  0.0 598.9 jit_solution(9219698922858964448)
XLA Ops:
  19.8 5.6 collective-permute-done.1.refs_2_
  33.4 13.3 %collective-permute-done.refs_2_ = bf16[1,96,768]{2,1,0:T(8,128)(2,1)S(1)} collective-permute-done((bf16[1,96,768]{2,1,0:T(8,128)(2,1)S(1)}, bf16[1,96,768]{2,1,0:T(8,128)(2,1)S(1)}, u32[]{:S(2)}, u32[]{:S(2)}) %collective-permute-start) | collective-permute-done | bytes 147488 | tf_op jit(solution)/shard_map/ppermute | solution.py:1109
  61.4 5.9 gather_fusion
  67.4 7.1 %collective-permute-done.2.refs_2_ = bf16[2,96,768]{2,1,0:T(8,128)(2,1)S(1)} collective-permute-done((bf16[2,96,768]{2,1,0:T(8,128)(2,1)}, bf16[2,96,768]{2,1,0:T(8,128)(2,1)S(1)}, u32[]{:S(2)}, u32[]{:S(2)}) %collective-permute-start.2) | collective-permute-done | bytes 294944 | tf_op jit(solution)/shard_map/ppermute | solution.py:1109
  99.1 6.7 %pack.1 = (bf16[2048,768]{1,0:T(8,128)(2,1)}, bf16[96,768]{1,0:T(8,128)(2,1)}, f32[8,128]{1,0:T(8,128)}) custom-call(s32[2048,8]{1,0:T(8,128)} %get-tuple-element.149.refs_0_, bf16[512,768]{1,0:T(8,128)(2,1)} %refs_1_.1, bf16[512,768]{1,0:T(8,128)(2,1)} %broadcast_select_fusion.refs_2_, bf16[96,768]{1,0:T(8,128)(2,1)} %dynamic-slice_bitcast_fusion.refs_3_, ...), custom_call_target="tpu_custom_call" | custom-call | flops 1 | bytes 1 | tf_op jit(solution)/shard_map/pack/pallas_call | solution.py:35
  105.8 5.2 all-to-all-start.1
  116.0 21.1 %collective-permute-done.9.refs_3_ = bf16[768,768]{1,0:T(8,128)(2,1)} collective-permute-done((bf16[768,768]{1,0:T(8,128)(2,1)}, bf16[768,768]{1,0:T(8,128)(2,1)}, u32[]{:S(2)}, u32[]{:S(2)}) %collective-permute-start.9) | collective-permute-done | bytes 1179680 | tf_op jit(solution)/shard_map/ppermute | solution.py:1109
  137.1 7.1 %collective-permute-start.10 = (bf16[768,768]{1,0:T(8,128)(2,1)}, bf16[768,768]{1,0:T(8,128)(2,1)}, u32[]{:S(2)}, u32[]{:S(2)}) collective-permute-start(bf16[768,768]{1,0:T(8,128)(2,1)} %collective-permute-done.9.refs_3_), channel_id=1, source_target_pairs={{0,1},{1,0},{2,3},{3,2},{4,5},{5,4},{6,7},{7,6},{8,9},{9,8},{10,11... | collective-permute-start | bytes 3538952 | tf_op jit(solution)/shard_map/ppermute | solution.py:1109
  147.8 8.1 %layout_lookup.2 = (f32[1024,384]{1,0:T(8,128)}, f32[1024,384]{1,0:T(8,128)}, f32[8,128]{1,0:T(8,128)}) custom-call(s32[1]{0:T(128)} %bitcast.21.refs_0_, s32[1024,8]{1,0:T(8,128)} %get-tuple-element.148.refs_1_, s32[1024,8]{1,0:T(8,128)} %copy.46.refs_2_, bf16[8,256,384]{2,1,0:T(8,128)(2,1)} %bitcast.100, f32[8,128]{1,0:T(8,128)} %get-tuple-element.158.refs_4_), custom_call_target="tpu_custom_call" | custom-call | flops 1 | bytes 1 | tf_op jit(solution)/shard_map/layout_lookup/pallas_call | solution.py:35
  155.9 5.2 arrange.1
  161.1 13.9 %collective-permute-done.7.refs_3_ = bf16[8,256,384]{2,1,0:T(8,128)(2,1)} collective-permute-done((bf16[8,256,384]{2,1,0:T(8,128)(2,1)}, bf16[8,256,384]{2,1,0:T(8,128)(2,1)}, u32[]{:S(2)}, u32[]{:S(2)}) %collective-permute-start.7) | collective-permute-done | bytes 1572896 | tf_op jit(solution)/shard_map/ppermute | solution.py:1109
  175.0 8.6 %layout_lookup.3 = (f32[1024,384]{1,0:T(8,128)}, f32[1024,384]{1,0:T(8,128)}, f32[8,128]{1,0:T(8,128)}) custom-call(s32[1]{0:T(128)S(6)} %sub.42.refs_0_, s32[1024,8]{1,0:T(8,128)} %get-tuple-element.148.refs_1_, s32[1024,8]{1,0:T(8,128)} %copy.46.refs_2_, bf16[8,256,384]{2,1,0:T(8,128)(2,1)} %collective-permute-done.7.refs_3_, ...), custom_call_target="tpu_custom_call" | custom-call | flops 1 | bytes 1 | tf_op jit(solution)/shard_map/layout_lookup/pallas_call | solution.py:35
  192.4 17.0 %embed.1 = (bf16[768,1024]{1,0:T(8,128)(2,1)}, bf16[1024,768]{1,0:T(8,128)(2,1)}, bf16[768,1024]{1,0:T(8,128)(2,1)}, bf16[3,1024,768]{2,1,0:T(8,128)(2,1)}, f32[8,128]{1,0:T(8,128)}) custom-call(s32[8,2048]{1,0:T(8,128)} %get-tuple-element.147.refs_0_, s32[1024,8]{1,0:T(8,128)} %get-tuple-element.148.refs_1_, bf16[2048,768]{1,0:T(8,128)(2,1)} %bitcast.90, ...), custom_call_target="tpu_custom_call" | custom-call | flops 1 | bytes 1 | tf_op jit(solution)/shard_map/embed/pallas_call | solution.py:35
  216.3 28.7 %attention_forward.1 = (bf16[1024,768]{1,0:T(8,128)(2,1)}, f32[1024,768]{1,0:T(8,128)}, f32[8,128]{1,0:T(8,128)}) custom-call(bf16[3,1024,768]{2,1,0:T(8,128)(2,1)} %get-tuple-element.170.refs_0_.refs_1_.refs_2_, bf16[3,1024,768]{2,1,0:T(8,128)(2,1)} %get-tuple-element.170.refs_0_.refs_1_.refs_2_, ...), custom_call_target="tpu_custom_call" | custom-call | flops 1 | bytes 1 | tf_op jit(solution)/shard_map/attention_forward/pallas_call | solution.py:35
  245.8 34.8 %feed_forward.1 = (bf16[1024,768]{1,0:T(8,128)(2,1)}, bf16[3072,1024]{1,0:T(8,128)(2,1)}, bf16[1024,3072]{1,0:T(8,128)(2,1)}, bf16[768,1024]{1,0:T(8,128)(2,1)},...) custom-call(s32[1]{0:T(128)} %bitcast.refs_0_, ...), custom_call_target="tpu_custom_call" | custom-call | flops 1 | bytes 1 | tf_op jit(solution)/shard_map/feed_forward/pallas_call | solution.py:35
  280.6 9.1 %contract_halves.2 = (bf16[3072,384]{1,0:T(8,128)(2,1)}, bf16[3072,384]{1,0:T(8,128)(2,1)}, f32[8,128]{1,0:T(8,128)}) custom-call(s32[1]{0:T(128)} %bitcast.refs_0_, bf16[3072,1024]{1,0:T(8,128)(2,1)} %get-tuple-element.186.refs_1_, bf16[1024,768]{1,0:T(8,128)(2,1)} %refs_2_.1, f32[8,128]{1,0:T(8,128)} %get-tuple-element.187.refs_3_), custom_call_target="tpu_custom_call" | custom-call | flops 1 | bytes 1 | tf_op jit(solution)/shard_map/contract_halves/pallas_call | solution.py:35
  294.0 9.8 %contract_quarters.1 = (bf16[2,8,2,96,384]{4,3,2,1,0:T(8,128)(2,1)}, bf16[2,8,2,96,384]{4,3,2,1,0:T(8,128)(2,1)}, f32[8,128]{1,0:T(8,128)}) custom-call(s32[1]{0:T(128)} %bitcast.refs_0_, bf16[768,1024]{1,0:T(8,128)(2,1)} %get-tuple-element.182.refs_1_, bf16[1024,3072]{1,0:T(8,128)(2,1)} %get-tuple-element.183.refs_2_, f32[8,128]{1,0:T(8,128)} %get-tuple-element.189.refs_3_), custom_call_target="tpu_custom_call" | custom-call | flops 1 | bytes 1 | tf_op jit(solution)/shard_map/contract_quarters/pallas_call | solution.py:35
  310.8 5.4 rows_fold.3
  319.4 4.9 fold.8
  326.3 36.6 %attention_backward.1 = (bf16[3,1024,768]{2,1,0:T(8,128)(2,1)}, f32[12,8,512]{2,1,0:T(8,128)}, f32[8,128]{1,0:T(8,128)}) custom-call(bf16[3,1024,768]{2,1,0:T(8,128)(2,1)} %get-tuple-element.170.refs_0_.refs_1_.refs_2_, bf16[3,1024,768]{2,1,0:T(8,128)(2,1)} %get-tuple-element.170.refs_0_.refs_1_.refs_2_, ...), custom_call_target="tpu_custom_call" | custom-call | flops 1 | bytes 1 | tf_op jit(solution)/shard_map/attention_backward/pallas_call | solution.py:35
  375.5 9.9 %input_grad.1 = (bf16[1024,768]{1,0:T(8,128)(2,1)}, bf16[1024,384]{1,0:T(8,128)(2,1)}, bf16[1024,384]{1,0:T(8,128)(2,1)}, f32[8,768]{1,0:T(8,128)}, f32[8,128]{1,0:T(8,128)}) custom-call(s32[1]{0:T(128)} %bitcast.refs_0_, bf16[1024,768]{1,0:T(8,128)(2,1)} %get-tuple-element.169.refs_1_, f32[1024,768]{1,0:T(8,128)} %get-tuple-element.179.refs_2_, ...), custom_call_target="tpu_custom_call" | custom-call | flops 1 | bytes 1 | tf_op jit(solution)/shard_map/input_grad/pallas_call | solution.py:35
  393.5 8.8 %return_rows.1 = (bf16[8,272,768]{2,1,0:T(8,128)(2,1)}, f32[8,128]{1,0:T(8,128)}) custom-call(s32[2048,1]{1,0:T(8,128)} %copy.50.refs_0_, bf16[1024,768]{1,0:T(8,128)(2,1)} %get-tuple-element.207.refs_1_.refs_4_, f32[8,768]{1,0:T(8,128)} %pad.27.refs_2_, f32[8,128]{1,0:T(8,128)} %get-tuple-element.216.refs_3_), custom_call_target="tpu_custom_call" | custom-call | flops 1 | bytes 1 | tf_op jit(solution)/shard_map/return_rows/pallas_call | solution.py:35
  411.2 13.0 %layout_grad.1 = (bf16[8,2,128,384]{3,2,1,0:T(8,128)(2,1)}, bf16[8,2,128,384]{3,2,1,0:T(8,128)(2,1)}, f32[8,128]{1,0:T(8,128)}) custom-call(s32[1]{0:T(128)} %bitcast.21.refs_0_, s32[8,1024]{1,0:T(8,128)} %get-tuple-element.218.refs_1_, s32[8,1024]{1,0:T(8,128)} %bitcast.144, bf16[1024,384]{1,0:T(8,128)(2,1)} %get-tuple-element.219.refs_3_, ...), custom_call_target="tpu_custom_call" | custom-call | flops 1 | bytes 1 | tf_op jit(solution)/shard_map/layout_grad/pallas_call | solution.py:35
  424.2 10.1 %square_grads.1 = (bf16[8,2,2,96,384]{4,3,2,1,0:T(8,128)(2,1)}, bf16[8,2,2,96,384]{4,3,2,1,0:T(8,128)(2,1)}, f32[8,128]{1,0:T(8,128)}) custom-call(s32[1]{0:T(128)} %bitcast.refs_0_, bf16[768,1024]{1,0:T(8,128)(2,1)} %get-tuple-element.224.refs_1_, bf16[3,1024,768]{2,1,0:T(8,128)(2,1)} %get-tuple-element.199.refs_3_.refs_2_, ...), custom_call_target="tpu_custom_call" | custom-call | flops 1 | bytes 1 | tf_op jit(solution)/shard_map/square_grads/pallas_call | solution.py:35
  440.5 4.9 fold.11
  446.8 23.9 %collective-permute-done.22 = bf16[8,2,128,384]{3,2,1,0:T(8,128)(2,1)S(1)} collective-permute-done((bf16[8,2,128,384]{3,2,1,0:T(8,128)(2,1)}, bf16[8,2,128,384]{3,2,1,0:T(8,128)(2,1)S(1)}, u32[]{:S(2)}, u32[]{:S(2)}) %collective-permute-start.22) | collective-permute-done | bytes 1572896 | tf_op jit(solution)/shard_map/ppermute | solution.py:1109
  481.0 6.2 %unpack_text.1 = (bf16[544,768]{1,0:T(8,128)(2,1)}, f32[8,128]{1,0:T(8,128)}) custom-call(s32[8,272]{1,0:T(8,128)} %pad.28.refs_0_, bf16[8,272,768]{2,1,0:T(8,128)(2,1)} %copy-done.2, s32[8,512]{1,0:T(8,128)} %get-tuple-element.150.refs_2_, f32[8,128]{1,0:T(8,128)} %get-tuple-element.235.refs_3_), custom_call_target="tpu_custom_call" | custom-call | flops 1 | bytes 1 | tf_op jit(solution)/shard_map/unpack_text/pallas_call | solution.py:35
  487.2 8.9 %collective-permute-done.25 = bf16[8,1,192,384]{3,2,1,0:T(8,128)(2,1)} collective-permute-done((bf16[8,1,192,384]{3,2,1,0:T(8,128)(2,1)}, bf16[8,1,192,384]{3,2,1,0:T(8,128)(2,1)}, u32[]{:S(2)}, u32[]{:S(2)}) %collective-permute-start.25) | collective-permute-done | bytes 1179680 | tf_op jit(solution)/shard_map/ppermute | solution.py:1109
  504.4 9.2 %collective-permute-done.26 = bf16[4,1,192,384]{3,2,1,0:T(8,128)(2,1)S(1)} collective-permute-done((bf16[4,1,192,384]{3,2,1,0:T(8,128)(2,1)}, bf16[4,1,192,384]{3,2,1,0:T(8,128)(2,1)S(1)}, u32[]{:S(2)}, u32[]{:S(2)}) %collective-permute-start.26) | collective-permute-done | bytes 589856 | tf_op jit(solution)/shard_map/ppermute | solution.py:1109
  524.7 8.4 %patch_grads.1 = (f32[512,768]{1,0:T(8,128)}, f32[8,128]{1,0:T(8,128)}) custom-call(s32[8,272]{1,0:T(8,128)} %pad.25.refs_0_, bf16[8,272,768]{2,1,0:T(8,128)(2,1)} %copy-done.2, bf16[4,768,768]{2,1,0:T(8,128)(2,1)} %get-tuple-element.166.refs_6_.refs_8_.refs_4_.refs_2_, f32[8,128]{1,0:T(8,128)} %get-tuple-element.243.refs_3_), custom_call_target="tpu_custom_call" | custom-call | flops 1 | bytes 1 | tf_op jit(solution)/shard_map/patch_grads/pallas_call | solution.py:35
  533.1 8.2 %collective-permute-done.32 = bf16[2,448,384]{2,1,0:T(8,128)(2,1)} collective-permute-done((bf16[2,448,384]{2,1,0:T(8,128)(2,1)}, bf16[2,448,384]{2,1,0:T(8,128)(2,1)}, u32[]{:S(2)}, u32[]{:S(2)}) %collective-permute-start.32) | collective-permute-done | bytes 688160 | tf_op jit(solution)/shard_map/ppermute | solution.py:1109
  549.2 17.7 %text_grads.1 = (f32[4016,768]{1,0:T(8,128)}, f32[8,128]{1,0:T(8,128)}) custom-call(bf16[544,768]{1,0:T(8,128)(2,1)} %get-tuple-element.245.refs_0_, bf16[544,768]{1,0:T(8,128)(2,1)} %copy-done.13, bf16[544,768]{1,0:T(8,128)(2,1)} %copy-done.15, bf16[544,768]{1,0:T(8,128)(2,1)} %copy-done.14, f32[8,128]{1,0:T(8,128)} %get-tuple-element.252.refs_4_), custom_call_target="tpu_custom_call" | custom-call | flops 1 | bytes 1 | tf_op jit(solution)/shard_map/text_grads/pallas_call | solution.py:35
  (260 shorter events, 200.1 us)
Async XLA Ops:
  7.2 237.8 %all-gather.6.cloned.1.call-start = ((), (), s32[]{:S(2)}) async-start(), calls=%async_computation.4 | async-start | bytes 4866048 | tf_op jit(solution)/shard_map/all_gather | solution.py:1229
  27.9 21.2 %collective-permute-start.3 = (bf16[2,320,384]{2,1,0:T(8,128)(2,1)}, bf16[2,320,384]{2,1,0:T(8,128)(2,1)S(1)}, u32[]{:S(2)}, u32[]{:S(2)}) collective-permute-start(bf16[2,320,384]{2,1,0:T(8,128)(2,1)} %bitcast.131), channel_id=1, source_target_pairs={{0,8},{4,12},{8,0},{12,4},{16,24},{20,28},{24,16},{28,20},{1,9},{5... | collective-permute-start | bytes 1474568 | tf_op jit(solution)/shard_map/ppermute | solution.py:1109
  30.3 16.5 %collective-permute-start = (bf16[1,96,768]{2,1,0:T(8,128)(2,1)S(1)}, bf16[1,96,768]{2,1,0:T(8,128)(2,1)S(1)}, u32[]{:S(2)}, u32[]{:S(2)}) collective-permute-start(bf16[1,96,768]{2,1,0:T(8,128)(2,1)S(1)} %fusion.5.refs_1_), channel_id=1, source_target_pairs={{0,16},{4,20},{8,24},{12,28},{16,0},{20,4},{24,8},{28,12},{1,17},{... | collective-permute-start | bytes 442376 | tf_op jit(solution)/shard_map/ppermute | solution.py:1109
  52.1 36.0 %collective-permute-start.5 = (bf16[4,320,384]{2,1,0:T(8,128)(2,1)}, bf16[4,320,384]{2,1,0:T(8,128)(2,1)S(1)}, u32[]{:S(2)}, u32[]{:S(2)}) collective-permute-start(bf16[4,320,384]{2,1,0:T(8,128)(2,1)} %bitcast.113), channel_id=1, source_target_pairs={{0,4},{4,0},{8,12},{12,8},{16,20},{20,16},{24,28},{28,24},{1,5},{5... | collective-permute-start | bytes 2949128 | tf_op jit(solution)/shard_map/ppermute | solution.py:1109
  53.9 29.4 %all-to-all-start = ((bf16[16,8,256]{2,0,1:T(8,128)(2,1)}), bf16[16,8,256]{2,0,1:T(8,128)(2,1)S(1)}, u32[]{:S(2)}, u32[]{:S(2)}) async-start(bf16[16,8,256]{2,0,1:T(8,128)(2,1)} %bitcast.88), calls=%async_computation | async-start | bytes 131072 | tf_op jit(solution)/shard_map/all_to_all | solution.py:1235
  58.4 186.7 %all-gather.4.cloned.1.call-start = ((), (), s32[]{:S(2)}) async-start(), calls=%async_computation.3 | async-start | bytes 4866048 | tf_op jit(solution)/shard_map/all_gather | solution.py:1257
  59.2 15.4 %collective-permute-start.2 = (bf16[2,96,768]{2,1,0:T(8,128)(2,1)}, bf16[2,96,768]{2,1,0:T(8,128)(2,1)S(1)}, u32[]{:S(2)}, u32[]{:S(2)}) collective-permute-start(bf16[2,96,768]{2,1,0:T(8,128)(2,1)} %bitcast.138), channel_id=1, source_target_pairs={{0,8},{4,12},{8,0},{12,4},{16,24},{20,28},{24,16},{28,20},{1,9},{5... | collective-permute-start | bytes 884744 | tf_op jit(solution)/shard_map/ppermute | solution.py:1109
  77.1 18.8 %collective-permute-start.4 = (bf16[4,96,768]{2,1,0:T(8,128)(2,1)}, bf16[4,96,768]{2,1,0:T(8,128)(2,1)S(1)}, u32[]{:S(2)}, u32[]{:S(2)}) collective-permute-start(bf16[4,96,768]{2,1,0:T(8,128)(2,1)} %bitcast.123), channel_id=1, source_target_pairs={{0,4},{4,0},{8,12},{12,8},{16,20},{20,16},{24,28},{28,24},{1,5},{5... | collective-permute-start | bytes 1769480 | tf_op jit(solution)/shard_map/ppermute | solution.py:1109
  105.8 84.9 %all-to-all-start.1 = ((bf16[8,256,768]{2,1,0:T(8,128)(2,1)}), bf16[8,256,768]{2,1,0:T(8,128)(2,1)S(1)}, u32[]{:S(2)}, u32[]{:S(2)}) async-start(bf16[8,256,768]{2,1,0:T(8,128)(2,1)} %bitcast.92), calls=%async_computation.1 | async-start | bytes 6291456 | tf_op jit(solution)/shard_map/all_to_all | solution.py:1254
  111.0 26.1 %collective-permute-start.9 = (bf16[768,768]{1,0:T(8,128)(2,1)}, bf16[768,768]{1,0:T(8,128)(2,1)}, u32[]{:S(2)}, u32[]{:S(2)}) collective-permute-start(bf16[768,768]{1,0:T(8,128)(2,1)} %bitcast.108), channel_id=1, source_target_pairs={{0,2},{1,3},{2,0},{3,1},{4,6},{5,7},{6,4},{7,5},{8,10},{9,11},{10,... | collective-permute-start | bytes 3538952 | tf_op jit(solution)/shard_map/ppermute | solution.py:1109
  112.4 62.6 %collective-permute-start.7 = (bf16[8,256,384]{2,1,0:T(8,128)(2,1)}, bf16[8,256,384]{2,1,0:T(8,128)(2,1)}, u32[]{:S(2)}, u32[]{:S(2)}) collective-permute-start(bf16[8,256,384]{2,1,0:T(8,128)(2,1)} %bitcast.99), channel_id=1, source_target_pairs={{0,2},{1,3},{2,0},{3,1},{4,6},{5,7},{6,4},{7,5},{8,10},{9,11},{10,... | collective-permute-start | bytes 4718600 | tf_op jit(solution)/shard_map/ppermute | solution.py:1109
  112.6 43.3 %collective-permute-start.8 = (bf16[768,768]{1,0:T(8,128)(2,1)}, bf16[768,768]{1,0:T(8,128)(2,1)}, u32[]{:S(2)}, u32[]{:S(2)}) collective-permute-start(bf16[768,768]{1,0:T(8,128)(2,1)} %bitcast.109), channel_id=1, source_target_pairs={{0,1},{1,0},{2,3},{3,2},{4,5},{5,4},{6,7},{7,6},{8,9},{9,8},{10,11... | collective-permute-start | bytes 3538952 | tf_op jit(solution)/shard_map/ppermute | solution.py:1109
  137.1 18.8 %collective-permute-start.10 = (bf16[768,768]{1,0:T(8,128)(2,1)}, bf16[768,768]{1,0:T(8,128)(2,1)}, u32[]{:S(2)}, u32[]{:S(2)}) collective-permute-start(bf16[768,768]{1,0:T(8,128)(2,1)} %collective-permute-done.9.refs_3_), channel_id=1, source_target_pairs={{0,1},{1,0},{2,3},{3,2},{4,5},{5,4},{6,7},{7,6},{8,9},{9,8},{10,11... | collective-permute-start | bytes 3538952 | tf_op jit(solution)/shard_map/ppermute | solution.py:1109
  187.3 22.1 %collective-permute-start.12 = (bf16[8,48,384]{2,1,0:T(8,128)(2,1)S(1)}, bf16[8,48,384]{2,1,0:T(8,128)(2,1)}, u32[]{:S(2)}, u32[]{:S(2)}) collective-permute-start(bf16[8,48,384]{2,1,0:T(8,128)(2,1)S(1)} %bitcast.137), channel_id=1, source_target_pairs={{0,2},{1,3},{2,0},{3,1},{4,6},{5,7},{6,4},{7,5},{8,10},{9,11},{10,... | collective-permute-start | bytes 884744 | tf_op jit(solution)/shard_map/ppermute | solution.py:1109
  211.3 33.6 %collective-permute-start.13 = (bf16[768,384]{1,0:T(8,128)(2,1)}, bf16[768,384]{1,0:T(8,128)(2,1)S(1)}, u32[]{:S(2)}, u32[]{:S(2)}) collective-permute-start(bf16[768,384]{1,0:T(8,128)(2,1)} %bitcast.121), channel_id=1, source_target_pairs={{0,1},{1,0},{2,3},{3,2},{4,5},{5,4},{6,7},{7,6},{8,9},{9,8},{10,11... | collective-permute-start | bytes 1769480 | tf_op jit(solution)/shard_map/ppermute | solution.py:1109
  289.7 19.5 %collective-permute-start.15 = (bf16[3072,384]{1,0:T(8,128)(2,1)}, bf16[3072,384]{1,0:T(8,128)(2,1)S(1)}, u32[]{:S(2)}, u32[]{:S(2)}) collective-permute-start(bf16[3072,384]{1,0:T(8,128)(2,1)} %get-tuple-element.193), channel_id=1, source_target_pairs={{0,1},{1,0},{2,3},{3,2},{4,5},{5,4},{6,7},{7,6},{8,9},{9,8},{10,11... | collective-permute-start | bytes 7077896 | tf_op jit(solution)/shard_map/ppermute | solution.py:1109
  316.2 46.7 %collective-permute-start.18 = (bf16[8,240,384]{2,1,0:T(8,128)(2,1)}, bf16[8,240,384]{2,1,0:T(8,128)(2,1)S(1)}, u32[]{:S(2)}, u32[]{:S(2)}) collective-permute-start(bf16[8,240,384]{2,1,0:T(8,128)(2,1)} %get-tuple-element.203), channel_id=1, source_target_pairs={{0,2},{1,3},{2,0},{3,1},{4,6},{5,7},{6,4},{7,5},{8,10},{9,11},{10,... | collective-permute-start | bytes 4423688 | tf_op jit(solution)/shard_map/ppermute | solution.py:1109
  324.4 42.9 %collective-permute-start.17 = (bf16[8,1,192,384]{3,2,1,0:T(8,128)(2,1)}, bf16[8,1,192,384]{3,2,1,0:T(8,128)(2,1)S(1)}, u32[]{:S(2)}, u32[]{:S(2)}) collective-permute-start(bf16[8,1,192,384]{3,2,1,0:T(8,128)(2,1)} %get-tuple-element.201), channel_id=1, source_target_pairs={{0,4},{4,0},{8,12},{12,8},{16,20},{20,16},{24,28},{28,24},{1,5},{5... | collective-permute-start | bytes 3538952 | tf_op jit(solution)/shard_map/ppermute | solution.py:1109
  371.2 15.6 %collective-permute-start.20 = (bf16[1,4,192,384]{3,2,1,0:T(8,128)(2,1)}, bf16[1,4,192,384]{3,2,1,0:T(8,128)(2,1)S(1)}, u32[]{:S(2)}, u32[]{:S(2)}) collective-permute-start(bf16[1,4,192,384]{3,2,1,0:T(8,128)(2,1)} %get-tuple-element.214), channel_id=1, source_target_pairs={{0,2},{1,3},{2,0},{3,1},{4,6},{5,7},{6,4},{7,5},{8,10},{9,11},{10,... | collective-permute-start | bytes 1769480 | tf_op jit(solution)/shard_map/ppermute | solution.py:1109
  371.3 17.2 %collective-permute-start.19 = (bf16[4,1,240,384]{3,2,1,0:T(8,128)(2,1)}, bf16[4,1,240,384]{3,2,1,0:T(8,128)(2,1)S(1)}, u32[]{:S(2)}, u32[]{:S(2)}) collective-permute-start(bf16[4,1,240,384]{3,2,1,0:T(8,128)(2,1)} %get-tuple-element.212), channel_id=1, source_target_pairs={{0,4},{4,0},{8,12},{12,8},{16,20},{20,16},{24,28},{28,24},{1,5},{5... | collective-permute-start | bytes 2211848 | tf_op jit(solution)/shard_map/ppermute | solution.py:1109
  402.3 76.9 %all-to-all-start.2 = ((bf16[8,272,768]{2,1,0:T(8,128)(2,1)}), bf16[8,272,768]{2,1,0:T(8,128)(2,1)S(1)}, u32[]{:S(2)}, u32[]{:S(2)}) async-start(bf16[8,272,768]{2,1,0:T(8,128)(2,1)} %get-tuple-element.217), calls=%async_computation.2 | async-start | bytes 6684672 | tf_op jit(solution)/shard_map/all_to_all | solution.py:1333
  434.7 36.1 %collective-permute-start.22 = (bf16[8,2,128,384]{3,2,1,0:T(8,128)(2,1)}, bf16[8,2,128,384]{3,2,1,0:T(8,128)(2,1)S(1)}, u32[]{:S(2)}, u32[]{:S(2)}) collective-permute-start(bf16[8,2,128,384]{3,2,1,0:T(8,128)(2,1)} %get-tuple-element.223), channel_id=1, source_target_pairs={{0,2},{1,3},{2,0},{3,1},{4,6},{5,7},{6,4},{7,5},{8,10},{9,11},{10,... | collective-permute-start | bytes 4718600 | tf_op jit(solution)/shard_map/ppermute | solution.py:1109
  445.4 50.7 %collective-permute-start.25 = (bf16[8,1,192,384]{3,2,1,0:T(8,128)(2,1)}, bf16[8,1,192,384]{3,2,1,0:T(8,128)(2,1)}, u32[]{:S(2)}, u32[]{:S(2)}) collective-permute-start(bf16[8,1,192,384]{3,2,1,0:T(8,128)(2,1)} %get-tuple-element.234), channel_id=1, source_target_pairs={{0,2},{1,3},{2,0},{3,1},{4,6},{5,7},{6,4},{7,5},{8,10},{9,11},{10,... | collective-permute-start | bytes 3538952 | tf_op jit(solution)/shard_map/ppermute | solution.py:1109
  475.2 29.1 %collective-permute-start.24 = (bf16[4,1,256,384]{3,2,1,0:T(8,128)(2,1)}, bf16[4,1,256,384]{3,2,1,0:T(8,128)(2,1)}, u32[]{:S(2)}, u32[]{:S(2)}) collective-permute-start(bf16[4,1,256,384]{3,2,1,0:T(8,128)(2,1)} %get-tuple-element.232), channel_id=1, source_target_pairs={{0,4},{4,0},{8,12},{12,8},{16,20},{20,16},{24,28},{28,24},{1,5},{5... | collective-permute-start | bytes 2359304 | tf_op jit(solution)/shard_map/ppermute | solution.py:1109
  477.0 25.1 %collective-permute-start.27 = (bf16[2,432,384]{2,1,0:T(8,128)(2,1)}, bf16[2,432,384]{2,1,0:T(8,128)(2,1)}, u32[]{:S(2)}, u32[]{:S(2)}) collective-permute-start(bf16[2,432,384]{2,1,0:T(8,128)(2,1)} %get-tuple-element.240), channel_id=1, source_target_pairs={{0,8},{4,12},{8,0},{12,4},{16,24},{20,28},{24,16},{28,20},{1,9},{5... | collective-permute-start | bytes 1990664 | tf_op jit(solution)/shard_map/ppermute | solution.py:1109
  500.7 21.3 %collective-permute-start.28 = (bf16[544,768]{1,0:T(8,128)(2,1)S(1)}, bf16[544,768]{1,0:T(8,128)(2,1)S(1)}, u32[]{:S(2)}, u32[]{:S(2)}) collective-permute-start(bf16[544,768]{1,0:T(8,128)(2,1)S(1)} %copy-done.12), channel_id=1, source_target_pairs={{0,2},{1,3},{2,0},{3,1},{4,6},{5,7},{6,4},{7,5},{8,10},{9,11},{10,... | collective-permute-start | bytes 2506760 | tf_op jit(solution)/shard_map/ppermute | solution.py:1109
  518.6 22.8 %collective-permute-start.32 = (bf16[2,448,384]{2,1,0:T(8,128)(2,1)}, bf16[2,448,384]{2,1,0:T(8,128)(2,1)}, u32[]{:S(2)}, u32[]{:S(2)}) collective-permute-start(bf16[2,448,384]{2,1,0:T(8,128)(2,1)} %get-tuple-element.249), channel_id=1, source_target_pairs={{0,8},{4,12},{8,0},{12,4},{16,24},{20,28},{24,16},{28,20},{1,9},{5... | collective-permute-start | bytes 2064392 | tf_op jit(solution)/shard_map/ppermute | solution.py:1109
  519.8 28.3 %collective-permute-start.29 = (bf16[544,768]{1,0:T(8,128)(2,1)S(1)}, bf16[544,768]{1,0:T(8,128)(2,1)S(1)}, u32[]{:S(2)}, u32[]{:S(2)}) collective-permute-start(bf16[544,768]{1,0:T(8,128)(2,1)S(1)} %copy-done.12), channel_id=1, source_target_pairs={{0,1},{1,0},{2,3},{3,2},{4,5},{5,4},{6,7},{7,6},{8,9},{9,8},{10,11... | collective-permute-start | bytes 2506760 | tf_op jit(solution)/shard_map/ppermute | solution.py:1109
  522.0 26.1 %collective-permute-start.30 = (bf16[544,768]{1,0:T(8,128)(2,1)S(1)}, bf16[544,768]{1,0:T(8,128)(2,1)S(1)}, u32[]{:S(2)}, u32[]{:S(2)}) collective-permute-start(bf16[544,768]{1,0:T(8,128)(2,1)S(1)} %collective-permute-done.28.refs_1_), channel_id=1, source_target_pairs={{0,1},{1,0},{2,3},{3,2},{4,5},{5,4},{6,7},{7,6},{8,9},{9,8},{10,11... | collective-permute-start | bytes 2506760 | tf_op jit(solution)/shard_map/ppermute | solution.py:1109
  522.0 22.8 %collective-permute-start.31 = (bf16[1,1,432,384]{3,2,1,0:T(8,128)(2,1)}, bf16[1,1,432,384]{3,2,1,0:T(8,128)(2,1)}, u32[]{:S(2)}, u32[]{:S(2)}) collective-permute-start(bf16[1,1,432,384]{3,2,1,0:T(8,128)(2,1)} %get-tuple-element.247), channel_id=1, source_target_pairs={{0,16},{4,20},{8,24},{12,28},{16,0},{20,4},{24,8},{28,12},{1,17},{... | collective-permute-start | bytes 995336 | tf_op jit(solution)/shard_map/ppermute | solution.py:1109
  543.9 23.1 %collective-permute-start.33 = (bf16[1,1,448,384]{3,2,1,0:T(8,128)(2,1)}, bf16[1,1,448,384]{3,2,1,0:T(8,128)(2,1)S(1)}, u32[]{:S(2)}, u32[]{:S(2)}) collective-permute-start(bf16[1,1,448,384]{3,2,1,0:T(8,128)(2,1)} %get-tuple-element.255), channel_id=1, source_target_pairs={{0,16},{4,20},{8,24},{12,28},{16,0},{20,4},{24,8},{28,12},{1,17},{... | collective-permute-start | bytes 1032200 | tf_op jit(solution)/shard_map/ppermute | solution.py:1109
  546.7 27.4 %collective-permute-start.38 = (bf16[432,384]{1,0:T(8,128)(2,1)}, bf16[432,384]{1,0:T(8,128)(2,1)}, u32[]{:S(2)}, u32[]{:S(2)}) collective-permute-start(bf16[432,384]{1,0:T(8,128)(2,1)} %get-tuple-element.258.refs_1_), channel_id=1, source_target_pairs={{0,2},{1,3},{2,0},{3,1},{4,6},{5,7},{6,4},{7,5},{8,10},{9,11},{10,... | collective-permute-start | bytes 995336 | tf_op jit(solution)/shard_map/ppermute | solution.py:1109
  (57 other events, 394.4 us)
Sparse Core Ops, SparseCore 0:
  11.0 78.9 all-gather.5
  105.9 110.0 all-gather.3
where the time goes:
time: 609 us; the launch traced here: 599 us
  Pallas kernels  319 us (52%)
  waiting for transfers between devices  132 us (22%)
  starting transfers between devices  76.9 us (13%)
  local copies, waits for them, and re-layouts  49.5 us (8%)
  between operations  15 us (2%)
    pallas_call x42, Pallas kernels, launch(): pl.pallas_call(body, out_shape=tuple(out_shape) + (jax.ShapeDtypeStruct((...  319 us
    ppermute x40, waiting for transfers between devices, swap(): return lax.ppermute(value, axis, [(i, i ^ bit) for i in range(count)])  129 us
    ppermute x40, starting transfers between devices, swap(): return lax.ppermute(value, axis, [(i, i ^ bit) for i in range(count)])  63.2 us
    unnamed x95, local copies, waits for them, and re-layouts  23.6 us
  transfers between devices with their start and end apart: 45, of which 19 were waited for; matrix products, arithmetic and copies ran while one was open for 5% of the time, Pallas kernels for 43%

commit v1 on v0

--- a/solution.py
+++ b/solution.py
@@ -22,14 +22,16 @@
         self.last = jnp.zeros((8, 128), jnp.float32)
 
 
-def launch(line, kernel, operands, in_specs, out_shape, out_specs, grid, name, scalars=(), scratch=()):
+def launch(
+    line, kernel, operands, in_specs, out_shape, out_specs, grid, name, scalars=(), scratch=(), waits=()
+):
     held, given, made = len(scalars), len(operands), len(out_shape)
     token = pl.BlockSpec((8, 128), lambda *_: (0, 0))
 
     def body(*refs):
-        outs = held + given + 1
-        refs[outs + made][...] = refs[outs - 1][...]
-        kernel(*refs[: outs - 1], *refs[outs : outs + made], *refs[outs + made + 1 :])
+        outs = held + given + 1 + len(waits)
+        refs[outs + made][...] = refs[held + given][...]
+        kernel(*refs[: held + given], *refs[outs : outs + made], *refs[outs + made + 1 :])
 
     out_shape = [jax.ShapeDtypeStruct(value.shape, value.dtype) for value in out_shape]
     results = pl.pallas_call(
@@ -38,14 +40,14 @@
         grid_spec=pltpu.PrefetchScalarGridSpec(
             num_scalar_prefetch=held,
             grid=grid,
-            in_specs=list(in_specs) + [token],
+            in_specs=list(in_specs) + [token] + [pl.BlockSpec(memory_space=pl.ANY)] * len(waits),
             out_specs=tuple(out_specs) + (token,),
             scratch_shapes=list(scratch),
         ),
         compiler_params=pltpu.CompilerParams(vmem_limit_bytes=VMEM_LIMIT),
         cost_estimate=SMALL,
         name=name,
-    )(*scalars, *operands, line.last)
+    )(*scalars, *operands, line.last, *waits)
     line.last = results[-1]
     return results[:-1]
 
@@ -575,20 +577,26 @@
 
 
 def return_kernel(place_ref, rows_ref, small_ref, out_ref):
-    capacity = place_ref.shape[0]
-    pick = as_bf16(iota((capacity, rows_ref.shape[0]), 1) == place_ref[...])
-    out_ref[:capacity, :] = dot_nn(pick, rows_ref[...]).astype(jnp.bfloat16)
-    out_ref[capacity:, :] = split_small(small_ref[0:3, :])
+    slots = place_ref.shape[0]
+    devices, capacity = out_ref.shape[0], out_ref.shape[1] - 16
+    pick = as_bf16(iota((slots, rows_ref.shape[0]), 1) == place_ref[...])
+    rows = dot_nn(pick, rows_ref[...]).astype(jnp.bfloat16)
+    small = split_small(small_ref[0:3, :])
+    for d in range(devices):
+        out_ref[d, :capacity, :] = rows[d * capacity : d * capacity + capacity]
+        out_ref[d, capacity:, :] = small
 
 
 def return_rows(line, places, rows, small, capacity):
     count = places.shape[0] // capacity
     width = rows.shape[1]
+    step = max(1, min(count, 512 // capacity))
     return launch(
         line, return_kernel, (places, rows, small),
-        [pl.BlockSpec((capacity, 1), lambda i: (i, 0)), fixed(rows), fixed(small)],
+        [pl.BlockSpec((step * capacity, 1), lambda i: (i, 0)), fixed(rows), fixed(small)],
         (bf16(count, capacity + 16, width),),
-        (pl.BlockSpec((None, capacity + 16, width), lambda i: (i, 0, 0)),), (count,), "return_rows",
+        (pl.BlockSpec((step, capacity + 16, width), lambda i: (i, 0, 0)),), (count // step,),
+        "return_rows",
     )[0]
 
 
@@ -867,7 +875,7 @@
 def fold(line, bit, value, got):
     a, _, b, rows, width = value.shape
     step = a
-    while step > 1 and step * b * rows * width * value.dtype.itemsize > 800_000:
+    while step > 1 and step * b * rows * width * value.dtype.itemsize > 1_600_000:
         step //= 2
     count = a // step
     source = pl.BlockSpec(
@@ -949,7 +957,7 @@
         out_ref[...] = got_ref[...]
 
 
-def stack(line, bit, value, got):
+def stack(line, bit, value, got, waits=()):
     a, rows, width = value.shape
     return launch(
         line, stack_kernel, (value, got), [fixed(value), fixed(got)],
@@ -959,7 +967,7 @@
                 (a, None, rows, width), lambda n, s: (0, jnp.where(n == 0, s[0], 1 - s[0]), 0, 0)
             ),
         ),
-        (2,), "stack", scalars=(bit,),
+        (2,), "stack", scalars=(bit,), waits=waits,
     )[0]
 
 
@@ -1020,87 +1028,64 @@
 
 
 def assemble_forward_kernel(me, *refs):
-    del me
     down_ref, mix_ref, in_ref = refs[4:]
+    half = refs[0].shape[1]
     for n in range(4):
-
-        @pl.when(pl.program_id(0) == n)
-        def _():
-            start = 0
-            for out_ref in (down_ref, mix_ref):
-                rows = out_ref.shape[0]
-                out_ref[...] = refs[n][start : start + rows, :].astype(jnp.float32)
-                start += rows
-            rows = in_ref.shape[0]
-            first = refs[n][start : start + rows, :]
-            second = refs[n][start + rows : start + 2 * rows, :]
-            in_ref[...] = jnp.concatenate([first, second], axis=1).astype(jnp.float32)
+        device = jnp.bitwise_xor(me[0], n)
+        side = jnp.right_shift(device, 1)
+        column = pl.ds(pl.multiple_of(jnp.bitwise_and(device, 1) * half, 128), half)
+        start = 0
+        for out_ref in (down_ref, mix_ref):
+            rows = out_ref.shape[1]
+            out_ref[side, :, column] = refs[n][start : start + rows, :].astype(jnp.float32)
+            start += rows
+        rows = in_ref.shape[0]
+        for h in range(2):
+            part = refs[n][start + h * rows : start + h * rows + rows, :].astype(jnp.float32)
+            in_ref[:, pl.ds(pl.multiple_of((2 * device + h) * half, 128), half)] = part
 
 
 def assemble_forward(line, me, values, down_rows, mix_rows, shard_rows):
     half = values[0].shape[1]
-
-    def part(rows):
-        return pl.BlockSpec(
-            (None, rows, half),
-            lambda n, s: (jnp.bitwise_xor(n, s[0]) // 2, 0, jnp.bitwise_xor(n, s[0]) % 2),
-        )
-
+    shapes = (f32(2, down_rows, 2 * half), f32(2, mix_rows, 2 * half), f32(shard_rows, 8 * half))
     return launch(
         line, assemble_forward_kernel, tuple(values), [fixed(value) for value in values],
-        (
-            f32(2, down_rows, 2 * half), f32(2, mix_rows, 2 * half), f32(shard_rows, 8 * half),
-        ),
-        (
-            part(down_rows), part(mix_rows),
-            pl.BlockSpec((shard_rows, 2 * half), lambda n, s: (0, jnp.bitwise_xor(n, s[0]))),
-        ),
-        (4,), "assemble_forward", scalars=(me,),
+        shapes, [fixed(value) for value in shapes], (1,), "assemble_forward", scalars=(me,),
     )
 
 
 def assemble_backward_kernel(me, *refs):
     layout_ref, qkv_ref, project_ref = refs[4:]
-    device, k = pl.program_id(0), pl.program_id(1)
-    layout_rows, rows = layout_ref.shape[0], project_ref.shape[0]
+    half = refs[0].shape[1]
+    layout_rows, rows = layout_ref.shape[1], project_ref.shape[0]
     for n in range(4):
-
-        @pl.when(device == jnp.bitwise_xor(me[0], n))
+        device = jnp.bitwise_xor(me[0], n)
+        side = jnp.right_shift(device, 1)
+        column = pl.ds(pl.multiple_of(jnp.bitwise_and(device, 1) * half, 128), half)
+        for k in range(2):
+            start = k * layout_rows
+            layout_ref[2 * side + k, :, column] = refs[n][start : start + layout_rows, :].astype(
+                jnp.float32
+            )
+        start = 2 * layout_rows
+        qkv_ref[2 * side, :, column] = refs[n][start : start + rows, :].astype(jnp.float32)
+        matrix = refs[n][start + rows : start + 2 * rows, :].astype(jnp.float32)
+
+        @pl.when(side == 0)
         def _():
-            for part in range(2):
-
-                @pl.when(k == part)
-                def _():
-                    start = part * layout_rows
-                    layout_ref[...] = refs[n][start : start + layout_rows, :].astype(jnp.float32)
-                    start = 2 * layout_rows + part * rows
-                    matrix = refs[n][start : start + rows, :].astype(jnp.float32)
-                    last = jnp.logical_and(device >= 2, k == 1)
-
-                    @pl.when(jnp.logical_not(last))
-                    def _():
-                        qkv_ref[...] = matrix
-
-                    @pl.when(last)
-                    def _():
-                        project_ref[...] = matrix
+            qkv_ref[1, :, column] = matrix
+
+        @pl.when(side == 1)
+        def _():
+            project_ref[:, column] = matrix
 
 
 def assemble_backward(line, me, values, layout_rows, rows):
     half = values[0].shape[1]
+    shapes = (f32(4, layout_rows, 2 * half), f32(3, rows, 2 * half), f32(rows, 2 * half))
     return launch(
         line, assemble_backward_kernel, tuple(values), [fixed(value) for value in values],
-        (f32(4, layout_rows, 2 * half), f32(3, rows, 2 * half), f32(rows, 2 * half)),
-        (
-            pl.BlockSpec(
-                (None, layout_rows, half), lambda t, k, s: (2 * (t // 2) + k, 0, t % 2)
-            ),
-            pl.BlockSpec(
-                (None, rows, half), lambda t, k, s: (jnp.minimum(2 * (t // 2) + k, 2), 0, t % 2)
-            ),
-            pl.BlockSpec((rows, half), lambda t, k, s: (0, jnp.where(t == 3, 1, 0))),
-        ),
-        (4, 2), "assemble_backward", scalars=(me,),
+        shapes, [fixed(value) for value in shapes], (1,), "assemble_backward", scalars=(me,),
     )
 
 
@@ -1124,9 +1109,9 @@
         self.bit = lax.axis_size("dp") // 2
         self.got = swap(self.value, "dp", self.bit)
 
-    def step(self):
+    def step(self, waits=()):
         rows, width = self.value.shape[1:]
-        value = stack(self.line, bit_index("dp", self.bit), self.value, self.got)
+        value = stack(self.line, bit_index("dp", self.bit), self.value, self.got, waits)
         self.value = value.reshape(-1, rows, width)
         self.bit //= 2
         self.got = swap(self.value, "dp", self.bit)
@@ -1223,9 +1208,10 @@
     table_rows, mix_rows = layout_part.shape[0], mix_part.shape[0]
     square = jnp.concatenate([w_qkv, patch_proj[None]], axis=0)
     square = lax.dynamic_index_in_dim(square, stream, 0, keepdims=False)
+    square = lax.all_gather(square, "dp", axis=0, tiled=True)
+    square_got = swap(square, "stream", 2)
     mix_part, gain_part = padded(mix_part), padded(gain_part)
     columns = Gather(line, jnp.concatenate([layout_part, mix_part, gain_part], axis=0))
-    square = Gather(line, square)
     full_in = lax.all_gather(in_quarter, ("stream", "dp"), axis=0, tiled=True)
     full_in = full_in.reshape(4, width, -1)
 
@@ -1235,18 +1221,13 @@
     arrived_meta = lax.all_to_all(
         meta.reshape(16, data_count, capacity), "dp", split_axis=1, concat_axis=1, tiled=True
     ).reshape(16, -1)
-    columns.step()
-    square.step()
-    columns.step()
-    square.step()
     column, across, place = place_meta(line, arrived_meta, tokens)
     column_other = swap(column, "stream", 1)
     across_other = column_other.T
+    columns.step()
+    columns.step(waits=(column_other,))
     tables, mix, gains = columns.finish((table_rows, mix_part.shape[0], gain_part.shape[0]))
     tables_got = swap(tables, "stream", 2)
-    (square,) = square.finish((shard_rows,))
-    square = square.reshape(width, width)
-    square_got = swap(square, "stream", 2)
     mix_got = swap(mix, "stream", 2)
     gains = gains[:, :2, :gain_count].transpose(1, 0, 2).reshape(2, width)
     text_rows = jnp.take(text_table, text_index[0], axis=0)
@@ -1382,14 +1363,14 @@
         square_keep.reshape(square_shape), square_got.reshape(square_shape),
     )
     backward_sum = Sum(line, dp_bits[:-2], value, swap(give, "dp", 2))
-    grad_patches = patch_grads(
-        line, slot_keys_of(1.0, slot_index), came_back, matrices, patches.shape[0]
-    )
+    text_grad_rows = (text_grad_rows, rows_side, rows_core, rows_both)
+    grad_text = text_grads(line, text_grad_rows, text_table.shape[0])
     backward_sum.step()
     forward_sum.finish()
     forward_group = stream_group(forward_sum.value)
-    text_grad_rows = (text_grad_rows, rows_side, rows_core, rows_both)
-    grad_text = text_grads(line, text_grad_rows, text_table.shape[0])
+    grad_patches = patch_grads(
+        line, slot_keys_of(1.0, slot_index), came_back, matrices, patches.shape[0]
+    )
     backward_sum.finish()
     small = [join_small(rows[texts + 16 :]) for rows in text_grad_rows]
     small = (small[0] + small[1]) + (small[2] + small[3])

time: 609 us -> 605 us (level)
  waiting for transfers between devices: 132 us -> 145 us
  Pallas kernels: 319 us -> 308 us
  starting transfers between devices: 76.9 us -> 66 us
    pallas_call x42 -> x39, Pallas kernels: 319 us -> 308 us  [launch(): pl.pallas_call(body, out_shape=tuple(out_shape) + (jax.ShapeDtypeStruct((...]
    ppermute x40 -> x37, starting transfers between devices: 63.2 us -> 53.6 us  [swap(): return lax.ppermute(value, axis, [(i, i ^ bit) for i in range(count)])]
    ppermute x40 -> x37, waiting for transfers between devices: 129 us -> 134 us  [swap(): return lax.ppermute(value, axis, [(i, i ^ bit) for i in range(count)])]
    unnamed x95 -> x101, local copies, waits for them, and re-layouts: 23.6 us -> 24.6 us
  transfers between devices with their start and end apart: 45 -> 43, of which waited for: 19 -> 18; matrix products, arithmetic and copies ran while one was open for 5% -> 6% of each run, Pallas kernels for 43% -> 42%
where the time goes in v1:
time: 605 us; the launch traced here: 595 us
  Pallas kernels  308 us (51%)
  waiting for transfers between devices  145 us (24%)
  starting transfers between devices  66 us (11%)
  local copies, waits for them, and re-layouts  51.2 us (8%)
  between operations  14.7 us (2%)
  other arithmetic  7.73 us (1%)
    pallas_call x39, Pallas kernels, launch(): pl.pallas_call(body, out_shape=tuple(out_shape) + (jax.ShapeDtypeStruct((...  308 us
    ppermute x37, waiting for transfers between devices, swap(): return lax.ppermute(value, axis, [(i, i ^ bit) for i in range(count)])  134 us
    ppermute x37, starting transfers between devices, swap(): return lax.ppermute(value, axis, [(i, i ^ bit) for i in range(count)])  53.6 us
    unnamed x101, local copies, waits for them, and re-layouts  24.6 us
  transfers between devices with their start and end apart: 43, of which 18 were waited for; matrix products, arithmetic and copies ran while one was open for 6% of the time, Pallas kernels for 42%

profile of v1, /device:TPU:1, one launch (start us, length us, event | category | flops | bytes accessed | tf_op | source)
XLA Modules:
  0.0 594.8 jit_solution(732796627713825633)
XLA Ops:
  16.7 4.7 find_slots.1
  26.5 5.7 all-to-all-done
  45.7 16.4 %collective-permute-done.1.refs_2_ = bf16[2,320,384]{2,1,0:T(8,128)(2,1)S(1)} collective-permute-done((bf16[2,320,384]{2,1,0:T(8,128)(2,1)}, bf16[2,320,384]{2,1,0:T(8,128)(2,1)S(1)}, u32[]{:S(2)}, u32[]{:S(2)}) %collective-permute-start.1) | collective-permute-done | bytes 491552 | tf_op jit(solution)/shard_map/ppermute | solution.py:1094
  67.9 5.9 gather_fusion
  76.5 12.2 %collective-permute-done.3.refs_2_ = bf16[4,320,384]{2,1,0:T(8,128)(2,1)S(1)} collective-permute-done((bf16[4,320,384]{2,1,0:T(8,128)(2,1)}, bf16[4,320,384]{2,1,0:T(8,128)(2,1)S(1)}, u32[]{:S(2)}, u32[]{:S(2)}) %collective-permute-start.3) | collective-permute-done | bytes 983072 | tf_op jit(solution)/shard_map/ppermute | solution.py:1094
  92.5 6.8 %pack.1 = (bf16[2048,768]{1,0:T(8,128)(2,1)}, bf16[96,768]{1,0:T(8,128)(2,1)}, f32[8,128]{1,0:T(8,128)}) custom-call(s32[2048,8]{1,0:T(8,128)} %get-tuple-element.137.refs_0_, bf16[512,768]{1,0:T(8,128)(2,1)} %refs_1_.1, bf16[512,768]{1,0:T(8,128)(2,1)} %broadcast_select_fusion.refs_2_, bf16[96,768]{1,0:T(8,128)(2,1)} %dynamic-slice_bitcast_fusion.refs_3_, ...), custom_call_target="tpu_custom_call" | custom-call | flops 1 | bytes 1 | tf_op jit(solution)/shard_map/pack/pallas_call | solution.py:37
  99.3 4.9 all-to-all-start.1
  109.2 29.5 %collective-permute-done.6.refs_3_ = bf16[768,768]{1,0:T(8,128)(2,1)S(1)} collective-permute-done((bf16[768,768]{1,0:T(8,128)(2,1)}, bf16[768,768]{1,0:T(8,128)(2,1)S(1)}, u32[]{:S(2)}, u32[]{:S(2)}) %collective-permute-start.6) | collective-permute-done | bytes 1179680 | tf_op jit(solution)/shard_map/ppermute | solution.py:1094
  138.7 5.0 collective-permute-start.7
  143.7 8.1 %layout_lookup.2 = (f32[1024,384]{1,0:T(8,128)}, f32[1024,384]{1,0:T(8,128)}, f32[8,128]{1,0:T(8,128)}) custom-call(s32[1]{0:T(128)} %bitcast.18.refs_0_, s32[1024,8]{1,0:T(8,128)} %get-tuple-element.136.refs_1_, s32[1024,8]{1,0:T(8,128)} %copy.47.refs_4_.refs_2_, bf16[8,256,384]{2,1,0:T(8,128)(2,1)} %bitcast.98, f32[8,128]{1,0:T(8,128)} %get-tuple-element.147.refs_4_), custom_call_target="tpu_custom_call" | custom-call | flops 1 | bytes 1 | tf_op jit(solution)/shard_map/layout_lookup/pallas_call | solution.py:37
  152.8 5.0 arrange.1
  157.8 15.2 %collective-permute-done.4.refs_3_ = bf16[8,256,384]{2,1,0:T(8,128)(2,1)S(1)} collective-permute-done((bf16[8,256,384]{2,1,0:T(8,128)(2,1)}, bf16[8,256,384]{2,1,0:T(8,128)(2,1)S(1)}, u32[]{:S(2)}, u32[]{:S(2)}) %collective-permute-start.4) | collective-permute-done | bytes 1572896 | tf_op jit(solution)/shard_map/ppermute | solution.py:1094
  174.2 8.6 %layout_lookup.3 = (f32[1024,384]{1,0:T(8,128)}, f32[1024,384]{1,0:T(8,128)}, f32[8,128]{1,0:T(8,128)}) custom-call(s32[1]{0:T(128)S(6)} %sub.42.refs_0_, s32[1024,8]{1,0:T(8,128)} %get-tuple-element.136.refs_1_, s32[1024,8]{1,0:T(8,128)} %copy.47.refs_4_.refs_2_, bf16[8,256,384]{2,1,0:T(8,128)(2,1)} %copy-done.7, f32[1024,384]{1,0:T(8,128)} %get-tuple-element.148.refs_4_, ...), custom_call_target="tpu_custom_call" | custom-call | flops 1 | bytes 1 | tf_op jit(solution)/shard_map/layout_lookup/pallas_call | solution.py:37
  190.8 17.0 %embed.1 = (bf16[768,1024]{1,0:T(8,128)(2,1)}, bf16[1024,768]{1,0:T(8,128)(2,1)}, bf16[768,1024]{1,0:T(8,128)(2,1)}, bf16[3,1024,768]{2,1,0:T(8,128)(2,1)}, f32[8,128]{1,0:T(8,128)}) custom-call(s32[8,2048]{1,0:T(8,128)} %get-tuple-element.135.refs_0_, s32[1024,8]{1,0:T(8,128)} %get-tuple-element.136.refs_1_, bf16[2048,768]{1,0:T(8,128)(2,1)} %bitcast.88, ...), custom_call_target="tpu_custom_call" | custom-call | flops 1 | bytes 1 | tf_op jit(solution)/shard_map/embed/pallas_call | solution.py:37
  215.2 28.7 %attention_forward.1 = (bf16[1024,768]{1,0:T(8,128)(2,1)}, f32[1024,768]{1,0:T(8,128)}, f32[8,128]{1,0:T(8,128)}) custom-call(bf16[3,1024,768]{2,1,0:T(8,128)(2,1)} %get-tuple-element.158.refs_0_.refs_1_.refs_2_, bf16[3,1024,768]{2,1,0:T(8,128)(2,1)} %get-tuple-element.158.refs_0_.refs_1_.refs_2_, ...), custom_call_target="tpu_custom_call" | custom-call | flops 1 | bytes 1 | tf_op jit(solution)/shard_map/attention_forward/pallas_call | solution.py:37
  244.7 34.8 %feed_forward.1 = (bf16[1024,768]{1,0:T(8,128)(2,1)}, bf16[3072,1024]{1,0:T(8,128)(2,1)}, bf16[1024,3072]{1,0:T(8,128)(2,1)}, bf16[768,1024]{1,0:T(8,128)(2,1)},...) custom-call(s32[1]{0:T(128)} %bitcast.refs_0_, ...), custom_call_target="tpu_custom_call" | custom-call | flops 1 | bytes 1 | tf_op jit(solution)/shard_map/feed_forward/pallas_call | solution.py:37
  279.5 9.1 %contract_halves.2 = (bf16[3072,384]{1,0:T(8,128)(2,1)}, bf16[3072,384]{1,0:T(8,128)(2,1)}, f32[8,128]{1,0:T(8,128)}) custom-call(s32[1]{0:T(128)} %bitcast.refs_0_, bf16[3072,1024]{1,0:T(8,128)(2,1)} %get-tuple-element.174.refs_1_, bf16[1024,768]{1,0:T(8,128)(2,1)} %refs_2_.1, f32[8,128]{1,0:T(8,128)} %get-tuple-element.175.refs_3_), custom_call_target="tpu_custom_call" | custom-call | flops 1 | bytes 1 | tf_op jit(solution)/shard_map/contract_halves/pallas_call | solution.py:37
  292.9 9.8 %contract_quarters.1 = (bf16[2,8,2,96,384]{4,3,2,1,0:T(8,128)(2,1)}, bf16[2,8,2,96,384]{4,3,2,1,0:T(8,128)(2,1)}, f32[8,128]{1,0:T(8,128)}) custom-call(s32[1]{0:T(128)} %bitcast.refs_0_, bf16[768,1024]{1,0:T(8,128)(2,1)} %get-tuple-element.170.refs_1_, bf16[1024,3072]{1,0:T(8,128)(2,1)} %get-tuple-element.171.refs_2_, f32[8,128]{1,0:T(8,128)} %get-tuple-element.177.refs_3_), custom_call_target="tpu_custom_call" | custom-call | flops 1 | bytes 1 | tf_op jit(solution)/shard_map/contract_quarters/pallas_call | solution.py:37
  303.4 4.7 collective-permute-done.13
  309.7 5.4 rows_fold.3
  324.4 36.6 %attention_backward.1 = (bf16[3,1024,768]{2,1,0:T(8,128)(2,1)}, f32[12,8,512]{2,1,0:T(8,128)}, f32[8,128]{1,0:T(8,128)}) custom-call(bf16[3,1024,768]{2,1,0:T(8,128)(2,1)} %get-tuple-element.158.refs_0_.refs_1_.refs_2_, bf16[3,1024,768]{2,1,0:T(8,128)(2,1)} %get-tuple-element.158.refs_0_.refs_1_.refs_2_, ...), custom_call_target="tpu_custom_call" | custom-call | flops 1 | bytes 1 | tf_op jit(solution)/shard_map/attention_backward/pallas_call | solution.py:37
  373.8 9.9 %input_grad.1 = (bf16[1024,768]{1,0:T(8,128)(2,1)}, bf16[1024,384]{1,0:T(8,128)(2,1)}, bf16[1024,384]{1,0:T(8,128)(2,1)}, f32[8,768]{1,0:T(8,128)}, f32[8,128]{1,0:T(8,128)}) custom-call(s32[1]{0:T(128)} %bitcast.refs_0_, bf16[1024,768]{1,0:T(8,128)(2,1)} %get-tuple-element.157.refs_1_, f32[1024,768]{1,0:T(8,128)} %get-tuple-element.167.refs_2_, ...), custom_call_target="tpu_custom_call" | custom-call | flops 1 | bytes 1 | tf_op jit(solution)/shard_map/input_grad/pallas_call | solution.py:37
  391.9 7.0 %return_rows.1 = (bf16[8,272,768]{2,1,0:T(8,128)(2,1)}, f32[8,128]{1,0:T(8,128)}) custom-call(s32[2048,1]{1,0:T(8,128)} %copy.53.refs_0_, bf16[1024,768]{1,0:T(8,128)(2,1)} %get-tuple-element.195.refs_1_.refs_4_, f32[8,768]{1,0:T(8,128)} %pad.27.refs_2_, f32[8,128]{1,0:T(8,128)} %get-tuple-element.204.refs_3_), custom_call_target="tpu_custom_call" | custom-call | flops 1 | bytes 1 | tf_op jit(solution)/shard_map/return_rows/pallas_call | solution.py:37
  407.7 13.0 %layout_grad.1 = (bf16[8,2,128,384]{3,2,1,0:T(8,128)(2,1)}, bf16[8,2,128,384]{3,2,1,0:T(8,128)(2,1)}, f32[8,128]{1,0:T(8,128)}) custom-call(s32[1]{0:T(128)} %bitcast.18.refs_0_, s32[8,1024]{1,0:T(8,128)} %get-tuple-element.210.refs_1_, s32[8,1024]{1,0:T(8,128)} %bitcast.141, bf16[1024,384]{1,0:T(8,128)(2,1)} %get-tuple-element.211.refs_3_, ...), custom_call_target="tpu_custom_call" | custom-call | flops 1 | bytes 1 | tf_op jit(solution)/shard_map/layout_grad/pallas_call | solution.py:37
  420.8 10.1 %square_grads.1 = (bf16[8,2,2,96,384]{4,3,2,1,0:T(8,128)(2,1)}, bf16[8,2,2,96,384]{4,3,2,1,0:T(8,128)(2,1)}, f32[8,128]{1,0:T(8,128)}) custom-call(s32[1]{0:T(128)} %bitcast.refs_0_, bf16[768,1024]{1,0:T(8,128)(2,1)} %get-tuple-element.208.refs_1_, bf16[3,1024,768]{2,1,0:T(8,128)(2,1)} %get-tuple-element.187.refs_3_.refs_2_, ...), custom_call_target="tpu_custom_call" | custom-call | flops 1 | bytes 1 | tf_op jit(solution)/shard_map/square_grads/pallas_call | solution.py:37
  443.2 24.1 %collective-permute-done.22 = bf16[8,2,128,384]{3,2,1,0:T(8,128)(2,1)} collective-permute-done((bf16[8,2,128,384]{3,2,1,0:T(8,128)(2,1)}, bf16[8,2,128,384]{3,2,1,0:T(8,128)(2,1)}, u32[]{:S(2)}, u32[]{:S(2)}) %collective-permute-start.22) | collective-permute-done | bytes 1572896 | tf_op jit(solution)/shard_map/ppermute | solution.py:1094
  470.7 5.0 all-to-all-done.2.refs_1_
  477.5 6.4 %unpack_text.1 = (bf16[544,768]{1,0:T(8,128)(2,1)}, f32[8,128]{1,0:T(8,128)}) custom-call(s32[8,272]{1,0:T(8,128)} %pad.28.refs_0_, bf16[8,272,768]{2,1,0:T(8,128)(2,1)} %copy-done.2, s32[8,512]{1,0:T(8,128)} %get-tuple-element.138.refs_2_, f32[8,128]{1,0:T(8,128)} %get-tuple-element.223.refs_3_), custom_call_target="tpu_custom_call" | custom-call | flops 1 | bytes 1 | tf_op jit(solution)/shard_map/unpack_text/pallas_call | solution.py:37
  487.6 5.1 collective-permute-done.21
  499.0 11.5 %collective-permute-done.27.refs_1_ = bf16[544,768]{1,0:T(8,128)(2,1)S(1)} collective-permute-done((bf16[544,768]{1,0:T(8,128)(2,1)}, bf16[544,768]{1,0:T(8,128)(2,1)S(1)}, u32[]{:S(2)}, u32[]{:S(2)}) %collective-permute-start.27) | collective-permute-done | bytes 835616 | tf_op jit(solution)/shard_map/ppermute | solution.py:1094
  527.1 17.6 %text_grads.1 = (f32[4016,768]{1,0:T(8,128)}, f32[8,128]{1,0:T(8,128)}) custom-call(bf16[544,768]{1,0:T(8,128)(2,1)} %get-tuple-element.235.refs_0_, bf16[544,768]{1,0:T(8,128)(2,1)} %copy-done.14, bf16[544,768]{1,0:T(8,128)(2,1)} %collective-permute-done.28.refs_2_, bf16[544,768]{1,0:T(8,128)(2,1)} %copy-done.15, f32[8,128]{1,0:T(8,128)} %get-tuple-element.236.refs_4_), custom_call_target="tpu_custom_call" | custom-call | flops 1 | bytes 1 | tf_op jit(solution)/shard_map/text_grads/pallas_call | solution.py:37
  554.4 8.4 %patch_grads.1 = (f32[512,768]{1,0:T(8,128)}, f32[8,128]{1,0:T(8,128)}) custom-call(s32[8,272]{1,0:T(8,128)} %pad.25.refs_0_, bf16[8,272,768]{2,1,0:T(8,128)(2,1)} %copy-done.2, bf16[4,768,768]{2,1,0:T(8,128)(2,1)} %get-tuple-element.154.refs_6_.refs_8_.refs_4_.refs_2_, f32[8,128]{1,0:T(8,128)} %get-tuple-element.239.refs_3_), custom_call_target="tpu_custom_call" | custom-call | flops 1 | bytes 1 | tf_op jit(solution)/shard_map/patch_grads/pallas_call | solution.py:37
  (260 shorter events, 187.7 us)
Async XLA Ops:
  7.2 97.0 %all-gather.8.cloned.1.call-start = ((), (), s32[]{:S(2)}) async-start(), calls=%async_computation.4 | async-start | bytes 1327104 | tf_op jit(solution)/shard_map/all_gather | solution.py:1211
  9.0 235.0 %all-gather.10.cloned.1.call-start = ((), (), s32[]{:S(2)}) async-start(), calls=%async_computation.5 | async-start | bytes 4866048 | tf_op jit(solution)/shard_map/all_gather | solution.py:1215
  12.9 24.2 %collective-permute-start = (bf16[1,320,384]{2,1,0:T(8,128)(2,1)S(1)}, bf16[1,320,384]{2,1,0:T(8,128)(2,1)S(1)}, u32[]{:S(2)}, u32[]{:S(2)}) collective-permute-start(bf16[1,320,384]{2,1,0:T(8,128)(2,1)S(1)} %fusion.4.refs_1_), channel_id=1, source_target_pairs={{0,16},{4,20},{8,24},{12,28},{16,0},{20,4},{24,8},{28,12},{1,17},{... | collective-permute-start | bytes 737288 | tf_op jit(solution)/shard_map/ppermute | solution.py:1094
  26.5 217.5 %all-gather.6.cloned.1.call-start = ((), (), s32[]{:S(2)}) async-start(), calls=%async_computation.3 | async-start | bytes 4866048 | tf_op jit(solution)/shard_map/all_gather | solution.py:1238
  39.7 22.4 %collective-permute-start.1 = (bf16[2,320,384]{2,1,0:T(8,128)(2,1)}, bf16[2,320,384]{2,1,0:T(8,128)(2,1)S(1)}, u32[]{:S(2)}, u32[]{:S(2)}) collective-permute-start(bf16[2,320,384]{2,1,0:T(8,128)(2,1)} %bitcast.129), channel_id=1, source_target_pairs={{0,8},{4,12},{8,0},{12,4},{16,24},{20,28},{24,16},{28,20},{1,9},{5... | collective-permute-start | bytes 1474568 | tf_op jit(solution)/shard_map/ppermute | solution.py:1094
  65.0 23.7 %collective-permute-start.3 = (bf16[4,320,384]{2,1,0:T(8,128)(2,1)}, bf16[4,320,384]{2,1,0:T(8,128)(2,1)S(1)}, u32[]{:S(2)}, u32[]{:S(2)}) collective-permute-start(bf16[4,320,384]{2,1,0:T(8,128)(2,1)} %bitcast.110), channel_id=1, source_target_pairs={{0,4},{4,0},{8,12},{12,8},{16,20},{20,16},{24,28},{28,24},{1,5},{5... | collective-permute-start | bytes 2949128 | tf_op jit(solution)/shard_map/ppermute | solution.py:1094
  99.3 89.9 %all-to-all-start.1 = ((bf16[8,256,768]{2,1,0:T(8,128)(2,1)}), bf16[8,256,768]{2,1,0:T(8,128)(2,1)S(1)}, u32[]{:S(2)}, u32[]{:S(2)}) async-start(bf16[8,256,768]{2,1,0:T(8,128)(2,1)} %bitcast.90), calls=%async_computation.1 | async-start | bytes 6291456 | tf_op jit(solution)/shard_map/all_to_all | solution.py:1235
  104.2 34.4 %collective-permute-start.6 = (bf16[768,768]{1,0:T(8,128)(2,1)}, bf16[768,768]{1,0:T(8,128)(2,1)S(1)}, u32[]{:S(2)}, u32[]{:S(2)}) collective-permute-start(bf16[768,768]{1,0:T(8,128)(2,1)} %bitcast.105), channel_id=1, source_target_pairs={{0,2},{1,3},{2,0},{3,1},{4,6},{5,7},{6,4},{7,5},{8,10},{9,11},{10,... | collective-permute-start | bytes 3538952 | tf_op jit(solution)/shard_map/ppermute | solution.py:1094
  105.5 67.5 %collective-permute-start.4 = (bf16[8,256,384]{2,1,0:T(8,128)(2,1)}, bf16[8,256,384]{2,1,0:T(8,128)(2,1)S(1)}, u32[]{:S(2)}, u32[]{:S(2)}) collective-permute-start(bf16[8,256,384]{2,1,0:T(8,128)(2,1)} %bitcast.97), channel_id=1, source_target_pairs={{0,2},{1,3},{2,0},{3,1},{4,6},{5,7},{6,4},{7,5},{8,10},{9,11},{10,... | collective-permute-start | bytes 4718600 | tf_op jit(solution)/shard_map/ppermute | solution.py:1094
  105.8 46.0 %collective-permute-start.5 = (bf16[768,768]{1,0:T(8,128)(2,1)}, bf16[768,768]{1,0:T(8,128)(2,1)S(1)}, u32[]{:S(2)}, u32[]{:S(2)}) collective-permute-start(bf16[768,768]{1,0:T(8,128)(2,1)} %bitcast.106), channel_id=1, source_target_pairs={{0,1},{1,0},{2,3},{3,2},{4,5},{5,4},{6,7},{7,6},{8,9},{9,8},{10,11... | collective-permute-start | bytes 3538952 | tf_op jit(solution)/shard_map/ppermute | solution.py:1094
  138.7 13.1 %collective-permute-start.7 = (bf16[768,768]{1,0:T(8,128)(2,1)S(1)}, bf16[768,768]{1,0:T(8,128)(2,1)}, u32[]{:S(2)}, u32[]{:S(2)}) collective-permute-start(bf16[768,768]{1,0:T(8,128)(2,1)S(1)} %collective-permute-done.6.refs_3_), channel_id=1, source_target_pairs={{0,1},{1,0},{2,3},{3,2},{4,5},{5,4},{6,7},{7,6},{8,9},{9,8},{10,11... | collective-permute-start | bytes 3538952 | tf_op jit(solution)/shard_map/ppermute | solution.py:1094
  185.8 22.1 %collective-permute-start.9 = (bf16[8,48,384]{2,1,0:T(8,128)(2,1)S(1)}, bf16[8,48,384]{2,1,0:T(8,128)(2,1)}, u32[]{:S(2)}, u32[]{:S(2)}) collective-permute-start(bf16[8,48,384]{2,1,0:T(8,128)(2,1)S(1)} %bitcast.136), channel_id=1, source_target_pairs={{0,2},{1,3},{2,0},{3,1},{4,6},{5,7},{6,4},{7,5},{8,10},{9,11},{10,... | collective-permute-start | bytes 884744 | tf_op jit(solution)/shard_map/ppermute | solution.py:1094
  209.8 34.1 %collective-permute-start.10 = (bf16[768,384]{1,0:T(8,128)(2,1)}, bf16[768,384]{1,0:T(8,128)(2,1)S(1)}, u32[]{:S(2)}, u32[]{:S(2)}) collective-permute-start(bf16[768,384]{1,0:T(8,128)(2,1)} %bitcast.121), channel_id=1, source_target_pairs={{0,1},{1,0},{2,3},{3,2},{4,5},{5,4},{6,7},{7,6},{8,9},{9,8},{10,11... | collective-permute-start | bytes 1769480 | tf_op jit(solution)/shard_map/ppermute | solution.py:1094
  288.6 19.5 %collective-permute-start.12 = (bf16[3072,384]{1,0:T(8,128)(2,1)}, bf16[3072,384]{1,0:T(8,128)(2,1)S(1)}, u32[]{:S(2)}, u32[]{:S(2)}) collective-permute-start(bf16[3072,384]{1,0:T(8,128)(2,1)} %get-tuple-element.181), channel_id=1, source_target_pairs={{0,1},{1,0},{2,3},{3,2},{4,5},{5,4},{6,7},{7,6},{8,9},{9,8},{10,11... | collective-permute-start | bytes 7077896 | tf_op jit(solution)/shard_map/ppermute | solution.py:1094
  302.7 14.1 %collective-permute-start.11 = (bf16[2,8,2,96,384]{4,3,2,1,0:T(8,128)(2,1)}, bf16[2,8,2,96,384]{4,3,2,1,0:T(8,128)(2,1)S(1)}, u32[]{:S(2)}, u32[]{:S(2)}) collective-permute-start(bf16[2,8,2,96,384]{4,3,2,1,0:T(8,128)(2,1)} %get-tuple-element.179), channel_id=1, source_target_pairs={{0,1},{1,0},{2,3},{3,2},{4,5},{5,4},{6,7},{7,6},{8,9},{9,8},{10,11... | collective-permute-start | bytes 7077896 | tf_op jit(solution)/shard_map/ppermute | solution.py:1094
  315.1 45.9 %collective-permute-start.15 = (bf16[8,240,384]{2,1,0:T(8,128)(2,1)}, bf16[8,240,384]{2,1,0:T(8,128)(2,1)S(1)}, u32[]{:S(2)}, u32[]{:S(2)}) collective-permute-start(bf16[8,240,384]{2,1,0:T(8,128)(2,1)} %get-tuple-element.191), channel_id=1, source_target_pairs={{0,2},{1,3},{2,0},{3,1},{4,6},{5,7},{6,4},{7,5},{8,10},{9,11},{10,... | collective-permute-start | bytes 4423688 | tf_op jit(solution)/shard_map/ppermute | solution.py:1094
  322.5 43.0 %collective-permute-start.14 = (bf16[8,1,192,384]{3,2,1,0:T(8,128)(2,1)}, bf16[8,1,192,384]{3,2,1,0:T(8,128)(2,1)S(1)}, u32[]{:S(2)}, u32[]{:S(2)}) collective-permute-start(bf16[8,1,192,384]{3,2,1,0:T(8,128)(2,1)} %get-tuple-element.189), channel_id=1, source_target_pairs={{0,4},{4,0},{8,12},{12,8},{16,20},{20,16},{24,28},{28,24},{1,5},{5... | collective-permute-start | bytes 3538952 | tf_op jit(solution)/shard_map/ppermute | solution.py:1094
  369.4 15.7 %collective-permute-start.17 = (bf16[1,4,192,384]{3,2,1,0:T(8,128)(2,1)}, bf16[1,4,192,384]{3,2,1,0:T(8,128)(2,1)S(1)}, u32[]{:S(2)}, u32[]{:S(2)}) collective-permute-start(bf16[1,4,192,384]{3,2,1,0:T(8,128)(2,1)} %get-tuple-element.202), channel_id=1, source_target_pairs={{0,2},{1,3},{2,0},{3,1},{4,6},{5,7},{6,4},{7,5},{8,10},{9,11},{10,... | collective-permute-start | bytes 1769480 | tf_op jit(solution)/shard_map/ppermute | solution.py:1094
  369.7 17.2 %collective-permute-start.16 = (bf16[4,1,240,384]{3,2,1,0:T(8,128)(2,1)}, bf16[4,1,240,384]{3,2,1,0:T(8,128)(2,1)S(1)}, u32[]{:S(2)}, u32[]{:S(2)}) collective-permute-start(bf16[4,1,240,384]{3,2,1,0:T(8,128)(2,1)} %get-tuple-element.200), channel_id=1, source_target_pairs={{0,4},{4,0},{8,12},{12,8},{16,20},{20,16},{24,28},{28,24},{1,5},{5... | collective-permute-start | bytes 2211848 | tf_op jit(solution)/shard_map/ppermute | solution.py:1094
  398.9 76.9 %all-to-all-start.2 = ((bf16[8,272,768]{2,1,0:T(8,128)(2,1)}), bf16[8,272,768]{2,1,0:T(8,128)(2,1)S(1)}, u32[]{:S(2)}, u32[]{:S(2)}) async-start(bf16[8,272,768]{2,1,0:T(8,128)(2,1)} %get-tuple-element.205), calls=%async_computation.2 | async-start | bytes 6684672 | tf_op jit(solution)/shard_map/all_to_all | solution.py:1314
  431.2 36.2 %collective-permute-start.22 = (bf16[8,2,128,384]{3,2,1,0:T(8,128)(2,1)}, bf16[8,2,128,384]{3,2,1,0:T(8,128)(2,1)}, u32[]{:S(2)}, u32[]{:S(2)}) collective-permute-start(bf16[8,2,128,384]{3,2,1,0:T(8,128)(2,1)} %get-tuple-element.221), channel_id=1, source_target_pairs={{0,2},{1,3},{2,0},{3,1},{4,6},{5,7},{6,4},{7,5},{8,10},{9,11},{10,... | collective-permute-start | bytes 4718600 | tf_op jit(solution)/shard_map/ppermute | solution.py:1094
  441.3 51.4 %collective-permute-start.21 = (bf16[8,1,192,384]{3,2,1,0:T(8,128)(2,1)}, bf16[8,1,192,384]{3,2,1,0:T(8,128)(2,1)}, u32[]{:S(2)}, u32[]{:S(2)}) collective-permute-start(bf16[8,1,192,384]{3,2,1,0:T(8,128)(2,1)} %get-tuple-element.219), channel_id=1, source_target_pairs={{0,2},{1,3},{2,0},{3,1},{4,6},{5,7},{6,4},{7,5},{8,10},{9,11},{10,... | collective-permute-start | bytes 3538952 | tf_op jit(solution)/shard_map/ppermute | solution.py:1094
  483.9 26.6 %collective-permute-start.27 = (bf16[544,768]{1,0:T(8,128)(2,1)}, bf16[544,768]{1,0:T(8,128)(2,1)S(1)}, u32[]{:S(2)}, u32[]{:S(2)}) collective-permute-start(bf16[544,768]{1,0:T(8,128)(2,1)} %get-tuple-element.235.refs_0_), channel_id=1, source_target_pairs={{0,2},{1,3},{2,0},{3,1},{4,6},{5,7},{6,4},{7,5},{8,10},{9,11},{10,... | collective-permute-start | bytes 2506760 | tf_op jit(solution)/shard_map/ppermute | solution.py:1094
  485.1 29.5 %collective-permute-start.24 = (bf16[4,1,256,384]{3,2,1,0:T(8,128)(2,1)S(1)}, bf16[4,1,256,384]{3,2,1,0:T(8,128)(2,1)S(1)}, u32[]{:S(2)}, u32[]{:S(2)}) collective-permute-start(bf16[4,1,256,384]{3,2,1,0:T(8,128)(2,1)S(1)} %copy-done.43), channel_id=1, source_target_pairs={{0,4},{4,0},{8,12},{12,8},{16,20},{20,16},{24,28},{28,24},{1,5},{5... | collective-permute-start | bytes 2359304 | tf_op jit(solution)/shard_map/ppermute | solution.py:1094
  487.6 23.8 %collective-permute-start.18 = (bf16[2,432,384]{2,1,0:T(8,128)(2,1)S(1)}, bf16[2,432,384]{2,1,0:T(8,128)(2,1)S(1)}, u32[]{:S(2)}, u32[]{:S(2)}) collective-permute-start(bf16[2,432,384]{2,1,0:T(8,128)(2,1)S(1)} %copy-done.44), channel_id=1, source_target_pairs={{0,8},{4,12},{8,0},{12,4},{16,24},{20,28},{24,16},{28,20},{1,9},{5... | collective-permute-start | bytes 1990664 | tf_op jit(solution)/shard_map/ppermute | solution.py:1094
  495.6 20.2 %collective-permute-start.25 = (bf16[4,1,192,384]{3,2,1,0:T(8,128)(2,1)}, bf16[4,1,192,384]{3,2,1,0:T(8,128)(2,1)S(1)}, u32[]{:S(2)}, u32[]{:S(2)}) collective-permute-start(bf16[4,1,192,384]{3,2,1,0:T(8,128)(2,1)} %get-tuple-element.231), channel_id=1, source_target_pairs={{0,4},{4,0},{8,12},{12,8},{16,20},{20,16},{24,28},{28,24},{1,5},{5... | collective-permute-start | bytes 1769480 | tf_op jit(solution)/shard_map/ppermute | solution.py:1094
  497.2 29.0 %collective-permute-start.28 = (bf16[544,768]{1,0:T(8,128)(2,1)S(1)}, bf16[544,768]{1,0:T(8,128)(2,1)}, u32[]{:S(2)}, u32[]{:S(2)}) collective-permute-start(bf16[544,768]{1,0:T(8,128)(2,1)S(1)} %copy-done.16), channel_id=1, source_target_pairs={{0,1},{1,0},{2,3},{3,2},{4,5},{5,4},{6,7},{7,6},{8,9},{9,8},{10,11... | collective-permute-start | bytes 2506760 | tf_op jit(solution)/shard_map/ppermute | solution.py:1094
  510.5 15.8 %collective-permute-start.29 = (bf16[544,768]{1,0:T(8,128)(2,1)S(1)}, bf16[544,768]{1,0:T(8,128)(2,1)S(1)}, u32[]{:S(2)}, u32[]{:S(2)}) collective-permute-start(bf16[544,768]{1,0:T(8,128)(2,1)S(1)} %collective-permute-done.27.refs_1_), channel_id=1, source_target_pairs={{0,1},{1,0},{2,3},{3,2},{4,5},{5,4},{6,7},{7,6},{8,9},{9,8},{10,11... | collective-permute-start | bytes 2506760 | tf_op jit(solution)/shard_map/ppermute | solution.py:1094
  520.7 24.0 %collective-permute-start.26 = (bf16[2,448,384]{2,1,0:T(8,128)(2,1)}, bf16[2,448,384]{2,1,0:T(8,128)(2,1)S(1)}, u32[]{:S(2)}, u32[]{:S(2)}) collective-permute-start(bf16[2,448,384]{2,1,0:T(8,128)(2,1)} %get-tuple-element.234), channel_id=1, source_target_pairs={{0,8},{4,12},{8,0},{12,4},{16,24},{20,28},{24,16},{28,20},{1,9},{5... | collective-permute-start | bytes 2064392 | tf_op jit(solution)/shard_map/ppermute | solution.py:1094
  523.2 28.3 %collective-permute-start.23 = (bf16[1,1,432,384]{3,2,1,0:T(8,128)(2,1)}, bf16[1,1,432,384]{3,2,1,0:T(8,128)(2,1)S(1)}, u32[]{:S(2)}, u32[]{:S(2)}) collective-permute-start(bf16[1,1,432,384]{3,2,1,0:T(8,128)(2,1)} %get-tuple-element.227), channel_id=1, source_target_pairs={{0,16},{4,20},{8,24},{12,28},{16,0},{20,4},{24,8},{28,12},{1,17},{... | collective-permute-start | bytes 995336 | tf_op jit(solution)/shard_map/ppermute | solution.py:1094
  548.2 17.2 %collective-permute-start.30 = (bf16[1,1,448,384]{3,2,1,0:T(8,128)(2,1)}, bf16[1,1,448,384]{3,2,1,0:T(8,128)(2,1)S(1)}, u32[]{:S(2)}, u32[]{:S(2)}) collective-permute-start(bf16[1,1,448,384]{3,2,1,0:T(8,128)(2,1)} %get-tuple-element.243), channel_id=1, source_target_pairs={{0,16},{4,20},{8,24},{12,28},{16,0},{20,4},{24,8},{28,12},{1,17},{... | collective-permute-start | bytes 1032200 | tf_op jit(solution)/shard_map/ppermute | solution.py:1094
  554.2 17.8 %collective-permute-start.35 = (bf16[432,384]{1,0:T(8,128)(2,1)}, bf16[432,384]{1,0:T(8,128)(2,1)S(1)}, u32[]{:S(2)}, u32[]{:S(2)}) collective-permute-start(bf16[432,384]{1,0:T(8,128)(2,1)} %get-tuple-element.246.refs_1_), channel_id=1, source_target_pairs={{0,2},{1,3},{2,0},{3,1},{4,6},{5,7},{6,4},{7,5},{8,10},{9,11},{10,... | collective-permute-start | bytes 995336 | tf_op jit(solution)/shard_map/ppermute | solution.py:1094
  (58 other events, 355.5 us)
Sparse Core Ops, SparseCore 0:
  10.8 45.7 all-gather.7
  59.5 86.9 all-gather.9
  149.5 83.5 all-gather.5

commit v2 on v1

--- a/solution.py
+++ b/solution.py
@@ -491,7 +491,7 @@
     raw = dot_nn(pick, arrived_ref[...])
     narrow = raw.astype(jnp.bfloat16)
     kind = column_ref[:, 0:1]
-    visual_ref[...] = jnp.where(kind == 1, raw, 0.0).T.astype(jnp.bfloat16)
+    visual_ref[...] = jnp.where(kind == 1, raw, 0.0).astype(jnp.bfloat16).T
     projected = dot_nn(narrow, project_ref[...])
     first = half_ref[0:1, 0:1] == 0
     own, got = own_ref[...], got_ref[...]
@@ -500,9 +500,8 @@
     packed_ref[...] = embedded.astype(jnp.bfloat16)
     packed = packed_ref[...].astype(jnp.float32)
     scale = lax.rsqrt(jnp.mean(packed * packed, axis=-1, keepdims=True) + EPSILON)
-    normed = packed * scale * gain_ref[0:1, :].astype(jnp.float32)
-    normed_ref[...] = normed.T.astype(jnp.bfloat16)
-    normed = normed.astype(jnp.bfloat16)
+    normed = (packed * scale * gain_ref[0:1, :].astype(jnp.float32)).astype(jnp.bfloat16)
+    normed_ref[...] = normed.T
     for part in range(3):
         out_ref[part] = dot_nn(normed, weight_ref[part]).astype(jnp.bfloat16)
 
@@ -693,13 +692,12 @@
     first = core[0] == 0
     mix = jnp.concatenate([jnp.where(first, own, other), jnp.where(first, other, own)], axis=1)
     attended = packed_ref[...].astype(jnp.float32) + dot_nn(mixed_ref[...], mix)
-    turned_ref[...] = mixed_ref[...].astype(jnp.float32).T.astype(jnp.bfloat16)
+    turned_ref[...] = mixed_ref[...].T
     scale = lax.rsqrt(jnp.mean(attended * attended, axis=-1, keepdims=True) + EPSILON)
     unit = attended * scale
     gain = gain_ref[0:1, :].astype(jnp.float32)
-    normed = unit * gain
-    normed_ref[...] = normed.T.astype(jnp.bfloat16)
-    normed = normed.astype(jnp.bfloat16)
+    normed = (unit * gain).astype(jnp.bfloat16)
+    normed_ref[...] = normed.T
     out_grad = grad_ref[...]
     result = attended
     back = jnp.zeros_like(attended)
@@ -710,9 +708,8 @@
         square = hidden * hidden
         tanh = jnp.tanh(hidden * (RATE + RATE * 0.044715 * square))
         half = 0.5 + 0.5 * tanh
-        active = hidden * half
-        active_ref[cut, :] = active.T.astype(jnp.bfloat16)
-        active = active.astype(jnp.bfloat16)
+        active = (hidden * half).astype(jnp.bfloat16)
+        active_ref[cut, :] = active.T
         slope = half + hidden * half * (1.0 - tanh) * (RATE + 3.0 * 0.044715 * RATE * square)
         result = result + dot_nn(active, down_ref[cut, :])
         grad_hidden = (dot_nt(out_grad, down_ref[cut, :]) * slope).astype(jnp.bfloat16)
@@ -1261,14 +1258,20 @@
         line, own_core, packed, mixed, out_grad, mix_own, mix_other, full_in, full_down, gains[1:]
     )
 
+    in_keep, in_give = contract_quarters(
+        line, own_core, normed_two, grad_hidden, data_count
+    )
+    in_got = swap(in_give, "stream", 1)
     down_keep, down_give = contract_halves(line, own_core, active, out_grad)
     down_got = swap(down_give, "stream", 1)
     mix_keep, mix_give = contract_halves(line, own_core, turned, grad_branch)
     mix_got = swap(mix_give, "stream", 1)
-    in_keep, in_give = contract_quarters(
-        line, own_core, normed_two, grad_hidden, data_count
-    )
-    in_got = swap(in_give, "stream", 1)
+    in_shape = (data_count, 2, 2 * shard_rows, half_width)
+    in_keep, in_give = fold(
+        line, bit_index("dp", 1), in_keep.reshape(in_shape)[:, :, None],
+        in_got.reshape(in_shape)[:, :, None],
+    )
+    in_got = swap(in_give, "dp", 1)
     down_shape = (data_count, 2, down_keep.shape[0] // data_count // 2, half_width)
     mix_shape = (data_count, 2, mix_rows, half_width)
     rows_keep, rows_give = rows_fold(
@@ -1276,12 +1279,6 @@
         mix_keep.reshape(mix_shape), mix_got.reshape(mix_shape),
     )
     rows_got = swap(rows_give, "stream", 2)
-    in_shape = (data_count, 2, 2 * shard_rows, half_width)
-    in_keep, in_give = fold(
-        line, bit_index("dp", 1), in_keep.reshape(in_shape)[:, :, None],
-        in_got.reshape(in_shape)[:, :, None],
-    )
-    in_got = swap(in_give, "dp", 1)
 
     qkv_grads, grad_rel = attention_backward(
         line, projections, mixed, grad_mixed, lse, aug_q, aug_k, mirrored

time: 605 us -> 600 us (level)
    unnamed x101 -> x99, local copies, waits for them, and re-layouts: 24.6 us -> 24.5 us
  transfers between devices with their start and end apart: 43 -> 43, of which waited for: 18 -> 17; matrix products, arithmetic and copies ran while one was open for 6% -> 6% of each run, Pallas kernels for 42% -> 41%
where the time goes in v2:
time: 600 us; the launch traced here: 590 us
  Pallas kernels  308 us (51%)
  waiting for transfers between devices  140 us (23%)
  starting transfers between devices  66.9 us (11%)
  local copies, waits for them, and re-layouts  51.2 us (9%)
  between operations  14.7 us (2%)
  other arithmetic  7.73 us (1%)
    pallas_call x39, Pallas kernels, launch(): pl.pallas_call(body, out_shape=tuple(out_shape) + (jax.ShapeDtypeStruct((...  308 us
    ppermute x37, waiting for transfers between devices, swap(): return lax.ppermute(value, axis, [(i, i ^ bit) for i in range(count)])  129 us
    ppermute x37, starting transfers between devices, swap(): return lax.ppermute(value, axis, [(i, i ^ bit) for i in range(count)])  54.5 us
    unnamed x99, local copies, waits for them, and re-layouts  24.5 us
  transfers between devices with their start and end apart: 43, of which 17 were waited for; matrix products, arithmetic and copies ran while one was open for 6% of the time, Pallas kernels for 41%

profile of v2, /device:TPU:1, one launch (start us, length us, event | category | flops | bytes accessed | tf_op | source)
XLA Modules:
  0.0 589.7 jit_solution(17947501994438304408)
XLA Ops:
  16.7 4.7 find_slots.1
  26.5 5.7 all-to-all-done
  45.7 16.4 %collective-permute-done.1.refs_2_ = bf16[2,320,384]{2,1,0:T(8,128)(2,1)S(1)} collective-permute-done((bf16[2,320,384]{2,1,0:T(8,128)(2,1)}, bf16[2,320,384]{2,1,0:T(8,128)(2,1)S(1)}, u32[]{:S(2)}, u32[]{:S(2)}) %collective-permute-start.1) | collective-permute-done | bytes 491552 | tf_op jit(solution)/shard_map/ppermute | solution.py:1091
  67.9 5.9 %gather_fusion = bf16[512,768]{1,0:T(8,128)(2,1)S(1)} fusion(bf16[4016,768]{1,0:T(8,128)(2,1)} %param.22, s32[1024]{0:T(1024)S(1)} %pad_clamp_fusion), kind=kCustom, calls=%fused_computation | custom fusion | bytes 1574912 | tf_op jit(solution)/shard_map/jit(_take)/gather | solution.py:1230
  76.5 12.2 %collective-permute-done.3.refs_2_ = bf16[4,320,384]{2,1,0:T(8,128)(2,1)S(1)} collective-permute-done((bf16[4,320,384]{2,1,0:T(8,128)(2,1)}, bf16[4,320,384]{2,1,0:T(8,128)(2,1)S(1)}, u32[]{:S(2)}, u32[]{:S(2)}) %collective-permute-start.3) | collective-permute-done | bytes 983072 | tf_op jit(solution)/shard_map/ppermute | solution.py:1091
  92.5 6.8 %pack.1 = (bf16[2048,768]{1,0:T(8,128)(2,1)}, bf16[96,768]{1,0:T(8,128)(2,1)}, f32[8,128]{1,0:T(8,128)}) custom-call(s32[2048,8]{1,0:T(8,128)} %get-tuple-element.137.refs_0_, bf16[512,768]{1,0:T(8,128)(2,1)} %refs_1_.1, bf16[512,768]{1,0:T(8,128)(2,1)} %broadcast_select_fusion.refs_2_, bf16[96,768]{1,0:T(8,128)(2,1)} %dynamic-slice_bitcast_fusion.refs_3_, ...), custom_call_target="tpu_custom_call" | custom-call | flops 1 | bytes 1 | tf_op jit(solution)/shard_map/pack/pallas_call | solution.py:37
  99.2 4.9 all-to-all-start.1
  109.1 29.5 %collective-permute-done.6.refs_3_ = bf16[768,768]{1,0:T(8,128)(2,1)S(1)} collective-permute-done((bf16[768,768]{1,0:T(8,128)(2,1)}, bf16[768,768]{1,0:T(8,128)(2,1)S(1)}, u32[]{:S(2)}, u32[]{:S(2)}) %collective-permute-start.6) | collective-permute-done | bytes 1179680 | tf_op jit(solution)/shard_map/ppermute | solution.py:1091
  138.6 5.0 collective-permute-start.7
  143.6 8.1 %layout_lookup.2 = (f32[1024,384]{1,0:T(8,128)}, f32[1024,384]{1,0:T(8,128)}, f32[8,128]{1,0:T(8,128)}) custom-call(s32[1]{0:T(128)} %bitcast.18.refs_0_, s32[1024,8]{1,0:T(8,128)} %get-tuple-element.136.refs_1_, s32[1024,8]{1,0:T(8,128)} %copy.47.refs_4_.refs_2_, bf16[8,256,384]{2,1,0:T(8,128)(2,1)} %bitcast.98, f32[8,128]{1,0:T(8,128)} %get-tuple-element.147.refs_4_), custom_call_target="tpu_custom_call" | custom-call | flops 1 | bytes 1 | tf_op jit(solution)/shard_map/layout_lookup/pallas_call | solution.py:37
  152.8 5.0 arrange.1
  157.8 15.1 %collective-permute-done.4.refs_3_ = bf16[8,256,384]{2,1,0:T(8,128)(2,1)S(1)} collective-permute-done((bf16[8,256,384]{2,1,0:T(8,128)(2,1)}, bf16[8,256,384]{2,1,0:T(8,128)(2,1)S(1)}, u32[]{:S(2)}, u32[]{:S(2)}) %collective-permute-start.4) | collective-permute-done | bytes 1572896 | tf_op jit(solution)/shard_map/ppermute | solution.py:1091
  174.1 8.6 %layout_lookup.3 = (f32[1024,384]{1,0:T(8,128)}, f32[1024,384]{1,0:T(8,128)}, f32[8,128]{1,0:T(8,128)}) custom-call(s32[1]{0:T(128)S(6)} %sub.42.refs_0_, s32[1024,8]{1,0:T(8,128)} %get-tuple-element.136.refs_1_, s32[1024,8]{1,0:T(8,128)} %copy.47.refs_4_.refs_2_, bf16[8,256,384]{2,1,0:T(8,128)(2,1)} %copy-done.7, f32[1024,384]{1,0:T(8,128)} %get-tuple-element.148.refs_4_, ...), custom_call_target="tpu_custom_call" | custom-call | flops 1 | bytes 1 | tf_op jit(solution)/shard_map/layout_lookup/pallas_call | solution.py:37
  190.8 17.0 %embed.1 = (bf16[768,1024]{1,0:T(8,128)(2,1)}, bf16[1024,768]{1,0:T(8,128)(2,1)}, bf16[768,1024]{1,0:T(8,128)(2,1)}, bf16[3,1024,768]{2,1,0:T(8,128)(2,1)}, f32[8,128]{1,0:T(8,128)}) custom-call(s32[8,2048]{1,0:T(8,128)} %get-tuple-element.135.refs_0_, s32[1024,8]{1,0:T(8,128)} %get-tuple-element.136.refs_1_, bf16[2048,768]{1,0:T(8,128)(2,1)} %bitcast.88, ...), custom_call_target="tpu_custom_call" | custom-call | flops 1 | bytes 1 | tf_op jit(solution)/shard_map/embed/pallas_call | solution.py:37
  215.2 28.7 %attention_forward.1 = (bf16[1024,768]{1,0:T(8,128)(2,1)}, f32[1024,768]{1,0:T(8,128)}, f32[8,128]{1,0:T(8,128)}) custom-call(bf16[3,1024,768]{2,1,0:T(8,128)(2,1)} %get-tuple-element.158.refs_0_.refs_1_.refs_2_, bf16[3,1024,768]{2,1,0:T(8,128)(2,1)} %get-tuple-element.158.refs_0_.refs_1_.refs_2_, ...), custom_call_target="tpu_custom_call" | custom-call | flops 1 | bytes 1 | tf_op jit(solution)/shard_map/attention_forward/pallas_call | solution.py:37
  244.8 34.7 %feed_forward.1 = (bf16[1024,768]{1,0:T(8,128)(2,1)}, bf16[3072,1024]{1,0:T(8,128)(2,1)}, bf16[1024,3072]{1,0:T(8,128)(2,1)}, bf16[768,1024]{1,0:T(8,128)(2,1)},...) custom-call(s32[1]{0:T(128)} %bitcast.refs_0_, ...), custom_call_target="tpu_custom_call" | custom-call | flops 1 | bytes 1 | tf_op jit(solution)/shard_map/feed_forward/pallas_call | solution.py:37
  279.4 9.8 %contract_quarters.1 = (bf16[2,8,2,96,384]{4,3,2,1,0:T(8,128)(2,1)}, bf16[2,8,2,96,384]{4,3,2,1,0:T(8,128)(2,1)}, f32[8,128]{1,0:T(8,128)}) custom-call(s32[1]{0:T(128)} %bitcast.refs_0_, bf16[768,1024]{1,0:T(8,128)(2,1)} %get-tuple-element.171.refs_1_, bf16[1024,3072]{1,0:T(8,128)(2,1)} %get-tuple-element.172.refs_2_, f32[8,128]{1,0:T(8,128)} %get-tuple-element.173.refs_3_), custom_call_target="tpu_custom_call" | custom-call | flops 1 | bytes 1 | tf_op jit(solution)/shard_map/contract_quarters/pallas_call | solution.py:37
  289.2 9.0 %contract_halves.2 = (bf16[3072,384]{1,0:T(8,128)(2,1)}, bf16[3072,384]{1,0:T(8,128)(2,1)}, f32[8,128]{1,0:T(8,128)}) custom-call(s32[1]{0:T(128)} %bitcast.refs_0_, bf16[3072,1024]{1,0:T(8,128)(2,1)} %get-tuple-element.170.refs_1_, bf16[1024,768]{1,0:T(8,128)(2,1)} %refs_2_.1, f32[8,128]{1,0:T(8,128)} %get-tuple-element.174.refs_3_), custom_call_target="tpu_custom_call" | custom-call | flops 1 | bytes 1 | tf_op jit(solution)/shard_map/contract_halves/pallas_call | solution.py:37
  310.5 5.4 rows_fold.3
  319.6 36.6 %attention_backward.1 = (bf16[3,1024,768]{2,1,0:T(8,128)(2,1)}, f32[12,8,512]{2,1,0:T(8,128)}, f32[8,128]{1,0:T(8,128)}) custom-call(bf16[3,1024,768]{2,1,0:T(8,128)(2,1)} %get-tuple-element.158.refs_0_.refs_1_.refs_2_, bf16[3,1024,768]{2,1,0:T(8,128)(2,1)} %get-tuple-element.158.refs_0_.refs_1_.refs_2_, ...), custom_call_target="tpu_custom_call" | custom-call | flops 1 | bytes 1 | tf_op jit(solution)/shard_map/attention_backward/pallas_call | solution.py:37
  369.0 9.9 %input_grad.1 = (bf16[1024,768]{1,0:T(8,128)(2,1)}, bf16[1024,384]{1,0:T(8,128)(2,1)}, bf16[1024,384]{1,0:T(8,128)(2,1)}, f32[8,768]{1,0:T(8,128)}, f32[8,128]{1,0:T(8,128)}) custom-call(s32[1]{0:T(128)} %bitcast.refs_0_, bf16[1024,768]{1,0:T(8,128)(2,1)} %get-tuple-element.157.refs_1_, f32[1024,768]{1,0:T(8,128)} %get-tuple-element.167.refs_2_, ...), custom_call_target="tpu_custom_call" | custom-call | flops 1 | bytes 1 | tf_op jit(solution)/shard_map/input_grad/pallas_call | solution.py:37
  386.7 7.0 %return_rows.1 = (bf16[8,272,768]{2,1,0:T(8,128)(2,1)}, f32[8,128]{1,0:T(8,128)}) custom-call(s32[2048,1]{1,0:T(8,128)} %copy.53.refs_0_, bf16[1024,768]{1,0:T(8,128)(2,1)} %get-tuple-element.195.refs_1_.refs_4_, f32[8,768]{1,0:T(8,128)} %pad.27.refs_2_, f32[8,128]{1,0:T(8,128)} %get-tuple-element.204.refs_3_), custom_call_target="tpu_custom_call" | custom-call | flops 1 | bytes 1 | tf_op jit(solution)/shard_map/return_rows/pallas_call | solution.py:37
  402.9 13.0 %layout_grad.1 = (bf16[8,2,128,384]{3,2,1,0:T(8,128)(2,1)}, bf16[8,2,128,384]{3,2,1,0:T(8,128)(2,1)}, f32[8,128]{1,0:T(8,128)}) custom-call(s32[1]{0:T(128)} %bitcast.18.refs_0_, s32[8,1024]{1,0:T(8,128)} %get-tuple-element.210.refs_1_, s32[8,1024]{1,0:T(8,128)} %bitcast.141, bf16[1024,384]{1,0:T(8,128)(2,1)} %get-tuple-element.211.refs_3_, ...), custom_call_target="tpu_custom_call" | custom-call | flops 1 | bytes 1 | tf_op jit(solution)/shard_map/layout_grad/pallas_call | solution.py:37
  415.9 10.1 %square_grads.1 = (bf16[8,2,2,96,384]{4,3,2,1,0:T(8,128)(2,1)}, bf16[8,2,2,96,384]{4,3,2,1,0:T(8,128)(2,1)}, f32[8,128]{1,0:T(8,128)}) custom-call(s32[1]{0:T(128)} %bitcast.refs_0_, bf16[768,1024]{1,0:T(8,128)(2,1)} %get-tuple-element.208.refs_1_, bf16[3,1024,768]{2,1,0:T(8,128)(2,1)} %get-tuple-element.187.refs_3_.refs_2_, ...), custom_call_target="tpu_custom_call" | custom-call | flops 1 | bytes 1 | tf_op jit(solution)/shard_map/square_grads/pallas_call | solution.py:37
  432.2 4.3 fold.11
  438.4 24.1 %collective-permute-done.22 = bf16[8,2,128,384]{3,2,1,0:T(8,128)(2,1)} collective-permute-done((bf16[8,2,128,384]{3,2,1,0:T(8,128)(2,1)}, bf16[8,2,128,384]{3,2,1,0:T(8,128)(2,1)}, u32[]{:S(2)}, u32[]{:S(2)}) %collective-permute-start.22) | collective-permute-done | bytes 1572896 | tf_op jit(solution)/shard_map/ppermute | solution.py:1091
  465.9 4.3 all-to-all-done.2.refs_1_
  472.0 6.4 %unpack_text.1 = (bf16[544,768]{1,0:T(8,128)(2,1)}, f32[8,128]{1,0:T(8,128)}) custom-call(s32[8,272]{1,0:T(8,128)} %pad.28.refs_0_, bf16[8,272,768]{2,1,0:T(8,128)(2,1)} %copy-done.2, s32[8,512]{1,0:T(8,128)} %get-tuple-element.138.refs_2_, f32[8,128]{1,0:T(8,128)} %get-tuple-element.223.refs_3_), custom_call_target="tpu_custom_call" | custom-call | flops 1 | bytes 1 | tf_op jit(solution)/shard_map/unpack_text/pallas_call | solution.py:37
  482.4 5.4 collective-permute-done.21
  494.2 11.5 %collective-permute-done.27.refs_1_ = bf16[544,768]{1,0:T(8,128)(2,1)S(1)} collective-permute-done((bf16[544,768]{1,0:T(8,128)(2,1)}, bf16[544,768]{1,0:T(8,128)(2,1)S(1)}, u32[]{:S(2)}, u32[]{:S(2)}) %collective-permute-start.27) | collective-permute-done | bytes 835616 | tf_op jit(solution)/shard_map/ppermute | solution.py:1091
  522.0 17.6 %text_grads.1 = (f32[4016,768]{1,0:T(8,128)}, f32[8,128]{1,0:T(8,128)}) custom-call(bf16[544,768]{1,0:T(8,128)(2,1)} %get-tuple-element.235.refs_0_, bf16[544,768]{1,0:T(8,128)(2,1)} %copy-done.14, bf16[544,768]{1,0:T(8,128)(2,1)} %collective-permute-done.28.refs_2_, bf16[544,768]{1,0:T(8,128)(2,1)} %copy-done.15, f32[8,128]{1,0:T(8,128)} %get-tuple-element.236.refs_4_), custom_call_target="tpu_custom_call" | custom-call | flops 1 | bytes 1 | tf_op jit(solution)/shard_map/text_grads/pallas_call | solution.py:37
  549.3 8.4 %patch_grads.1 = (f32[512,768]{1,0:T(8,128)}, f32[8,128]{1,0:T(8,128)}) custom-call(s32[8,272]{1,0:T(8,128)} %pad.25.refs_0_, bf16[8,272,768]{2,1,0:T(8,128)(2,1)} %copy-done.2, bf16[4,768,768]{2,1,0:T(8,128)(2,1)} %get-tuple-element.154.refs_6_.refs_8_.refs_4_.refs_2_, f32[8,128]{1,0:T(8,128)} %get-tuple-element.239.refs_3_), custom_call_target="tpu_custom_call" | custom-call | flops 1 | bytes 1 | tf_op jit(solution)/shard_map/patch_grads/pallas_call | solution.py:37
  (258 shorter events, 183.5 us)
Async XLA Ops:
  7.2 97.0 %all-gather.8.cloned.1.call-start = ((), (), s32[]{:S(2)}) async-start(), calls=%async_computation.4 | async-start | bytes 1327104 | tf_op jit(solution)/shard_map/all_gather | solution.py:1208
  9.0 235.0 %all-gather.10.cloned.1.call-start = ((), (), s32[]{:S(2)}) async-start(), calls=%async_computation.5 | async-start | bytes 4866048 | tf_op jit(solution)/shard_map/all_gather | solution.py:1212
  12.9 24.1 %collective-permute-start = (bf16[1,320,384]{2,1,0:T(8,128)(2,1)S(1)}, bf16[1,320,384]{2,1,0:T(8,128)(2,1)S(1)}, u32[]{:S(2)}, u32[]{:S(2)}) collective-permute-start(bf16[1,320,384]{2,1,0:T(8,128)(2,1)S(1)} %fusion.4.refs_1_), channel_id=1, source_target_pairs={{0,16},{4,20},{8,24},{12,28},{16,0},{20,4},{24,8},{28,12},{1,17},{... | collective-permute-start | bytes 737288 | tf_op jit(solution)/shard_map/ppermute | solution.py:1091
  26.5 217.5 %all-gather.6.cloned.1.call-start = ((), (), s32[]{:S(2)}) async-start(), calls=%async_computation.3 | async-start | bytes 4866048 | tf_op jit(solution)/shard_map/all_gather | solution.py:1235
  39.7 22.4 %collective-permute-start.1 = (bf16[2,320,384]{2,1,0:T(8,128)(2,1)}, bf16[2,320,384]{2,1,0:T(8,128)(2,1)S(1)}, u32[]{:S(2)}, u32[]{:S(2)}) collective-permute-start(bf16[2,320,384]{2,1,0:T(8,128)(2,1)} %bitcast.129), channel_id=1, source_target_pairs={{0,8},{4,12},{8,0},{12,4},{16,24},{20,28},{24,16},{28,20},{1,9},{5... | collective-permute-start | bytes 1474568 | tf_op jit(solution)/shard_map/ppermute | solution.py:1091
  65.0 23.7 %collective-permute-start.3 = (bf16[4,320,384]{2,1,0:T(8,128)(2,1)}, bf16[4,320,384]{2,1,0:T(8,128)(2,1)S(1)}, u32[]{:S(2)}, u32[]{:S(2)}) collective-permute-start(bf16[4,320,384]{2,1,0:T(8,128)(2,1)} %bitcast.110), channel_id=1, source_target_pairs={{0,4},{4,0},{8,12},{12,8},{16,20},{20,16},{24,28},{28,24},{1,5},{5... | collective-permute-start | bytes 2949128 | tf_op jit(solution)/shard_map/ppermute | solution.py:1091
  99.2 89.9 %all-to-all-start.1 = ((bf16[8,256,768]{2,1,0:T(8,128)(2,1)}), bf16[8,256,768]{2,1,0:T(8,128)(2,1)S(1)}, u32[]{:S(2)}, u32[]{:S(2)}) async-start(bf16[8,256,768]{2,1,0:T(8,128)(2,1)} %bitcast.90), calls=%async_computation.1 | async-start | bytes 6291456 | tf_op jit(solution)/shard_map/all_to_all | solution.py:1232
  104.2 34.4 %collective-permute-start.6 = (bf16[768,768]{1,0:T(8,128)(2,1)}, bf16[768,768]{1,0:T(8,128)(2,1)S(1)}, u32[]{:S(2)}, u32[]{:S(2)}) collective-permute-start(bf16[768,768]{1,0:T(8,128)(2,1)} %bitcast.105), channel_id=1, source_target_pairs={{0,2},{1,3},{2,0},{3,1},{4,6},{5,7},{6,4},{7,5},{8,10},{9,11},{10,... | collective-permute-start | bytes 3538952 | tf_op jit(solution)/shard_map/ppermute | solution.py:1091
  105.4 67.5 %collective-permute-start.4 = (bf16[8,256,384]{2,1,0:T(8,128)(2,1)}, bf16[8,256,384]{2,1,0:T(8,128)(2,1)S(1)}, u32[]{:S(2)}, u32[]{:S(2)}) collective-permute-start(bf16[8,256,384]{2,1,0:T(8,128)(2,1)} %bitcast.97), channel_id=1, source_target_pairs={{0,2},{1,3},{2,0},{3,1},{4,6},{5,7},{6,4},{7,5},{8,10},{9,11},{10,... | collective-permute-start | bytes 4718600 | tf_op jit(solution)/shard_map/ppermute | solution.py:1091
  105.7 46.1 %collective-permute-start.5 = (bf16[768,768]{1,0:T(8,128)(2,1)}, bf16[768,768]{1,0:T(8,128)(2,1)S(1)}, u32[]{:S(2)}, u32[]{:S(2)}) collective-permute-start(bf16[768,768]{1,0:T(8,128)(2,1)} %bitcast.106), channel_id=1, source_target_pairs={{0,1},{1,0},{2,3},{3,2},{4,5},{5,4},{6,7},{7,6},{8,9},{9,8},{10,11... | collective-permute-start | bytes 3538952 | tf_op jit(solution)/shard_map/ppermute | solution.py:1091
  138.6 13.2 %collective-permute-start.7 = (bf16[768,768]{1,0:T(8,128)(2,1)S(1)}, bf16[768,768]{1,0:T(8,128)(2,1)}, u32[]{:S(2)}, u32[]{:S(2)}) collective-permute-start(bf16[768,768]{1,0:T(8,128)(2,1)S(1)} %collective-permute-done.6.refs_3_), channel_id=1, source_target_pairs={{0,1},{1,0},{2,3},{3,2},{4,5},{5,4},{6,7},{7,6},{8,9},{9,8},{10,11... | collective-permute-start | bytes 3538952 | tf_op jit(solution)/shard_map/ppermute | solution.py:1091
  185.7 22.1 %collective-permute-start.9 = (bf16[8,48,384]{2,1,0:T(8,128)(2,1)S(1)}, bf16[8,48,384]{2,1,0:T(8,128)(2,1)}, u32[]{:S(2)}, u32[]{:S(2)}) collective-permute-start(bf16[8,48,384]{2,1,0:T(8,128)(2,1)S(1)} %bitcast.136), channel_id=1, source_target_pairs={{0,2},{1,3},{2,0},{3,1},{4,6},{5,7},{6,4},{7,5},{8,10},{9,11},{10,... | collective-permute-start | bytes 884744 | tf_op jit(solution)/shard_map/ppermute | solution.py:1091
  209.8 34.2 %collective-permute-start.10 = (bf16[768,384]{1,0:T(8,128)(2,1)}, bf16[768,384]{1,0:T(8,128)(2,1)S(1)}, u32[]{:S(2)}, u32[]{:S(2)}) collective-permute-start(bf16[768,384]{1,0:T(8,128)(2,1)} %bitcast.121), channel_id=1, source_target_pairs={{0,1},{1,0},{2,3},{3,2},{4,5},{5,4},{6,7},{7,6},{8,9},{9,8},{10,11... | collective-permute-start | bytes 1769480 | tf_op jit(solution)/shard_map/ppermute | solution.py:1091
  289.2 14.0 %collective-permute-start.13 = (bf16[2,8,2,96,384]{4,3,2,1,0:T(8,128)(2,1)}, bf16[2,8,2,96,384]{4,3,2,1,0:T(8,128)(2,1)S(1)}, u32[]{:S(2)}, u32[]{:S(2)}) collective-permute-start(bf16[2,8,2,96,384]{4,3,2,1,0:T(8,128)(2,1)} %get-tuple-element.183), channel_id=1, source_target_pairs={{0,1},{1,0},{2,3},{3,2},{4,5},{5,4},{6,7},{7,6},{8,9},{9,8},{10,11... | collective-permute-start | bytes 7077896 | tf_op jit(solution)/shard_map/ppermute | solution.py:1091
  315.9 40.3 %collective-permute-start.15 = (bf16[8,240,384]{2,1,0:T(8,128)(2,1)}, bf16[8,240,384]{2,1,0:T(8,128)(2,1)S(1)}, u32[]{:S(2)}, u32[]{:S(2)}) collective-permute-start(bf16[8,240,384]{2,1,0:T(8,128)(2,1)} %get-tuple-element.191), channel_id=1, source_target_pairs={{0,2},{1,3},{2,0},{3,1},{4,6},{5,7},{6,4},{7,5},{8,10},{9,11},{10,... | collective-permute-start | bytes 4423688 | tf_op jit(solution)/shard_map/ppermute | solution.py:1091
  317.6 43.0 %collective-permute-start.14 = (bf16[8,1,192,384]{3,2,1,0:T(8,128)(2,1)}, bf16[8,1,192,384]{3,2,1,0:T(8,128)(2,1)S(1)}, u32[]{:S(2)}, u32[]{:S(2)}) collective-permute-start(bf16[8,1,192,384]{3,2,1,0:T(8,128)(2,1)} %get-tuple-element.189), channel_id=1, source_target_pairs={{0,4},{4,0},{8,12},{12,8},{16,20},{20,16},{24,28},{28,24},{1,5},{5... | collective-permute-start | bytes 3538952 | tf_op jit(solution)/shard_map/ppermute | solution.py:1091
  364.6 15.7 %collective-permute-start.17 = (bf16[1,4,192,384]{3,2,1,0:T(8,128)(2,1)}, bf16[1,4,192,384]{3,2,1,0:T(8,128)(2,1)S(1)}, u32[]{:S(2)}, u32[]{:S(2)}) collective-permute-start(bf16[1,4,192,384]{3,2,1,0:T(8,128)(2,1)} %get-tuple-element.202), channel_id=1, source_target_pairs={{0,2},{1,3},{2,0},{3,1},{4,6},{5,7},{6,4},{7,5},{8,10},{9,11},{10,... | collective-permute-start | bytes 1769480 | tf_op jit(solution)/shard_map/ppermute | solution.py:1091
  364.8 16.9 %collective-permute-start.16 = (bf16[4,1,240,384]{3,2,1,0:T(8,128)(2,1)}, bf16[4,1,240,384]{3,2,1,0:T(8,128)(2,1)S(1)}, u32[]{:S(2)}, u32[]{:S(2)}) collective-permute-start(bf16[4,1,240,384]{3,2,1,0:T(8,128)(2,1)} %get-tuple-element.200), channel_id=1, source_target_pairs={{0,4},{4,0},{8,12},{12,8},{16,20},{20,16},{24,28},{28,24},{1,5},{5... | collective-permute-start | bytes 2211848 | tf_op jit(solution)/shard_map/ppermute | solution.py:1091
  393.7 76.5 %all-to-all-start.2 = ((bf16[8,272,768]{2,1,0:T(8,128)(2,1)}), bf16[8,272,768]{2,1,0:T(8,128)(2,1)S(1)}, u32[]{:S(2)}, u32[]{:S(2)}) async-start(bf16[8,272,768]{2,1,0:T(8,128)(2,1)} %get-tuple-element.205), calls=%async_computation.2 | async-start | bytes 6684672 | tf_op jit(solution)/shard_map/all_to_all | solution.py:1311
  426.4 36.2 %collective-permute-start.22 = (bf16[8,2,128,384]{3,2,1,0:T(8,128)(2,1)}, bf16[8,2,128,384]{3,2,1,0:T(8,128)(2,1)}, u32[]{:S(2)}, u32[]{:S(2)}) collective-permute-start(bf16[8,2,128,384]{3,2,1,0:T(8,128)(2,1)} %get-tuple-element.221), channel_id=1, source_target_pairs={{0,2},{1,3},{2,0},{3,1},{4,6},{5,7},{6,4},{7,5},{8,10},{9,11},{10,... | collective-permute-start | bytes 4718600 | tf_op jit(solution)/shard_map/ppermute | solution.py:1091
  436.5 51.4 %collective-permute-start.21 = (bf16[8,1,192,384]{3,2,1,0:T(8,128)(2,1)}, bf16[8,1,192,384]{3,2,1,0:T(8,128)(2,1)}, u32[]{:S(2)}, u32[]{:S(2)}) collective-permute-start(bf16[8,1,192,384]{3,2,1,0:T(8,128)(2,1)} %get-tuple-element.219), channel_id=1, source_target_pairs={{0,2},{1,3},{2,0},{3,1},{4,6},{5,7},{6,4},{7,5},{8,10},{9,11},{10,... | collective-permute-start | bytes 3538952 | tf_op jit(solution)/shard_map/ppermute | solution.py:1091
  478.3 27.3 %collective-permute-start.27 = (bf16[544,768]{1,0:T(8,128)(2,1)}, bf16[544,768]{1,0:T(8,128)(2,1)S(1)}, u32[]{:S(2)}, u32[]{:S(2)}) collective-permute-start(bf16[544,768]{1,0:T(8,128)(2,1)} %get-tuple-element.235.refs_0_), channel_id=1, source_target_pairs={{0,2},{1,3},{2,0},{3,1},{4,6},{5,7},{6,4},{7,5},{8,10},{9,11},{10,... | collective-permute-start | bytes 2506760 | tf_op jit(solution)/shard_map/ppermute | solution.py:1091
  479.6 30.2 %collective-permute-start.24 = (bf16[4,1,256,384]{3,2,1,0:T(8,128)(2,1)S(1)}, bf16[4,1,256,384]{3,2,1,0:T(8,128)(2,1)S(1)}, u32[]{:S(2)}, u32[]{:S(2)}) collective-permute-start(bf16[4,1,256,384]{3,2,1,0:T(8,128)(2,1)S(1)} %copy-done.43), channel_id=1, source_target_pairs={{0,4},{4,0},{8,12},{12,8},{16,20},{20,16},{24,28},{28,24},{1,5},{5... | collective-permute-start | bytes 2359304 | tf_op jit(solution)/shard_map/ppermute | solution.py:1091
  482.4 24.2 %collective-permute-start.18 = (bf16[2,432,384]{2,1,0:T(8,128)(2,1)S(1)}, bf16[2,432,384]{2,1,0:T(8,128)(2,1)S(1)}, u32[]{:S(2)}, u32[]{:S(2)}) collective-permute-start(bf16[2,432,384]{2,1,0:T(8,128)(2,1)S(1)} %copy-done.44), channel_id=1, source_target_pairs={{0,8},{4,12},{8,0},{12,4},{16,24},{20,28},{24,16},{28,20},{1,9},{5... | collective-permute-start | bytes 1990664 | tf_op jit(solution)/shard_map/ppermute | solution.py:1091
  490.7 19.8 %collective-permute-start.25 = (bf16[4,1,192,384]{3,2,1,0:T(8,128)(2,1)}, bf16[4,1,192,384]{3,2,1,0:T(8,128)(2,1)S(1)}, u32[]{:S(2)}, u32[]{:S(2)}) collective-permute-start(bf16[4,1,192,384]{3,2,1,0:T(8,128)(2,1)} %get-tuple-element.231), channel_id=1, source_target_pairs={{0,4},{4,0},{8,12},{12,8},{16,20},{20,16},{24,28},{28,24},{1,5},{5... | collective-permute-start | bytes 1769480 | tf_op jit(solution)/shard_map/ppermute | solution.py:1091
  492.4 28.7 %collective-permute-start.28 = (bf16[544,768]{1,0:T(8,128)(2,1)S(1)}, bf16[544,768]{1,0:T(8,128)(2,1)}, u32[]{:S(2)}, u32[]{:S(2)}) collective-permute-start(bf16[544,768]{1,0:T(8,128)(2,1)S(1)} %copy-done.16), channel_id=1, source_target_pairs={{0,1},{1,0},{2,3},{3,2},{4,5},{5,4},{6,7},{7,6},{8,9},{9,8},{10,11... | collective-permute-start | bytes 2506760 | tf_op jit(solution)/shard_map/ppermute | solution.py:1091
  505.6 15.5 %collective-permute-start.29 = (bf16[544,768]{1,0:T(8,128)(2,1)S(1)}, bf16[544,768]{1,0:T(8,128)(2,1)S(1)}, u32[]{:S(2)}, u32[]{:S(2)}) collective-permute-start(bf16[544,768]{1,0:T(8,128)(2,1)S(1)} %collective-permute-done.27.refs_1_), channel_id=1, source_target_pairs={{0,1},{1,0},{2,3},{3,2},{4,5},{5,4},{6,7},{7,6},{8,9},{9,8},{10,11... | collective-permute-start | bytes 2506760 | tf_op jit(solution)/shard_map/ppermute | solution.py:1091
  515.5 24.1 %collective-permute-start.26 = (bf16[2,448,384]{2,1,0:T(8,128)(2,1)}, bf16[2,448,384]{2,1,0:T(8,128)(2,1)S(1)}, u32[]{:S(2)}, u32[]{:S(2)}) collective-permute-start(bf16[2,448,384]{2,1,0:T(8,128)(2,1)} %get-tuple-element.234), channel_id=1, source_target_pairs={{0,8},{4,12},{8,0},{12,4},{16,24},{20,28},{24,16},{28,20},{1,9},{5... | collective-permute-start | bytes 2064392 | tf_op jit(solution)/shard_map/ppermute | solution.py:1091
  518.1 28.4 %collective-permute-start.23 = (bf16[1,1,432,384]{3,2,1,0:T(8,128)(2,1)}, bf16[1,1,432,384]{3,2,1,0:T(8,128)(2,1)S(1)}, u32[]{:S(2)}, u32[]{:S(2)}) collective-permute-start(bf16[1,1,432,384]{3,2,1,0:T(8,128)(2,1)} %get-tuple-element.227), channel_id=1, source_target_pairs={{0,16},{4,20},{8,24},{12,28},{16,0},{20,4},{24,8},{28,12},{1,17},{... | collective-permute-start | bytes 995336 | tf_op jit(solution)/shard_map/ppermute | solution.py:1091
  543.0 17.2 %collective-permute-start.30 = (bf16[1,1,448,384]{3,2,1,0:T(8,128)(2,1)}, bf16[1,1,448,384]{3,2,1,0:T(8,128)(2,1)S(1)}, u32[]{:S(2)}, u32[]{:S(2)}) collective-permute-start(bf16[1,1,448,384]{3,2,1,0:T(8,128)(2,1)} %get-tuple-element.243), channel_id=1, source_target_pairs={{0,16},{4,20},{8,24},{12,28},{16,0},{20,4},{24,8},{28,12},{1,17},{... | collective-permute-start | bytes 1032200 | tf_op jit(solution)/shard_map/ppermute | solution.py:1091
  549.0 17.8 %collective-permute-start.35 = (bf16[432,384]{1,0:T(8,128)(2,1)}, bf16[432,384]{1,0:T(8,128)(2,1)S(1)}, u32[]{:S(2)}, u32[]{:S(2)}) collective-permute-start(bf16[432,384]{1,0:T(8,128)(2,1)} %get-tuple-element.246.refs_1_), channel_id=1, source_target_pairs={{0,2},{1,3},{2,0},{3,1},{4,6},{5,7},{6,4},{7,5},{8,10},{9,11},{10,... | collective-permute-start | bytes 995336 | tf_op jit(solution)/shard_map/ppermute | solution.py:1091
  566.9 12.0 %collective-permute-start.31 = (bf16[448,384]{1,0:T(8,128)(2,1)}, bf16[448,384]{1,0:T(8,128)(2,1)S(1)}, u32[]{:S(2)}, u32[]{:S(2)}) collective-permute-start(bf16[448,384]{1,0:T(8,128)(2,1)} %get-tuple-element.245.refs_1_), channel_id=1, source_target_pairs={{0,1},{1,0},{2,3},{3,2},{4,5},{5,4},{6,7},{7,6},{8,9},{9,8},{10,11... | collective-permute-start | bytes 1032200 | tf_op jit(solution)/shard_map/ppermute | solution.py:1091
  (57 other events, 345.3 us)
Sparse Core Ops, SparseCore 0:
  10.8 45.8 all-gather.7
  59.5 86.8 all-gather.9
  149.3 83.6 all-gather.5

commit v3 on v2

--- a/solution.py
+++ b/solution.py
@@ -161,6 +161,16 @@
         out_ref[rows, :] = jnp.where(left, outs[0], outs[1]).astype(jnp.bfloat16)
         lse_ref[rows, :] = jnp.where(left, lses[0], lses[1])
 
+def put_blocks(ref, slot, first, value, held):
+    for n in range(value.shape[1] // BLK):
+        cut = slice((first + n) * BLK, (first + n) * BLK + BLK)
+        part = value[:, n * BLK : n * BLK + BLK]
+        if first + n in held:
+            ref[slot, :, cut] += part
+        else:
+            ref[slot, :, cut] = part
+
+
 def backward_kernel(
     q_ref, k_ref, v_ref, mixed_ref, grad_ref, lse_ref, aug_q, aug_k, table,
     grads_ref, rel_ref,
@@ -171,8 +181,7 @@
     middle = (count - 1) * BLK
     lane = lax.broadcasted_iota(jnp.int32, (1, 128), 1)
     left = lane < 64
-    rel[...] = jnp.zeros_like(rel)
-    dq_acc[...] = jnp.zeros_like(dq_acc)
+    rel_blocks, dq_blocks = set(), set()
     inner = mixed_ref[...].astype(jnp.float32) * grad_ref[...].astype(jnp.float32)
     query = q_ref[...] * jnp.bfloat16(0.125)
     for h in range(2):
@@ -196,12 +205,14 @@
             s = dot_nt(ka[h, keys, :], qa[h, rows, :]) + strip[h, :, cut]
             p = jnp.exp(s)
             ds = p * dot_nt(va[h, keys, :], ga[h, rows, :])
-            rel[h, :, cut] += ds
+            put_blocks(rel, h, offset // BLK + low, ds, rel_blocks)
             p = p.astype(jnp.bfloat16)
             ds = ds.astype(jnp.bfloat16)
             dvs.append(dot_nn(p, ga[h, rows, :]))
             dks.append(dot_nn(ds, qa[h, rows, :]))
-            dq_acc[h, :, rows] += dot_tn(ka[h, keys, :], ds)
+            put_blocks(dq_acc, h, low, dot_tn(ka[h, keys, :], ds), dq_blocks)
+        rel_blocks.update(range(offset // BLK + low, offset // BLK + high))
+        dq_blocks.update(range(low, high))
         grads_ref[1, keys, :] = jnp.where(left, dks[0], dks[1]).astype(jnp.bfloat16)
         grads_ref[2, keys, :] = jnp.where(left, dvs[0], dvs[1]).astype(jnp.bfloat16)
     row = lax.broadcasted_iota(jnp.int32, (128, 1), 0)
@@ -211,13 +222,13 @@
         out = []
         for place in range(5):
             start = middle + (2 - place) * BLK
-            if place == 0:
-                far = rel[h, :, middle + 2 * BLK :]
-                summed = jnp.sum(jnp.sum(far, axis=0, keepdims=True).reshape(-1, BLK), axis=0, keepdims=True)
-                out.append(jnp.concatenate([summed, jnp.zeros_like(summed)], axis=1))
-            elif place == 4:
-                far = rel[h, :, : middle - BLK]
-                summed = jnp.sum(jnp.sum(far, axis=0, keepdims=True).reshape(-1, BLK), axis=0, keepdims=True)
+            if place in (0, 4):
+                near = middle // BLK
+                summed = jnp.zeros((1, BLK), jnp.float32)
+                for block in sorted(rel_blocks):
+                    if (block >= near + 2) if place == 0 else (block <= near - 2):
+                        part = rel[h, :, block * BLK : block * BLK + BLK]
+                        summed = summed + jnp.sum(part, axis=0, keepdims=True)
                 out.append(jnp.concatenate([summed, jnp.zeros_like(summed)], axis=1))
             else:
                 out.append(diagonal_sums(rel[h, :, start : start + BLK]))

time: 600 us -> 600 us (level)
  no operation moved by 1% of the time
where the time goes in v3:
time: 600 us; the launch traced here: 590 us
  Pallas kernels  308 us (51%)
  waiting for transfers between devices  140 us (23%)
  starting transfers between devices  66.8 us (11%)
  local copies, waits for them, and re-layouts  51.2 us (9%)
  between operations  14.7 us (2%)
  other arithmetic  7.73 us (1%)
    pallas_call x39, Pallas kernels, launch(): pl.pallas_call(body, out_shape=tuple(out_shape) + (jax.ShapeDtypeStruct((...  308 us
    ppermute x37, waiting for transfers between devices, swap(): return lax.ppermute(value, axis, [(i, i ^ bit) for i in range(count)])  129 us
    ppermute x37, starting transfers between devices, swap(): return lax.ppermute(value, axis, [(i, i ^ bit) for i in range(count)])  54.4 us
    unnamed x99, local copies, waits for them, and re-layouts  24.5 us
  transfers between devices with their start and end apart: 43, of which 17 were waited for; matrix products, arithmetic and copies ran while one was open for 6% of the time, Pallas kernels for 41%

profile of v3, /device:TPU:1, one launch (start us, length us, event | category | flops | bytes accessed | tf_op | source)
XLA Modules:
  0.0 589.7 jit_solution(12241264296842931204)
XLA Ops:
  16.7 4.7 find_slots.1
  26.5 5.7 all-to-all-done
  45.7 16.4 %collective-permute-done.1.refs_2_ = bf16[2,320,384]{2,1,0:T(8,128)(2,1)S(1)} collective-permute-done((bf16[2,320,384]{2,1,0:T(8,128)(2,1)}, bf16[2,320,384]{2,1,0:T(8,128)(2,1)S(1)}, u32[]{:S(2)}, u32[]{:S(2)}) %collective-permute-start.1) | collective-permute-done | bytes 491552 | tf_op jit(solution)/shard_map/ppermute | solution.py:1102
  67.9 5.9 %gather_fusion = bf16[512,768]{1,0:T(8,128)(2,1)S(1)} fusion(bf16[4016,768]{1,0:T(8,128)(2,1)} %param.22, s32[1024]{0:T(1024)S(1)} %pad_clamp_fusion), kind=kCustom, calls=%fused_computation | custom fusion | bytes 1574912 | tf_op jit(solution)/shard_map/jit(_take)/gather | solution.py:1241
  76.5 12.2 %collective-permute-done.3.refs_2_ = bf16[4,320,384]{2,1,0:T(8,128)(2,1)S(1)} collective-permute-done((bf16[4,320,384]{2,1,0:T(8,128)(2,1)}, bf16[4,320,384]{2,1,0:T(8,128)(2,1)S(1)}, u32[]{:S(2)}, u32[]{:S(2)}) %collective-permute-start.3) | collective-permute-done | bytes 983072 | tf_op jit(solution)/shard_map/ppermute | solution.py:1102
  92.5 6.8 %pack.1 = (bf16[2048,768]{1,0:T(8,128)(2,1)}, bf16[96,768]{1,0:T(8,128)(2,1)}, f32[8,128]{1,0:T(8,128)}) custom-call(s32[2048,8]{1,0:T(8,128)} %get-tuple-element.137.refs_0_, bf16[512,768]{1,0:T(8,128)(2,1)} %refs_1_.1, bf16[512,768]{1,0:T(8,128)(2,1)} %broadcast_select_fusion.refs_2_, bf16[96,768]{1,0:T(8,128)(2,1)} %dynamic-slice_bitcast_fusion.refs_3_, ...), custom_call_target="tpu_custom_call" | custom-call | flops 1 | bytes 1 | tf_op jit(solution)/shard_map/pack/pallas_call | solution.py:37
  99.2 4.9 all-to-all-start.1
  109.1 29.5 %collective-permute-done.6.refs_3_ = bf16[768,768]{1,0:T(8,128)(2,1)S(1)} collective-permute-done((bf16[768,768]{1,0:T(8,128)(2,1)}, bf16[768,768]{1,0:T(8,128)(2,1)S(1)}, u32[]{:S(2)}, u32[]{:S(2)}) %collective-permute-start.6) | collective-permute-done | bytes 1179680 | tf_op jit(solution)/shard_map/ppermute | solution.py:1102
  138.6 5.0 collective-permute-start.7
  143.6 8.1 %layout_lookup.2 = (f32[1024,384]{1,0:T(8,128)}, f32[1024,384]{1,0:T(8,128)}, f32[8,128]{1,0:T(8,128)}) custom-call(s32[1]{0:T(128)} %bitcast.18.refs_0_, s32[1024,8]{1,0:T(8,128)} %get-tuple-element.136.refs_1_, s32[1024,8]{1,0:T(8,128)} %copy.47.refs_4_.refs_2_, bf16[8,256,384]{2,1,0:T(8,128)(2,1)} %bitcast.98, f32[8,128]{1,0:T(8,128)} %get-tuple-element.147.refs_4_), custom_call_target="tpu_custom_call" | custom-call | flops 1 | bytes 1 | tf_op jit(solution)/shard_map/layout_lookup/pallas_call | solution.py:37
  152.8 5.0 arrange.1
  157.8 15.1 %collective-permute-done.4.refs_3_ = bf16[8,256,384]{2,1,0:T(8,128)(2,1)S(1)} collective-permute-done((bf16[8,256,384]{2,1,0:T(8,128)(2,1)}, bf16[8,256,384]{2,1,0:T(8,128)(2,1)S(1)}, u32[]{:S(2)}, u32[]{:S(2)}) %collective-permute-start.4) | collective-permute-done | bytes 1572896 | tf_op jit(solution)/shard_map/ppermute | solution.py:1102
  174.1 8.6 %layout_lookup.3 = (f32[1024,384]{1,0:T(8,128)}, f32[1024,384]{1,0:T(8,128)}, f32[8,128]{1,0:T(8,128)}) custom-call(s32[1]{0:T(128)S(6)} %sub.42.refs_0_, s32[1024,8]{1,0:T(8,128)} %get-tuple-element.136.refs_1_, s32[1024,8]{1,0:T(8,128)} %copy.47.refs_4_.refs_2_, bf16[8,256,384]{2,1,0:T(8,128)(2,1)} %copy-done.7, f32[1024,384]{1,0:T(8,128)} %get-tuple-element.148.refs_4_, ...), custom_call_target="tpu_custom_call" | custom-call | flops 1 | bytes 1 | tf_op jit(solution)/shard_map/layout_lookup/pallas_call | solution.py:37
  190.8 17.0 %embed.1 = (bf16[768,1024]{1,0:T(8,128)(2,1)}, bf16[1024,768]{1,0:T(8,128)(2,1)}, bf16[768,1024]{1,0:T(8,128)(2,1)}, bf16[3,1024,768]{2,1,0:T(8,128)(2,1)}, f32[8,128]{1,0:T(8,128)}) custom-call(s32[8,2048]{1,0:T(8,128)} %get-tuple-element.135.refs_0_, s32[1024,8]{1,0:T(8,128)} %get-tuple-element.136.refs_1_, bf16[2048,768]{1,0:T(8,128)(2,1)} %bitcast.88, ...), custom_call_target="tpu_custom_call" | custom-call | flops 1 | bytes 1 | tf_op jit(solution)/shard_map/embed/pallas_call | solution.py:37
  215.2 28.7 %attention_forward.1 = (bf16[1024,768]{1,0:T(8,128)(2,1)}, f32[1024,768]{1,0:T(8,128)}, f32[8,128]{1,0:T(8,128)}) custom-call(bf16[3,1024,768]{2,1,0:T(8,128)(2,1)} %get-tuple-element.158.refs_0_.refs_1_.refs_2_, bf16[3,1024,768]{2,1,0:T(8,128)(2,1)} %get-tuple-element.158.refs_0_.refs_1_.refs_2_, ...), custom_call_target="tpu_custom_call" | custom-call | flops 1 | bytes 1 | tf_op jit(solution)/shard_map/attention_forward/pallas_call | solution.py:37
  244.8 34.7 %feed_forward.1 = (bf16[1024,768]{1,0:T(8,128)(2,1)}, bf16[3072,1024]{1,0:T(8,128)(2,1)}, bf16[1024,3072]{1,0:T(8,128)(2,1)}, bf16[768,1024]{1,0:T(8,128)(2,1)},...) custom-call(s32[1]{0:T(128)} %bitcast.refs_0_, ...), custom_call_target="tpu_custom_call" | custom-call | flops 1 | bytes 1 | tf_op jit(solution)/shard_map/feed_forward/pallas_call | solution.py:37
  279.4 9.8 %contract_quarters.1 = (bf16[2,8,2,96,384]{4,3,2,1,0:T(8,128)(2,1)}, bf16[2,8,2,96,384]{4,3,2,1,0:T(8,128)(2,1)}, f32[8,128]{1,0:T(8,128)}) custom-call(s32[1]{0:T(128)} %bitcast.refs_0_, bf16[768,1024]{1,0:T(8,128)(2,1)} %get-tuple-element.171.refs_1_, bf16[1024,3072]{1,0:T(8,128)(2,1)} %get-tuple-element.172.refs_2_, f32[8,128]{1,0:T(8,128)} %get-tuple-element.173.refs_3_), custom_call_target="tpu_custom_call" | custom-call | flops 1 | bytes 1 | tf_op jit(solution)/shard_map/contract_quarters/pallas_call | solution.py:37
  289.2 9.0 %contract_halves.2 = (bf16[3072,384]{1,0:T(8,128)(2,1)}, bf16[3072,384]{1,0:T(8,128)(2,1)}, f32[8,128]{1,0:T(8,128)}) custom-call(s32[1]{0:T(128)} %bitcast.refs_0_, bf16[3072,1024]{1,0:T(8,128)(2,1)} %get-tuple-element.170.refs_1_, bf16[1024,768]{1,0:T(8,128)(2,1)} %refs_2_.1, f32[8,128]{1,0:T(8,128)} %get-tuple-element.174.refs_3_), custom_call_target="tpu_custom_call" | custom-call | flops 1 | bytes 1 | tf_op jit(solution)/shard_map/contract_halves/pallas_call | solution.py:37
  310.5 5.4 rows_fold.3
  319.6 36.7 %attention_backward.1 = (bf16[3,1024,768]{2,1,0:T(8,128)(2,1)}, f32[12,8,512]{2,1,0:T(8,128)}, f32[8,128]{1,0:T(8,128)}) custom-call(bf16[3,1024,768]{2,1,0:T(8,128)(2,1)} %get-tuple-element.158.refs_0_.refs_1_.refs_2_, bf16[3,1024,768]{2,1,0:T(8,128)(2,1)} %get-tuple-element.158.refs_0_.refs_1_.refs_2_, ...), custom_call_target="tpu_custom_call" | custom-call | flops 1 | bytes 1 | tf_op jit(solution)/shard_map/attention_backward/pallas_call | solution.py:37
  369.0 9.9 %input_grad.1 = (bf16[1024,768]{1,0:T(8,128)(2,1)}, bf16[1024,384]{1,0:T(8,128)(2,1)}, bf16[1024,384]{1,0:T(8,128)(2,1)}, f32[8,768]{1,0:T(8,128)}, f32[8,128]{1,0:T(8,128)}) custom-call(s32[1]{0:T(128)} %bitcast.refs_0_, bf16[1024,768]{1,0:T(8,128)(2,1)} %get-tuple-element.157.refs_1_, f32[1024,768]{1,0:T(8,128)} %get-tuple-element.167.refs_2_, ...), custom_call_target="tpu_custom_call" | custom-call | flops 1 | bytes 1 | tf_op jit(solution)/shard_map/input_grad/pallas_call | solution.py:37
  386.7 7.0 %return_rows.1 = (bf16[8,272,768]{2,1,0:T(8,128)(2,1)}, f32[8,128]{1,0:T(8,128)}) custom-call(s32[2048,1]{1,0:T(8,128)} %copy.53.refs_0_, bf16[1024,768]{1,0:T(8,128)(2,1)} %get-tuple-element.195.refs_1_.refs_4_, f32[8,768]{1,0:T(8,128)} %pad.27.refs_2_, f32[8,128]{1,0:T(8,128)} %get-tuple-element.204.refs_3_), custom_call_target="tpu_custom_call" | custom-call | flops 1 | bytes 1 | tf_op jit(solution)/shard_map/return_rows/pallas_call | solution.py:37
  403.0 13.0 %layout_grad.1 = (bf16[8,2,128,384]{3,2,1,0:T(8,128)(2,1)}, bf16[8,2,128,384]{3,2,1,0:T(8,128)(2,1)}, f32[8,128]{1,0:T(8,128)}) custom-call(s32[1]{0:T(128)} %bitcast.18.refs_0_, s32[8,1024]{1,0:T(8,128)} %get-tuple-element.210.refs_1_, s32[8,1024]{1,0:T(8,128)} %bitcast.141, bf16[1024,384]{1,0:T(8,128)(2,1)} %get-tuple-element.211.refs_3_, ...), custom_call_target="tpu_custom_call" | custom-call | flops 1 | bytes 1 | tf_op jit(solution)/shard_map/layout_grad/pallas_call | solution.py:37
  416.0 10.1 %square_grads.1 = (bf16[8,2,2,96,384]{4,3,2,1,0:T(8,128)(2,1)}, bf16[8,2,2,96,384]{4,3,2,1,0:T(8,128)(2,1)}, f32[8,128]{1,0:T(8,128)}) custom-call(s32[1]{0:T(128)} %bitcast.refs_0_, bf16[768,1024]{1,0:T(8,128)(2,1)} %get-tuple-element.208.refs_1_, bf16[3,1024,768]{2,1,0:T(8,128)(2,1)} %get-tuple-element.187.refs_3_.refs_2_, ...), custom_call_target="tpu_custom_call" | custom-call | flops 1 | bytes 1 | tf_op jit(solution)/shard_map/square_grads/pallas_call | solution.py:37
  432.2 4.3 fold.11
  438.5 24.1 %collective-permute-done.22 = bf16[8,2,128,384]{3,2,1,0:T(8,128)(2,1)} collective-permute-done((bf16[8,2,128,384]{3,2,1,0:T(8,128)(2,1)}, bf16[8,2,128,384]{3,2,1,0:T(8,128)(2,1)}, u32[]{:S(2)}, u32[]{:S(2)}) %collective-permute-start.22) | collective-permute-done | bytes 1572896 | tf_op jit(solution)/shard_map/ppermute | solution.py:1102
  466.0 4.3 all-to-all-done.2.refs_1_
  472.0 6.4 %unpack_text.1 = (bf16[544,768]{1,0:T(8,128)(2,1)}, f32[8,128]{1,0:T(8,128)}) custom-call(s32[8,272]{1,0:T(8,128)} %pad.28.refs_0_, bf16[8,272,768]{2,1,0:T(8,128)(2,1)} %copy-done.2, s32[8,512]{1,0:T(8,128)} %get-tuple-element.138.refs_2_, f32[8,128]{1,0:T(8,128)} %get-tuple-element.223.refs_3_), custom_call_target="tpu_custom_call" | custom-call | flops 1 | bytes 1 | tf_op jit(solution)/shard_map/unpack_text/pallas_call | solution.py:37
  482.5 5.4 collective-permute-done.21
  494.2 11.5 %collective-permute-done.27.refs_1_ = bf16[544,768]{1,0:T(8,128)(2,1)S(1)} collective-permute-done((bf16[544,768]{1,0:T(8,128)(2,1)}, bf16[544,768]{1,0:T(8,128)(2,1)S(1)}, u32[]{:S(2)}, u32[]{:S(2)}) %collective-permute-start.27) | collective-permute-done | bytes 835616 | tf_op jit(solution)/shard_map/ppermute | solution.py:1102
  522.0 17.6 %text_grads.1 = (f32[4016,768]{1,0:T(8,128)}, f32[8,128]{1,0:T(8,128)}) custom-call(bf16[544,768]{1,0:T(8,128)(2,1)} %get-tuple-element.235.refs_0_, bf16[544,768]{1,0:T(8,128)(2,1)} %copy-done.14, bf16[544,768]{1,0:T(8,128)(2,1)} %collective-permute-done.28.refs_2_, bf16[544,768]{1,0:T(8,128)(2,1)} %copy-done.15, f32[8,128]{1,0:T(8,128)} %get-tuple-element.236.refs_4_), custom_call_target="tpu_custom_call" | custom-call | flops 1 | bytes 1 | tf_op jit(solution)/shard_map/text_grads/pallas_call | solution.py:37
  549.3 8.4 %patch_grads.1 = (f32[512,768]{1,0:T(8,128)}, f32[8,128]{1,0:T(8,128)}) custom-call(s32[8,272]{1,0:T(8,128)} %pad.25.refs_0_, bf16[8,272,768]{2,1,0:T(8,128)(2,1)} %copy-done.2, bf16[4,768,768]{2,1,0:T(8,128)(2,1)} %get-tuple-element.154.refs_6_.refs_8_.refs_4_.refs_2_, f32[8,128]{1,0:T(8,128)} %get-tuple-element.239.refs_3_), custom_call_target="tpu_custom_call" | custom-call | flops 1 | bytes 1 | tf_op jit(solution)/shard_map/patch_grads/pallas_call | solution.py:37
  (258 shorter events, 183.5 us)
Async XLA Ops:
  7.2 97.0 %all-gather.8.cloned.1.call-start = ((), (), s32[]{:S(2)}) async-start(), calls=%async_computation.4 | async-start | bytes 1327104 | tf_op jit(solution)/shard_map/all_gather | solution.py:1219
  9.0 235.0 %all-gather.10.cloned.1.call-start = ((), (), s32[]{:S(2)}) async-start(), calls=%async_computation.5 | async-start | bytes 4866048 | tf_op jit(solution)/shard_map/all_gather | solution.py:1223
  12.9 24.1 %collective-permute-start = (bf16[1,320,384]{2,1,0:T(8,128)(2,1)S(1)}, bf16[1,320,384]{2,1,0:T(8,128)(2,1)S(1)}, u32[]{:S(2)}, u32[]{:S(2)}) collective-permute-start(bf16[1,320,384]{2,1,0:T(8,128)(2,1)S(1)} %fusion.4.refs_1_), channel_id=1, source_target_pairs={{0,16},{4,20},{8,24},{12,28},{16,0},{20,4},{24,8},{28,12},{1,17},{... | collective-permute-start | bytes 737288 | tf_op jit(solution)/shard_map/ppermute | solution.py:1102
  26.5 217.5 %all-gather.6.cloned.1.call-start = ((), (), s32[]{:S(2)}) async-start(), calls=%async_computation.3 | async-start | bytes 4866048 | tf_op jit(solution)/shard_map/all_gather | solution.py:1246
  39.7 22.4 %collective-permute-start.1 = (bf16[2,320,384]{2,1,0:T(8,128)(2,1)}, bf16[2,320,384]{2,1,0:T(8,128)(2,1)S(1)}, u32[]{:S(2)}, u32[]{:S(2)}) collective-permute-start(bf16[2,320,384]{2,1,0:T(8,128)(2,1)} %bitcast.129), channel_id=1, source_target_pairs={{0,8},{4,12},{8,0},{12,4},{16,24},{20,28},{24,16},{28,20},{1,9},{5... | collective-permute-start | bytes 1474568 | tf_op jit(solution)/shard_map/ppermute | solution.py:1102
  65.0 23.7 %collective-permute-start.3 = (bf16[4,320,384]{2,1,0:T(8,128)(2,1)}, bf16[4,320,384]{2,1,0:T(8,128)(2,1)S(1)}, u32[]{:S(2)}, u32[]{:S(2)}) collective-permute-start(bf16[4,320,384]{2,1,0:T(8,128)(2,1)} %bitcast.110), channel_id=1, source_target_pairs={{0,4},{4,0},{8,12},{12,8},{16,20},{20,16},{24,28},{28,24},{1,5},{5... | collective-permute-start | bytes 2949128 | tf_op jit(solution)/shard_map/ppermute | solution.py:1102
  99.2 89.9 %all-to-all-start.1 = ((bf16[8,256,768]{2,1,0:T(8,128)(2,1)}), bf16[8,256,768]{2,1,0:T(8,128)(2,1)S(1)}, u32[]{:S(2)}, u32[]{:S(2)}) async-start(bf16[8,256,768]{2,1,0:T(8,128)(2,1)} %bitcast.90), calls=%async_computation.1 | async-start | bytes 6291456 | tf_op jit(solution)/shard_map/all_to_all | solution.py:1243
  104.2 34.4 %collective-permute-start.6 = (bf16[768,768]{1,0:T(8,128)(2,1)}, bf16[768,768]{1,0:T(8,128)(2,1)S(1)}, u32[]{:S(2)}, u32[]{:S(2)}) collective-permute-start(bf16[768,768]{1,0:T(8,128)(2,1)} %bitcast.105), channel_id=1, source_target_pairs={{0,2},{1,3},{2,0},{3,1},{4,6},{5,7},{6,4},{7,5},{8,10},{9,11},{10,... | collective-permute-start | bytes 3538952 | tf_op jit(solution)/shard_map/ppermute | solution.py:1102
  105.4 67.5 %collective-permute-start.4 = (bf16[8,256,384]{2,1,0:T(8,128)(2,1)}, bf16[8,256,384]{2,1,0:T(8,128)(2,1)S(1)}, u32[]{:S(2)}, u32[]{:S(2)}) collective-permute-start(bf16[8,256,384]{2,1,0:T(8,128)(2,1)} %bitcast.97), channel_id=1, source_target_pairs={{0,2},{1,3},{2,0},{3,1},{4,6},{5,7},{6,4},{7,5},{8,10},{9,11},{10,... | collective-permute-start | bytes 4718600 | tf_op jit(solution)/shard_map/ppermute | solution.py:1102
  105.7 46.1 %collective-permute-start.5 = (bf16[768,768]{1,0:T(8,128)(2,1)}, bf16[768,768]{1,0:T(8,128)(2,1)S(1)}, u32[]{:S(2)}, u32[]{:S(2)}) collective-permute-start(bf16[768,768]{1,0:T(8,128)(2,1)} %bitcast.106), channel_id=1, source_target_pairs={{0,1},{1,0},{2,3},{3,2},{4,5},{5,4},{6,7},{7,6},{8,9},{9,8},{10,11... | collective-permute-start | bytes 3538952 | tf_op jit(solution)/shard_map/ppermute | solution.py:1102
  138.6 13.2 %collective-permute-start.7 = (bf16[768,768]{1,0:T(8,128)(2,1)S(1)}, bf16[768,768]{1,0:T(8,128)(2,1)}, u32[]{:S(2)}, u32[]{:S(2)}) collective-permute-start(bf16[768,768]{1,0:T(8,128)(2,1)S(1)} %collective-permute-done.6.refs_3_), channel_id=1, source_target_pairs={{0,1},{1,0},{2,3},{3,2},{4,5},{5,4},{6,7},{7,6},{8,9},{9,8},{10,11... | collective-permute-start | bytes 3538952 | tf_op jit(solution)/shard_map/ppermute | solution.py:1102
  185.7 22.1 %collective-permute-start.9 = (bf16[8,48,384]{2,1,0:T(8,128)(2,1)S(1)}, bf16[8,48,384]{2,1,0:T(8,128)(2,1)}, u32[]{:S(2)}, u32[]{:S(2)}) collective-permute-start(bf16[8,48,384]{2,1,0:T(8,128)(2,1)S(1)} %bitcast.136), channel_id=1, source_target_pairs={{0,2},{1,3},{2,0},{3,1},{4,6},{5,7},{6,4},{7,5},{8,10},{9,11},{10,... | collective-permute-start | bytes 884744 | tf_op jit(solution)/shard_map/ppermute | solution.py:1102
  209.8 34.2 %collective-permute-start.10 = (bf16[768,384]{1,0:T(8,128)(2,1)}, bf16[768,384]{1,0:T(8,128)(2,1)S(1)}, u32[]{:S(2)}, u32[]{:S(2)}) collective-permute-start(bf16[768,384]{1,0:T(8,128)(2,1)} %bitcast.121), channel_id=1, source_target_pairs={{0,1},{1,0},{2,3},{3,2},{4,5},{5,4},{6,7},{7,6},{8,9},{9,8},{10,11... | collective-permute-start | bytes 1769480 | tf_op jit(solution)/shard_map/ppermute | solution.py:1102
  289.2 14.0 %collective-permute-start.13 = (bf16[2,8,2,96,384]{4,3,2,1,0:T(8,128)(2,1)}, bf16[2,8,2,96,384]{4,3,2,1,0:T(8,128)(2,1)S(1)}, u32[]{:S(2)}, u32[]{:S(2)}) collective-permute-start(bf16[2,8,2,96,384]{4,3,2,1,0:T(8,128)(2,1)} %get-tuple-element.183), channel_id=1, source_target_pairs={{0,1},{1,0},{2,3},{3,2},{4,5},{5,4},{6,7},{7,6},{8,9},{9,8},{10,11... | collective-permute-start | bytes 7077896 | tf_op jit(solution)/shard_map/ppermute | solution.py:1102
  315.9 40.4 %collective-permute-start.15 = (bf16[8,240,384]{2,1,0:T(8,128)(2,1)}, bf16[8,240,384]{2,1,0:T(8,128)(2,1)S(1)}, u32[]{:S(2)}, u32[]{:S(2)}) collective-permute-start(bf16[8,240,384]{2,1,0:T(8,128)(2,1)} %get-tuple-element.191), channel_id=1, source_target_pairs={{0,2},{1,3},{2,0},{3,1},{4,6},{5,7},{6,4},{7,5},{8,10},{9,11},{10,... | collective-permute-start | bytes 4423688 | tf_op jit(solution)/shard_map/ppermute | solution.py:1102
  317.6 43.0 %collective-permute-start.14 = (bf16[8,1,192,384]{3,2,1,0:T(8,128)(2,1)}, bf16[8,1,192,384]{3,2,1,0:T(8,128)(2,1)S(1)}, u32[]{:S(2)}, u32[]{:S(2)}) collective-permute-start(bf16[8,1,192,384]{3,2,1,0:T(8,128)(2,1)} %get-tuple-element.189), channel_id=1, source_target_pairs={{0,4},{4,0},{8,12},{12,8},{16,20},{20,16},{24,28},{28,24},{1,5},{5... | collective-permute-start | bytes 3538952 | tf_op jit(solution)/shard_map/ppermute | solution.py:1102
  364.6 15.7 %collective-permute-start.17 = (bf16[1,4,192,384]{3,2,1,0:T(8,128)(2,1)}, bf16[1,4,192,384]{3,2,1,0:T(8,128)(2,1)S(1)}, u32[]{:S(2)}, u32[]{:S(2)}) collective-permute-start(bf16[1,4,192,384]{3,2,1,0:T(8,128)(2,1)} %get-tuple-element.202), channel_id=1, source_target_pairs={{0,2},{1,3},{2,0},{3,1},{4,6},{5,7},{6,4},{7,5},{8,10},{9,11},{10,... | collective-permute-start | bytes 1769480 | tf_op jit(solution)/shard_map/ppermute | solution.py:1102
  364.9 16.9 %collective-permute-start.16 = (bf16[4,1,240,384]{3,2,1,0:T(8,128)(2,1)}, bf16[4,1,240,384]{3,2,1,0:T(8,128)(2,1)S(1)}, u32[]{:S(2)}, u32[]{:S(2)}) collective-permute-start(bf16[4,1,240,384]{3,2,1,0:T(8,128)(2,1)} %get-tuple-element.200), channel_id=1, source_target_pairs={{0,4},{4,0},{8,12},{12,8},{16,20},{20,16},{24,28},{28,24},{1,5},{5... | collective-permute-start | bytes 2211848 | tf_op jit(solution)/shard_map/ppermute | solution.py:1102
  393.8 76.5 %all-to-all-start.2 = ((bf16[8,272,768]{2,1,0:T(8,128)(2,1)}), bf16[8,272,768]{2,1,0:T(8,128)(2,1)S(1)}, u32[]{:S(2)}, u32[]{:S(2)}) async-start(bf16[8,272,768]{2,1,0:T(8,128)(2,1)} %get-tuple-element.205), calls=%async_computation.2 | async-start | bytes 6684672 | tf_op jit(solution)/shard_map/all_to_all | solution.py:1322
  426.4 36.2 %collective-permute-start.22 = (bf16[8,2,128,384]{3,2,1,0:T(8,128)(2,1)}, bf16[8,2,128,384]{3,2,1,0:T(8,128)(2,1)}, u32[]{:S(2)}, u32[]{:S(2)}) collective-permute-start(bf16[8,2,128,384]{3,2,1,0:T(8,128)(2,1)} %get-tuple-element.221), channel_id=1, source_target_pairs={{0,2},{1,3},{2,0},{3,1},{4,6},{5,7},{6,4},{7,5},{8,10},{9,11},{10,... | collective-permute-start | bytes 4718600 | tf_op jit(solution)/shard_map/ppermute | solution.py:1102
  436.5 51.4 %collective-permute-start.21 = (bf16[8,1,192,384]{3,2,1,0:T(8,128)(2,1)}, bf16[8,1,192,384]{3,2,1,0:T(8,128)(2,1)}, u32[]{:S(2)}, u32[]{:S(2)}) collective-permute-start(bf16[8,1,192,384]{3,2,1,0:T(8,128)(2,1)} %get-tuple-element.219), channel_id=1, source_target_pairs={{0,2},{1,3},{2,0},{3,1},{4,6},{5,7},{6,4},{7,5},{8,10},{9,11},{10,... | collective-permute-start | bytes 3538952 | tf_op jit(solution)/shard_map/ppermute | solution.py:1102
  478.4 27.3 %collective-permute-start.27 = (bf16[544,768]{1,0:T(8,128)(2,1)}, bf16[544,768]{1,0:T(8,128)(2,1)S(1)}, u32[]{:S(2)}, u32[]{:S(2)}) collective-permute-start(bf16[544,768]{1,0:T(8,128)(2,1)} %get-tuple-element.235.refs_0_), channel_id=1, source_target_pairs={{0,2},{1,3},{2,0},{3,1},{4,6},{5,7},{6,4},{7,5},{8,10},{9,11},{10,... | collective-permute-start | bytes 2506760 | tf_op jit(solution)/shard_map/ppermute | solution.py:1102
  479.6 30.2 %collective-permute-start.24 = (bf16[4,1,256,384]{3,2,1,0:T(8,128)(2,1)S(1)}, bf16[4,1,256,384]{3,2,1,0:T(8,128)(2,1)S(1)}, u32[]{:S(2)}, u32[]{:S(2)}) collective-permute-start(bf16[4,1,256,384]{3,2,1,0:T(8,128)(2,1)S(1)} %copy-done.43), channel_id=1, source_target_pairs={{0,4},{4,0},{8,12},{12,8},{16,20},{20,16},{24,28},{28,24},{1,5},{5... | collective-permute-start | bytes 2359304 | tf_op jit(solution)/shard_map/ppermute | solution.py:1102
  482.5 24.2 %collective-permute-start.18 = (bf16[2,432,384]{2,1,0:T(8,128)(2,1)S(1)}, bf16[2,432,384]{2,1,0:T(8,128)(2,1)S(1)}, u32[]{:S(2)}, u32[]{:S(2)}) collective-permute-start(bf16[2,432,384]{2,1,0:T(8,128)(2,1)S(1)} %copy-done.44), channel_id=1, source_target_pairs={{0,8},{4,12},{8,0},{12,4},{16,24},{20,28},{24,16},{28,20},{1,9},{5... | collective-permute-start | bytes 1990664 | tf_op jit(solution)/shard_map/ppermute | solution.py:1102
  490.8 19.9 %collective-permute-start.25 = (bf16[4,1,192,384]{3,2,1,0:T(8,128)(2,1)}, bf16[4,1,192,384]{3,2,1,0:T(8,128)(2,1)S(1)}, u32[]{:S(2)}, u32[]{:S(2)}) collective-permute-start(bf16[4,1,192,384]{3,2,1,0:T(8,128)(2,1)} %get-tuple-element.231), channel_id=1, source_target_pairs={{0,4},{4,0},{8,12},{12,8},{16,20},{20,16},{24,28},{28,24},{1,5},{5... | collective-permute-start | bytes 1769480 | tf_op jit(solution)/shard_map/ppermute | solution.py:1102
  492.4 28.7 %collective-permute-start.28 = (bf16[544,768]{1,0:T(8,128)(2,1)S(1)}, bf16[544,768]{1,0:T(8,128)(2,1)}, u32[]{:S(2)}, u32[]{:S(2)}) collective-permute-start(bf16[544,768]{1,0:T(8,128)(2,1)S(1)} %copy-done.16), channel_id=1, source_target_pairs={{0,1},{1,0},{2,3},{3,2},{4,5},{5,4},{6,7},{7,6},{8,9},{9,8},{10,11... | collective-permute-start | bytes 2506760 | tf_op jit(solution)/shard_map/ppermute | solution.py:1102
  505.7 15.5 %collective-permute-start.29 = (bf16[544,768]{1,0:T(8,128)(2,1)S(1)}, bf16[544,768]{1,0:T(8,128)(2,1)S(1)}, u32[]{:S(2)}, u32[]{:S(2)}) collective-permute-start(bf16[544,768]{1,0:T(8,128)(2,1)S(1)} %collective-permute-done.27.refs_1_), channel_id=1, source_target_pairs={{0,1},{1,0},{2,3},{3,2},{4,5},{5,4},{6,7},{7,6},{8,9},{9,8},{10,11... | collective-permute-start | bytes 2506760 | tf_op jit(solution)/shard_map/ppermute | solution.py:1102
  515.6 24.1 %collective-permute-start.26 = (bf16[2,448,384]{2,1,0:T(8,128)(2,1)}, bf16[2,448,384]{2,1,0:T(8,128)(2,1)S(1)}, u32[]{:S(2)}, u32[]{:S(2)}) collective-permute-start(bf16[2,448,384]{2,1,0:T(8,128)(2,1)} %get-tuple-element.234), channel_id=1, source_target_pairs={{0,8},{4,12},{8,0},{12,4},{16,24},{20,28},{24,16},{28,20},{1,9},{5... | collective-permute-start | bytes 2064392 | tf_op jit(solution)/shard_map/ppermute | solution.py:1102
  518.1 28.4 %collective-permute-start.23 = (bf16[1,1,432,384]{3,2,1,0:T(8,128)(2,1)}, bf16[1,1,432,384]{3,2,1,0:T(8,128)(2,1)S(1)}, u32[]{:S(2)}, u32[]{:S(2)}) collective-permute-start(bf16[1,1,432,384]{3,2,1,0:T(8,128)(2,1)} %get-tuple-element.227), channel_id=1, source_target_pairs={{0,16},{4,20},{8,24},{12,28},{16,0},{20,4},{24,8},{28,12},{1,17},{... | collective-permute-start | bytes 995336 | tf_op jit(solution)/shard_map/ppermute | solution.py:1102
  543.1 17.2 %collective-permute-start.30 = (bf16[1,1,448,384]{3,2,1,0:T(8,128)(2,1)}, bf16[1,1,448,384]{3,2,1,0:T(8,128)(2,1)S(1)}, u32[]{:S(2)}, u32[]{:S(2)}) collective-permute-start(bf16[1,1,448,384]{3,2,1,0:T(8,128)(2,1)} %get-tuple-element.243), channel_id=1, source_target_pairs={{0,16},{4,20},{8,24},{12,28},{16,0},{20,4},{24,8},{28,12},{1,17},{... | collective-permute-start | bytes 1032200 | tf_op jit(solution)/shard_map/ppermute | solution.py:1102
  549.1 17.8 %collective-permute-start.35 = (bf16[432,384]{1,0:T(8,128)(2,1)}, bf16[432,384]{1,0:T(8,128)(2,1)S(1)}, u32[]{:S(2)}, u32[]{:S(2)}) collective-permute-start(bf16[432,384]{1,0:T(8,128)(2,1)} %get-tuple-element.246.refs_1_), channel_id=1, source_target_pairs={{0,2},{1,3},{2,0},{3,1},{4,6},{5,7},{6,4},{7,5},{8,10},{9,11},{10,... | collective-permute-start | bytes 995336 | tf_op jit(solution)/shard_map/ppermute | solution.py:1102
  566.9 12.0 %collective-permute-start.31 = (bf16[448,384]{1,0:T(8,128)(2,1)}, bf16[448,384]{1,0:T(8,128)(2,1)S(1)}, u32[]{:S(2)}, u32[]{:S(2)}) collective-permute-start(bf16[448,384]{1,0:T(8,128)(2,1)} %get-tuple-element.245.refs_1_), channel_id=1, source_target_pairs={{0,1},{1,0},{2,3},{3,2},{4,5},{5,4},{6,7},{7,6},{8,9},{9,8},{10,11... | collective-permute-start | bytes 1032200 | tf_op jit(solution)/shard_map/ppermute | solution.py:1102
  (57 other events, 345.3 us)
Sparse Core Ops, SparseCore 0:
  10.8 45.8 all-gather.7
  59.5 86.8 all-gather.9
  149.3 83.6 all-gather.5
